TPU v7x, 1024 devices: a whole 4x4x32 slice. The times are simulated.
1024 devices in a mesh: tower: 2 (over core), dp: 32 (over x, z_lo), tensor: 16 (over z_hi, y).
Axes of the slice: x: 4, y: 4, z: 32 (z_hi: 4, z_lo: 8; z = z_hi * 8 + z_lo), core: 2. Of those that a mesh axis runs over, the one named last changes fastest.
Arguments:
- text_query: bfloat16 [2, 8, 64, 64, 128], P('tower', None, 'tensor'), may hold values from -6 to 6
- attn_out: bfloat16 [2, 8, 64, 64, 128], P('tower', None, 'tensor'), may hold values from -6 to 6
- grad_out: bfloat16 [2, 8, 64, 64, 128], P('tower', None, 'tensor'), may hold values from -6 to 6
- log_norm: bfloat16 [2, 8, 64, 64], P('tower', None, 'tensor'), may hold values from 2.5 to 4.5
- image_keys: bfloat16 [2, 26624, 1024], P('tower', ('dp', 'tensor')), may hold values from -6 to 6
- image_values: bfloat16 [2, 26624, 1024], P('tower', ('dp', 'tensor')), may hold values from -6 to 6
- k_weight: bfloat16 [2, 8192, 1024], P('tower', 'tensor'), may hold values from -0.0625 to 0.0625
- v_weight: bfloat16 [2, 8192, 1024], P('tower', 'tensor'), may hold values from -0.0625 to 0.0625
- layer_gate: float32 [2], P('tower'), may hold values from 0.3 to 1.2
- tile_counts: int32 [8], replicated, may hold values from 1 to 2, as said below
- text_lens: int32 [8], replicated, may hold values from 1 to 64, as said below
Outputs:
- feat_grad: float32 [26624, 8192], P(('dp', 'tensor'), 'tower')
Inputs may be any that keep to these rules, and one draw needn't show every extreme that they name: `tile_counts`: some sample has 2 tiles. `text_lens`: some sample has 64 text tokens.
All inputs are finite; a program needn't handle non-finite values.
Results may differ from a plain program's by a relative error of at most 0.025.
Values may be sent and summed in bfloat16 or wider, within the bound.
No kernel may reach another device: no remote copies, remote signals or barrier semaphores. Data moves between devices by JAX's collectives and lax.ppermute only.
A program may use at most 64 MiB of HBM per device.

v0:
```python
import math

import jax
import jax.numpy as jnp
from jax import lax
from jax.sharding import PartitionSpec as P

H = 64
KVH = 8
TILE_LEN = 1601
TILE_PAD = 1664


def body(
    text_query,
    attn_out,
    grad_out,
    log_norm,
    image_keys,
    image_values,
    k_weight,
    v_weight,
    layer_gate,
    tile_counts,
    text_lens,
):
    samples = tile_counts.shape[0]
    share = lax.axis_size("dp") // samples
    sample = lax.axis_index("dp") // share
    local_query = lax.dynamic_index_in_dim(text_query[0], sample, 0, keepdims=False)
    local_out = lax.dynamic_index_in_dim(attn_out[0], sample, 0, keepdims=False)
    local_cot = lax.dynamic_index_in_dim(grad_out[0], sample, 0, keepdims=False)
    local_norm = lax.dynamic_index_in_dim(log_norm[0], sample, 0, keepdims=False)
    text_rows = local_query.shape[1]
    head_size = local_query.shape[2]
    scaling = 1.0 / math.sqrt(head_size)
    row_mask = (jnp.arange(text_rows) < text_lens[sample]).astype(jnp.float32)
    scaled_grad = (
        jnp.tanh(layer_gate[0]) * local_cot.astype(jnp.float32) * row_mask[None, :, None]
    ).astype(jnp.bfloat16)
    row_delta = jnp.sum(
        scaled_grad.astype(jnp.float32) * local_out.astype(jnp.float32), axis=-1
    ).astype(jnp.bfloat16)
    key_rows = image_keys[0]
    rows_here = key_rows.shape[0]
    kv_width = key_rows.shape[1]
    block_index = lax.axis_index("dp") % share * lax.axis_size("tensor") + lax.axis_index("tensor")
    position = block_index * rows_here + jnp.arange(rows_here)
    key_mask = (
        (position // TILE_PAD < tile_counts[sample]) & (position % TILE_PAD < TILE_LEN)
    ).astype(jnp.float32)
    keys_split = key_rows.reshape(rows_here, KVH, head_size)
    values_split = image_values[0].reshape(rows_here, KVH, head_size)
    group_size = H // KVH
    query_in = lax.all_gather(local_query, "tensor", axis=0, tiled=True)
    grad_in = lax.all_gather(scaled_grad, "tensor", axis=0, tiled=True)
    norm_in = lax.all_gather(local_norm, "tensor", axis=0, tiled=True)
    delta_in = lax.all_gather(row_delta, "tensor", axis=0, tiled=True)
    head_count = query_in.shape[0]
    kv_index = jnp.arange(head_count) // group_size
    key_head = jnp.take(keys_split, kv_index, axis=1)
    value_head = jnp.take(values_split, kv_index, axis=1)
    scores = (
        jnp.einsum("hrd,phd->hrp", query_in, key_head, preferred_element_type=jnp.float32) * scaling
    )
    attention = jnp.exp(scores - norm_in.astype(jnp.float32)[:, :, None]) * key_mask[None, None, :]
    value_part = jnp.einsum(
        "hrp,hrd->phd", attention.astype(jnp.bfloat16), grad_in, preferred_element_type=jnp.float32
    )
    grad_probs = jnp.einsum("hrd,phd->hrp", grad_in, value_head, preferred_element_type=jnp.float32)
    grad_scores = (attention * (grad_probs - delta_in.astype(jnp.float32)[:, :, None])).astype(
        jnp.bfloat16
    )
    key_part = (
        jnp.einsum("hrp,hrd->phd", grad_scores, query_in, preferred_element_type=jnp.float32)
        * scaling
    )
    select = (kv_index[:, None] == jnp.arange(KVH)[None, :]).astype(jnp.float32)
    highest = lax.Precision.HIGHEST
    key_grad = jnp.einsum("phd,hk->pkd", key_part, select, precision=highest)
    value_grad = jnp.einsum("phd,hk->pkd", value_part, select, precision=highest)
    both_grads = jnp.concatenate(
        [
            key_grad.reshape(rows_here, kv_width).astype(jnp.bfloat16),
            value_grad.reshape(rows_here, kv_width).astype(jnp.bfloat16),
        ],
        axis=1,
    )
    key_block = k_weight[0]
    value_block = v_weight[0]
    contract = (((1,), (1,)), ((), ()))
    piece = lax.all_gather(both_grads, "tensor", axis=0, tiled=True)
    key_term = lax.dot_general(
        piece[:, :kv_width], key_block, contract, preferred_element_type=jnp.float32
    )
    value_term = lax.dot_general(
        piece[:, kv_width:], value_block, contract, preferred_element_type=jnp.float32
    )
    partial_feat = key_term + value_term
    owned = lax.all_to_all(partial_feat, "tensor", split_axis=0, concat_axis=1, tiled=True)
    feat_grad = lax.psum_scatter(owned, "tower", scatter_dimension=1, tiled=True)
    return feat_grad


def solution(mesh):
    in_specs = (
        P("tower", None, "tensor", None, None),
        P("tower", None, "tensor", None, None),
        P("tower", None, "tensor", None, None),
        P("tower", None, "tensor", None),
        P("tower", ("dp", "tensor"), None),
        P("tower", ("dp", "tensor"), None),
        P("tower", "tensor", None),
        P("tower", "tensor", None),
        P("tower"),
        P(),
        P(),
    )
    out_specs = P(("dp", "tensor"), "tower")
    return jax.shard_map(body, mesh=mesh, in_specs=in_specs, out_specs=out_specs, check_vma=False)
```

profile of v0, /device:TPU:1, one launch (start us, length us, event | category | flops | bytes accessed | tf_op | source)
XLA Modules:
  0.0 723.2 jit_solution(7862299764839598336)
XLA Ops:
  6.5 1.5 dynamic-slice_bitcast_fusion
  8.1 0.0 all-gather.8.cloned.1.call-start
  8.9 1.2 dynamic_slice.24
  10.1 0.6 compare_convert_fusion
  10.7 1.6 fusion.41
  12.4 1.3 dynamic_slice.22
  13.7 0.7 constant_dynamic-slice_fusion
  14.4 81.8 %all-gather.1 = bf16[1,1,64,64]{3,1,0,2:T(2,128)(2,1)S(1)} all-gather(bf16[1,1,4,64]{3,1,0,2:T(2,128)(2,1)S(1)} %copy.26), channel_id=3, replica_groups=mesh['tower'=2,'dp'=32,'tensor'=16] {'tensor'}, dimensions={2}, use_global_device_ids=true | all-gather | bytes 8704 | tf_op jit(solution)/shard_map/all_gather | solution.py:57
  96.2 61.1 %all-gather.2 = bf16[16,4,64]{2,1,0:T(4,128)(2,1)S(1)} all-gather(bf16[1,4,64]{2,1,0:T(4,128)(2,1)S(1)} %bitcast.84), channel_id=1, replica_groups=mesh['tower'=2,'dp'=32,'tensor'=16] {'tensor'}, dimensions={0}, use_global_device_ids=true | all-gather | bytes 8704 | tf_op jit(solution)/shard_map/all_gather | solution.py:58
  157.3 0.9 copy.27
  158.3 0.9 copy.28
  159.3 1.6 gather_fusion.1
  160.9 1.6 gather_fusion
  162.5 0.7 and_convert_fusion
  163.2 2.3 exponential_multiply_fusion
  165.5 106.8 %all-gather.8.cloned.1.call-done = bf16[64,64,128]{2,1,0:T(8,128)(2,1)} async-done(((bf16[4,64,128]{2,1,0:T(8,128)(2,1)}), bf16[64,64,128]{2,1,0:T(8,128)(2,1)}) %all-gather.8.cloned.1.call-update) | async-done | bytes 1048592 | tf_op jit(solution)/shard_map/all_gather | solution.py:56
  272.3 4.3 multiply_bitcast_fusion
  276.6 2.4 fusion.20
  279.0 0.6 convolution_bitcast_fusion
  279.6 0.8 fusion.17
  280.5 0.7 maximum_bitcast_fusion
  281.3 220.8 %all-gather.12.cloned.1.call-done = bf16[16,52,2048]{2,1,0:T(8,128)(2,1)} async-done(((bf16[1,52,2048]{2,1,0:T(8,128)(2,1)}), bf16[16,52,2048]{2,1,0:T(8,128)(2,1)}) %all-gather.12.cloned.1.call-update) | async-done | bytes 3407888 | tf_op jit(solution)/shard_map/all_gather | solution.py:92
  502.0 4.6 reshape.91
  506.6 2.7 fusion
  509.3 0.1 copy-done.3
  509.4 2.3 fusion.8
  511.7 1.5 all_to_all.14
  513.2 173.9 %all_to_all.19 = f32[16,52,512]{2,1,0:T(8,128)S(1)} all-to-all(f32[16,52,512]{2,1,0:T(8,128)S(1)} %all_to_all.14), channel_id=1, replica_groups=mesh['tower'=2,'dp'=32,'tensor'=16] {'tensor'}, dimensions={0} | all-to-all | bytes 3407872 | tf_op jit(solution)/shard_map/all_to_all | solution.py:100
  687.0 1.0 copy.24
  688.0 0.2 pad.6
  688.3 2.3 copy.31
  690.6 26.1 %reduce-scatter.2.cloned.1.call-done = f32[52,4096]{1,0:T(8,128)} async-done(((f32[52,8192]{1,0:T(8,128)}), f32[52,4096]{1,0:T(8,128)}) %reduce-scatter.2.cloned.1.call-update) | async-done | bytes 851984 | tf_op jit(solution)/shard_map/reduce_scatter | solution.py:101
  (30 shorter events, 0.4 us)
Async XLA Ops:
  6.5 500.1 %copy-start = (bf16[1,512,1024]{2,1,0:T(8,128)(2,1)S(1)}, bf16[1,512,1024]{2,1,0:T(8,128)(2,1)}, u32[]{:S(2)}) copy-start(bf16[1,512,1024]{2,1,0:T(8,128)(2,1)} %param.20) | copy-start | bytes 3145732
  6.5 156.7 %all-gather.10.cloned.1.call-start = ((), (), s32[]{:S(2)}) async-start(), calls=%async_computation.4 | async-start | bytes 1114112 | tf_op jit(solution)/shard_map/all_gather | solution.py:55
  8.1 264.2 %all-gather.8.cloned.1.call-start = ((), (), s32[]{:S(2)}) async-start(), calls=%async_computation.2 | async-start | bytes 1114112 | tf_op jit(solution)/shard_map/all_gather | solution.py:56
  12.4 489.7 %all-gather.12.cloned.1.call-start = ((), (), s32[]{:S(2)}) async-start(), calls=%async_computation.5 | async-start | bytes 3899392 | tf_op jit(solution)/shard_map/all_gather | solution.py:92
  276.6 2.4 copy-start.1
  281.2 435.5 %reduce-scatter.2.cloned.1.call-start = ((), (), s32[]{:S(2)}) async-start(), calls=%async_computation.3 | async-start | bytes 2752512 | tf_op jit(solution)/shard_map/reduce_scatter | solution.py:101
  506.6 2.7 copy-start.2
  506.6 2.8 copy-start.3
Sparse Core Ops, SparseCore 0:
  11.5 137.3 all-gather.9
  153.2 119.0 all-gather.7
  281.3 220.6 all-gather.11
  690.7 25.9 reduce-scatter.1
where the time goes:
time: 724 us; the launch traced here: 723 us
  waiting for transfers between devices  354 us (49%)
  blocking collectives  317 us (44%)
  local copies, waits for them, and re-layouts  19.6 us (3%)
  matrix products  15.3 us (2%)
  between operations  14 us (2%)
    all_gather x1, waiting for transfers between devices, body(): piece = lax.all_gather(both_grads, 'tensor', axis=0, tiled=True)  221 us
    all_to_all x1, blocking collectives, body(): lax.all_to_all(partial_feat, 'tensor', split_axis=0, concat_axis=1, tiled...  174 us
    all_gather x1, waiting for transfers between devices, body(): grad_in = lax.all_gather(scaled_grad, 'tensor', axis=0, tiled=True)  107 us
    all_gather x1, blocking collectives, body(): norm_in = lax.all_gather(local_norm, 'tensor', axis=0, tiled=True)  81.8 us
    all_gather x1, blocking collectives, body(): delta_in = lax.all_gather(row_delta, 'tensor', axis=0, tiled=True)  61.1 us
    reduce_scatter x1, waiting for transfers between devices, body(): lax.psum_scatter(owned, 'tower', scatter_dimension=1, tiled=True)  26.1 us
  transfers between devices with their start and end apart: 4, of which 3 were waited for; matrix products, arithmetic and copies ran while one was open for 2% of the time, Pallas kernels for 0%

commit v1 on v0

v1 whole, which is shorter than its diff:
```python
import math

import jax
import jax.numpy as jnp
from jax import lax
from jax.experimental import pallas as pl
from jax.experimental.pallas import tpu as pltpu
from jax.sharding import Mesh, PartitionSpec as P

H = 64
KVH = 8
HD = 128
TXT = 64
TILE_LEN = 1601
TILE_PAD = 1664
NAMES = ("core", "x", "zb", "zq", "zh", "y")
SIZES = (2, 4, 2, 4, 4, 4)
SCALING = 1.0 / math.sqrt(HD)
LOCAL = H // 16
QROWS = LOCAL * TXT
META = 2 * QROWS
PACK = META + 16
NT = (((1,), (1,)), ((), ()))
NN = (((1,), (0,)), ((), ()))


def attention_kernel(pack_ref, key_ref, value_ref, mask_ref, out_ref):
    query = pack_ref[:, 0, 0:QROWS, :].reshape(2 * QROWS, HD)
    grad = pack_ref[:, 0, QROWS : 2 * QROWS, :].reshape(2 * QROWS, HD)
    meta = pack_ref[:, 0, META : META + 16, :].astype(jnp.float32)
    norm = jnp.concatenate([meta[i, j : j + 1] for i in range(2) for j in (0, 1)], axis=1)
    delta = jnp.concatenate([meta[i, j : j + 1] for i in range(2) for j in (2, 3)], axis=1)
    mask = mask_ref[...]
    scores = lax.dot_general(key_ref[0], query, NT, preferred_element_type=jnp.float32) * SCALING
    attention = jnp.exp(scores - norm) * mask
    out_ref[1] = lax.dot_general(
        attention.astype(jnp.bfloat16), grad, NN, preferred_element_type=jnp.float32
    ).astype(jnp.bfloat16)
    probs = lax.dot_general(value_ref[0], grad, NT, preferred_element_type=jnp.float32)
    grad_scores = (attention * (probs - delta)).astype(jnp.bfloat16)
    out_ref[0] = (
        lax.dot_general(grad_scores, query, NN, preferred_element_type=jnp.float32) * SCALING
    ).astype(jnp.bfloat16)


def attention_grads(packed, keys, values, mask):
    rows = keys.shape[1]
    block = pl.BlockSpec((1, rows, HD), lambda g: (0, 0, g))
    return pl.pallas_call(
        attention_kernel,
        grid=(KVH,),
        in_specs=[
            pl.BlockSpec((2, 1, PACK, HD), lambda g: (g % 2, g // 2, 0, 0)),
            block,
            block,
            pl.BlockSpec((rows, 1), lambda g: (0, 0)),
        ],
        out_specs=pl.BlockSpec((2, rows, HD), lambda g: (0, 0, g)),
        out_shape=jax.ShapeDtypeStruct((2, rows, KVH * HD), jnp.bfloat16),
        compiler_params=pltpu.CompilerParams(vmem_limit_bytes=16 * 1024 * 1024),
        cost_estimate=pl.CostEstimate(
            flops=8 * rows * H * TXT * HD, bytes_accessed=3 << 20, transcendentals=rows * H * TXT
        ),
    )(packed, keys, values, mask)


def body(
    text_query,
    attn_out,
    grad_out,
    log_norm,
    image_keys,
    image_values,
    k_weight,
    v_weight,
    layer_gate,
    tile_counts,
    text_lens,
):
    x = lax.axis_index("x")
    zb = lax.axis_index("zb")
    zq = lax.axis_index("zq")
    zh = lax.axis_index("zh")
    y = lax.axis_index("y")
    sample = x * 2 + zb

    feature = x * 128 + (zb * 4 + zq) * 16
    weight = jnp.concatenate(
        [
            lax.dynamic_slice_in_dim(k_weight[0], feature, 16, 0),
            lax.dynamic_slice_in_dim(v_weight[0], feature, 16, 0),
        ],
        axis=1,
    )
    weight = lax.all_gather(weight, ("zh", "zb", "zq"), axis=0, tiled=True)

    query = lax.dynamic_index_in_dim(text_query[0], sample, 0, keepdims=False)
    out = lax.dynamic_index_in_dim(attn_out[0], sample, 0, keepdims=False)
    cot = lax.dynamic_index_in_dim(grad_out[0], sample, 0, keepdims=False)
    norm = lax.dynamic_index_in_dim(log_norm[0], sample, 0, keepdims=False)
    row_mask = (jnp.arange(TXT) < text_lens[sample]).astype(jnp.float32)
    scaled = (jnp.tanh(layer_gate[0]) * cot.astype(jnp.float32) * row_mask[None, :, None]).astype(
        jnp.bfloat16
    )
    delta = jnp.sum(scaled.astype(jnp.float32) * out.astype(jnp.float32), axis=-1).astype(
        jnp.bfloat16
    )
    packed = jnp.concatenate(
        [
            query.reshape(QROWS, HD),
            scaled.reshape(QROWS, HD),
            norm.reshape(QROWS // HD, HD),
            delta.reshape(QROWS // HD, HD),
            jnp.zeros((16 - 2 * (QROWS // HD), HD), jnp.bfloat16),
        ],
        axis=0,
    )
    packed = lax.all_gather(packed, "zh", axis=0, tiled=False)
    packed = jnp.broadcast_to(packed[None], (4, 4, PACK, HD))
    packed = lax.all_to_all(packed, "y", split_axis=0, concat_axis=0, tiled=True)

    rows = image_keys.shape[1]
    position = (zq * 16 + zh * 4 + y) * rows + jnp.arange(rows)
    key_mask = (
        (position // TILE_PAD < tile_counts[sample]) & (position % TILE_PAD < TILE_LEN)
    ).astype(jnp.float32)
    grads = attention_grads(packed, image_keys, image_values, key_mask[:, None])

    both = jnp.concatenate([grads[0], grads[1]], axis=1)
    both = jnp.broadcast_to(both[None], (16, rows, 2 * KVH * HD))
    both = lax.all_to_all(both, ("x", "y"), split_axis=0, concat_axis=0, tiled=True)
    both = both.reshape(16 * rows, 2 * KVH * HD)
    halves = weight.reshape(2, 256, 2 * KVH * HD)
    part = jnp.stack(
        [
            lax.dot_general(both, halves[t], NT, preferred_element_type=jnp.float32).astype(
                jnp.bfloat16
            )
            for t in range(2)
        ]
    )
    part = part.reshape(32, rows, 256)
    part = lax.all_to_all(part, ("core", "x", "y"), split_axis=0, concat_axis=0, tiled=True)
    part = part.reshape(2, 4, 4, rows, 2, HD).astype(jnp.float32)
    total = part[0] + part[1]
    return total.transpose(2, 3, 1, 0, 4).reshape(rows, 2 * 4 * 4 * HD)


def solution(mesh):
    fine = Mesh(mesh.devices.reshape(SIZES), NAMES)
    tensor = ("zh", "y")
    rows = ("x", "zb", "zq", "zh", "y")
    in_specs = (
        P("core", None, tensor, None, None),
        P("core", None, tensor, None, None),
        P("core", None, tensor, None, None),
        P("core", None, tensor, None),
        P("core", rows, None),
        P("core", rows, None),
        P("core", tensor, None),
        P("core", tensor, None),
        P("core"),
        P(),
        P(),
    )
    return jax.shard_map(
        body, mesh=fine, in_specs=in_specs, out_specs=P(rows, "core"), check_vma=False
    )
```

time: 724 us -> 257 us (0.35)
  waiting for transfers between devices: 354 us -> 68.3 us
  blocking collectives: 317 us -> 144 us
  matrix products: 15.3 us -> 4.57 us
    all_gather x3 -> x1, waiting for transfers between devices: 328 us -> 50.6 us  [body(): weight = lax.all_gather(weight, ('zh', 'zb', 'zq'), axis=0, tiled=True)]
    all_to_all x1 -> x2, blocking collectives: 174 us -> 82.3 us  [the longest x1 42 us: body(): lax.all_to_all(both, ('x', 'y'), split_axis=0, concat_axis=0, tiled=True)]
    all_gather x2 -> x1, blocking collectives: 143 us -> 61.2 us  [body(): packed = lax.all_gather(packed, 'zh', axis=0, tiled=False)]
    reduce_scatter x1 -> x0, waiting for transfers between devices: 26.1 us -> none  [body(): lax.psum_scatter(owned, 'tower', scatter_dimension=1, tiled=True)]
    all_to_all x0 -> x1, waiting for transfers between devices: none -> 17.8 us  [body(): lax.all_to_all(packed, 'y', split_axis=0, concat_axis=0, tiled=True)]
    dot_general x7 -> x2, matrix products: 15.3 us -> 4.57 us  [body(): lax.dot_general(both, halves[t], NT, preferred_element_type=jnp.float32)]
    unnamed x19 -> x12, local copies, waits for them, and re-layouts: 10.6 us -> 0.48 us
  transfers between devices with their start and end apart: 4 -> 2, of which waited for: 3 -> 2; matrix products, arithmetic and copies ran while one was open for 2% -> 3% of each run, Pallas kernels for 0% -> 2%
where the time goes in v1:
time: 257 us
  blocking collectives  144 us (56%)
  waiting for transfers between devices  68.3 us (27%)
  between operations  14.3 us (6%)
  local copies, waits for them, and re-layouts  13.4 us (5%)
  matrix products  4.57 us (2%)
  other arithmetic  4.27 us (2%)
  Pallas kernels  4.27 us (2%)
  starting transfers between devices  4.19 us (2%)
    all_gather x1, blocking collectives, body(): packed = lax.all_gather(packed, 'zh', axis=0, tiled=False)  61.2 us
    all_gather x1, waiting for transfers between devices, body(): weight = lax.all_gather(weight, ('zh', 'zb', 'zq'), axis=0, tiled=True)  50.6 us
    all_to_all x1, blocking collectives, body(): lax.all_to_all(both, ('x', 'y'), split_axis=0, concat_axis=0, tiled=True)  42 us
    all_to_all x1, blocking collectives, body(): lax.all_to_all(part, ('core', 'x', 'y'), split_axis=0, concat_axis=0, til...  40.4 us
    all_to_all x1, waiting for transfers between devices, body(): lax.all_to_all(packed, 'y', split_axis=0, concat_axis=0, tiled=True)  17.8 us
  transfers between devices with their start and end apart: 2, of which 2 were waited for; matrix products, arithmetic and copies ran while one was open for 3% of the time, Pallas kernels for 2%

profile of v1, /device:TPU:1, one launch (start us, length us, event | category | flops | bytes accessed | tf_op | source)
XLA Modules:
  0.0 256.8 jit_solution(8643389358759031293)
XLA Ops:
  7.3 1.3 dynamic_slice.32
  8.6 0.6 compare_convert_fusion
  9.3 0.9 convert_multiply_fusion.1
  10.1 1.1 fusion.4
  11.2 0.1 convert_element_type.63
  11.3 0.7 constant_dynamic-slice_fusion
  12.0 0.1 reshape.117
  12.1 0.1 fusion.6
  12.2 0.2 concatenate.9
  12.4 61.2 %all-gather = bf16[2112,128]{1,0:T(8,128)(2,1)S(1)} all-gather(bf16[528,128]{1,0:T(8,128)(2,1)S(1)} %concatenate.9), channel_id=2, replica_groups=mesh['core'=2,'x'=4,'zb'=2,'zq'=4,'zh'=4,'y'=4] {'zh'}, dimensions={0}, use_global_device_ids=true | all-gather | bytes 675840 | tf_op jit(solution)/shard_map/all_gather | solution.py:118
  73.6 1.6 broadcast_in_dim.7
  75.2 4.2 %all-to-all-start = ((bf16[4,4,528,128]{3,2,1,0:T(8,128)(2,1)}), bf16[4,4,528,128]{3,2,1,0:T(8,128)(2,1)S(1)}, u32[]{:S(2)}, u32[]{:S(2)}) async-start(bf16[4,4,528,128]{3,2,1,0:T(8,128)(2,1)} %broadcast_in_dim.7), calls=%async_computation | async-start | bytes 4325376 | tf_op jit(solution)/shard_map/all_to_all | solution.py:120
  79.4 0.8 dynamic-slice_bitcast_fusion
  80.2 0.6 pad_maximum_fusion.2
  80.9 0.6 dynamic_slice.35
  81.5 0.6 fusion.13.mask_ref
  82.1 17.8 %all-to-all-done.pack_ref = bf16[4,4,528,128]{3,2,1,0:T(8,128)(2,1)S(1)} async-done(((bf16[4,4,528,128]{3,2,1,0:T(8,128)(2,1)}), bf16[4,4,528,128]{3,2,1,0:T(8,128)(2,1)S(1)}, u32[]{:S(2)}, u32[]{:S(2)}) %all-to-all-start) | async-done | bytes 2162720 | tf_op jit(solution)/shard_map/all_to_all | solution.py:120
  99.9 4.3 %shard_map.109 = bf16[2,52,1024]{2,1,0:T(8,128)(2,1)S(1)} custom-call(bf16[4,4,528,128]{3,2,1,0:T(8,128)(2,1)S(1)} %all-to-all-done.pack_ref, bf16[1,52,1024]{2,1,0:T(8,128)(2,1)S(1)} %copy-done.1, bf16[1,52,1024]{2,1,0:T(8,128)(2,1)S(1)} %copy-done.2, f32[52,1]{1,0:T(8,128)S(1)} %fusion.13.mask_ref), custom_call_target="tpu_custom_call" | custom-call | flops 218103808 | bytes 3145728 | tf_op jit(solution)/shard_map/pallas_call | solution.py:49
  104.2 0.4 broadcast_in_dim.8
  104.7 42.0 %all_to_all.15 = bf16[16,52,2048]{2,1,0:T(8,128)(2,1)} all-to-all(bf16[16,52,2048]{2,1,0:T(8,128)(2,1)S(1)} %broadcast_in_dim.8), channel_id=1, replica_groups=mesh['core'=2,'x'=4,'zb'=2,'zq'=4,'zh'=4,'y'=4] {'x','y'}, dimensions={0} | all-to-all | bytes 6815744 | tf_op jit(solution)/shard_map/all_to_all | solution.py:131
  146.6 4.6 %reshape.118 = bf16[832,2048]{1,0:T(8,128)(2,1)} reshape(bf16[16,52,2048]{2,1,0:T(8,128)(2,1)} %all_to_all.15) | data formatting | bytes 6815744 | tf_op jit(solution)/shard_map/reshape | solution.py:132
  151.2 50.6 %all-gather.3.cloned.1.call-done = bf16[512,2048]{1,0:T(8,128)(2,1)} async-done(((bf16[16,2048]{1,0:T(8,128)(2,1)}), bf16[512,2048]{1,0:T(8,128)(2,1)}) %all-gather.3.cloned.1.call-update) | async-done | bytes 2097168 | tf_op jit(solution)/shard_map/all_gather | solution.py:95
  201.8 3.5 %fusion = bf16[1,832,256]{2,1,0:T(8,128)(2,1)S(1)} fusion(bf16[832,2048]{1,0:T(8,128)(2,1)} %reshape.118, bf16[512,2048]{1,0:T(8,128)(2,1)} %all-gather.3.cloned.1.call-done), kind=kOutput, calls=%fused_computation.2 | convolution fusion | flops 872628224 | bytes 4882432 | tf_op jit(solution)/shard_map/dot_general | solution.py:136
  205.3 0.5 copy-done.4
  205.7 1.1 fusion.1
  206.9 0.2 reshape.119
  207.1 40.4 %all_to_all.16 = bf16[32,52,256]{2,1,0:T(8,128)(2,1)S(1)} all-to-all(bf16[32,52,256]{2,1,0:T(8,128)(2,1)S(1)} %reshape.119), channel_id=1, replica_groups=mesh['core'=2,'x'=4,'zb'=2,'zq'=4,'zh'=4,'y'=4] {'core','x','y'}, dimensions={0} | all-to-all | bytes 1703936 | tf_op jit(solution)/shard_map/all_to_all | solution.py:143
  247.4 0.1 convert_element_type.67
  247.6 0.1 slice_add_fusion
  247.7 0.4 reshape.123
  248.2 0.6 copy.15
  248.7 1.3 reshape.120
  (20 shorter events, 0.3 us)
Async XLA Ops:
  6.5 4.8 %copy-start = (bf16[1,8,4,64,128]{4,3,2,1,0:T(8,128)(2,1)S(1)}, bf16[1,8,4,64,128]{4,3,2,1,0:T(8,128)(2,1)}, u32[]{:S(2)}) copy-start(bf16[1,8,4,64,128]{4,3,2,1,0:T(8,128)(2,1)} %param.11) | copy-start | bytes 1572868
  73.6 7.3 %copy-start.5 = (s32[8]{0:T(128)S(1)}, s32[8]{0:T(128)}, u32[]{:S(2)}) copy-start(s32[8]{0:T(128)} %param.20) | copy-start | bytes 100
  73.6 26.3 %copy-start.1 = (bf16[1,52,1024]{2,1,0:T(8,128)(2,1)S(1)}, bf16[1,52,1024]{2,1,0:T(8,128)(2,1)}, u32[]{:S(2)}) copy-start(bf16[1,52,1024]{2,1,0:T(8,128)(2,1)} %key_ref.1) | copy-start | bytes 319492
  73.6 26.3 %copy-start.2 = (bf16[1,52,1024]{2,1,0:T(8,128)(2,1)S(1)}, bf16[1,52,1024]{2,1,0:T(8,128)(2,1)}, u32[]{:S(2)}) copy-start(bf16[1,52,1024]{2,1,0:T(8,128)(2,1)} %value_ref.1) | copy-start | bytes 319492
  75.2 24.7 %all-to-all-start = ((bf16[4,4,528,128]{3,2,1,0:T(8,128)(2,1)}), bf16[4,4,528,128]{3,2,1,0:T(8,128)(2,1)S(1)}, u32[]{:S(2)}, u32[]{:S(2)}) async-start(bf16[4,4,528,128]{3,2,1,0:T(8,128)(2,1)} %broadcast_in_dim.7), calls=%async_computation | async-start | bytes 4325376 | tf_op jit(solution)/shard_map/all_to_all | solution.py:120
  79.4 122.4 %all-gather.3.cloned.1.call-start = ((), (), s32[]{:S(2)}) async-start(), calls=%async_computation.3 | async-start | bytes 2162688 | tf_op jit(solution)/shard_map/all_gather | solution.py:95
  201.8 3.5 %copy-start.3 = (bf16[832,2048]{1,0:T(8,128)(2,1)S(1)}, bf16[832,2048]{1,0:T(8,128)(2,1)}, u32[]{:S(2)}) copy-start(bf16[832,2048]{1,0:T(8,128)(2,1)} %reshape.118) | copy-start | bytes 10223620
  201.8 4.0 %copy-start.4 = (bf16[512,2048]{1,0:T(8,128)(2,1)S(1)}, bf16[512,2048]{1,0:T(8,128)(2,1)}, u32[]{:S(2)}) copy-start(bf16[512,2048]{1,0:T(8,128)(2,1)} %all-gather.3.cloned.1.call-done) | copy-start | bytes 6291460
Sparse Core Ops, SparseCore 0:
  82.9 118.8 all-gather.2

commit v2 on v1

--- a/solution.py
+++ b/solution.py
@@ -24,44 +24,50 @@
 NN = (((1,), (0,)), ((), ()))
 
 
-def attention_kernel(pack_ref, key_ref, value_ref, mask_ref, out_ref):
-    query = pack_ref[:, 0, 0:QROWS, :].reshape(2 * QROWS, HD)
-    grad = pack_ref[:, 0, QROWS : 2 * QROWS, :].reshape(2 * QROWS, HD)
-    meta = pack_ref[:, 0, META : META + 16, :].astype(jnp.float32)
+def attention_kernel(block_ref, pack_ref, key_ref, value_ref, mask_ref, done_ref, out_ref):
+    del block_ref, done_ref
+    query = pack_ref[:, 0:QROWS, :].reshape(2 * QROWS, HD)
+    grad = pack_ref[:, QROWS : 2 * QROWS, :].reshape(2 * QROWS, HD)
+    meta = pack_ref[:, META : META + 16, :].astype(jnp.float32)
     norm = jnp.concatenate([meta[i, j : j + 1] for i in range(2) for j in (0, 1)], axis=1)
     delta = jnp.concatenate([meta[i, j : j + 1] for i in range(2) for j in (2, 3)], axis=1)
     mask = mask_ref[...]
-    scores = lax.dot_general(key_ref[0], query, NT, preferred_element_type=jnp.float32) * SCALING
+    scores = lax.dot_general(key_ref[...], query, NT, preferred_element_type=jnp.float32) * SCALING
     attention = jnp.exp(scores - norm) * mask
     out_ref[1] = lax.dot_general(
         attention.astype(jnp.bfloat16), grad, NN, preferred_element_type=jnp.float32
     ).astype(jnp.bfloat16)
-    probs = lax.dot_general(value_ref[0], grad, NT, preferred_element_type=jnp.float32)
+    probs = lax.dot_general(value_ref[...], grad, NT, preferred_element_type=jnp.float32)
     grad_scores = (attention * (probs - delta)).astype(jnp.bfloat16)
     out_ref[0] = (
         lax.dot_general(grad_scores, query, NN, preferred_element_type=jnp.float32) * SCALING
     ).astype(jnp.bfloat16)
 
 
-def attention_grads(packed, keys, values, mask):
-    rows = keys.shape[1]
-    block = pl.BlockSpec((1, rows, HD), lambda g: (0, 0, g))
+def attention_grads(block, packed, keys, values, mask, done):
+    rows = keys.shape[0]
+    head = pl.BlockSpec((rows, HD), lambda p, b: (0, 2 * b[0] + p))
     return pl.pallas_call(
         attention_kernel,
-        grid=(KVH,),
-        in_specs=[
-            pl.BlockSpec((2, 1, PACK, HD), lambda g: (g % 2, g // 2, 0, 0)),
-            block,
-            block,
-            pl.BlockSpec((rows, 1), lambda g: (0, 0)),
-        ],
-        out_specs=pl.BlockSpec((2, rows, HD), lambda g: (0, 0, g)),
+        grid_spec=pltpu.PrefetchScalarGridSpec(
+            num_scalar_prefetch=1,
+            grid=(2,),
+            in_specs=[
+                pl.BlockSpec((2, PACK, HD), lambda p, b: (p, 0, 0)),
+                head,
+                head,
+                pl.BlockSpec((rows, 1), lambda p, b: (0, 0)),
+                pl.BlockSpec(memory_space=pl.ANY),
+            ],
+            out_specs=pl.BlockSpec((2, rows, HD), lambda p, b: (0, 0, 2 * b[0] + p)),
+        ),
         out_shape=jax.ShapeDtypeStruct((2, rows, KVH * HD), jnp.bfloat16),
+        input_output_aliases={5: 0},
         compiler_params=pltpu.CompilerParams(vmem_limit_bytes=16 * 1024 * 1024),
         cost_estimate=pl.CostEstimate(
-            flops=8 * rows * H * TXT * HD, bytes_accessed=3 << 20, transcendentals=rows * H * TXT
+            flops=2 * rows * H * TXT * HD, bytes_accessed=1 << 20, transcendentals=rows * H * TXT // 4
         ),
-    )(packed, keys, values, mask)
+    )(block, packed, keys, values, mask, done)
 
 
 def body(
@@ -115,21 +121,37 @@
         ],
         axis=0,
     )
-    packed = lax.all_gather(packed, "zh", axis=0, tiled=False)
-    packed = jnp.broadcast_to(packed[None], (4, 4, PACK, HD))
-    packed = lax.all_to_all(packed, "y", split_axis=0, concat_axis=0, tiled=True)
+    rows = image_keys.shape[1]
+    padded = -(-rows // 8) * 8
+    row = jnp.arange(padded)
+    position = (zq * 16 + zh * 4 + y) * rows + row
+    key_mask = (
+        (position // TILE_PAD < tile_counts[sample])
+        & (position % TILE_PAD < TILE_LEN)
+        & (row < rows)
+    ).astype(jnp.float32)
+    keys = jnp.pad(image_keys[0], ((0, padded - rows), (0, 0)))
+    values = jnp.pad(image_values[0], ((0, padded - rows), (0, 0)))
+    nothing = jnp.zeros((2, padded, KVH * HD), jnp.bfloat16)
 
-    rows = image_keys.shape[1]
-    position = (zq * 16 + zh * 4 + y) * rows + jnp.arange(rows)
-    key_mask = (
-        (position // TILE_PAD < tile_counts[sample]) & (position % TILE_PAD < TILE_LEN)
-    ).astype(jnp.float32)
-    grads = attention_grads(packed, image_keys, image_values, key_mask[:, None])
+    def attend(packed):
+        grads = nothing
+        for shift in (0, 1, 3, 2):
+            piece = packed
+            if shift:
+                piece = lax.ppermute(packed, "zh", [(i, (i + shift) % 4) for i in range(4)])
+            piece = jnp.broadcast_to(piece[None], (4, PACK, HD))
+            piece = lax.all_to_all(piece, "y", split_axis=0, concat_axis=0, tiled=True)
+            block = ((zh - shift) % 4).astype(jnp.int32).reshape(1)
+            grads = attention_grads(block, piece, keys, values, key_mask[:, None], grads)
+        return grads
+
+    grads = lax.cond(jnp.max(text_lens) > 0, attend, lambda _: nothing, packed)
 
     both = jnp.concatenate([grads[0], grads[1]], axis=1)
-    both = jnp.broadcast_to(both[None], (16, rows, 2 * KVH * HD))
+    both = jnp.broadcast_to(both[None], (16, padded, 2 * KVH * HD))
     both = lax.all_to_all(both, ("x", "y"), split_axis=0, concat_axis=0, tiled=True)
-    both = both.reshape(16 * rows, 2 * KVH * HD)
+    both = both.reshape(16 * padded, 2 * KVH * HD)
     halves = weight.reshape(2, 256, 2 * KVH * HD)
     part = jnp.stack(
         [
@@ -139,10 +161,10 @@
             for t in range(2)
         ]
     )
-    part = part.reshape(32, rows, 256)
+    part = part.reshape(32, padded, 256)
     part = lax.all_to_all(part, ("core", "x", "y"), split_axis=0, concat_axis=0, tiled=True)
-    part = part.reshape(2, 4, 4, rows, 2, HD).astype(jnp.float32)
-    total = part[0] + part[1]
+    part = part.reshape(2, 4, 4, padded, 2, HD).astype(jnp.float32)
+    total = (part[0] + part[1])[:, :, :rows]
     return total.transpose(2, 3, 1, 0, 4).reshape(rows, 2 * 4 * 4 * HD)
 
 

time: 257 us -> 249 us (0.969)
  the two profiles are of different devices: /device:TPU:1 before, /device:TPU:224 now
where the time goes in v2:
time: 249 us
  waiting for transfers between devices  86.2 us (35%)
  blocking collectives  67.4 us (27%)
  starting transfers between devices  50.6 us (20%)
  between operations  14.9 us (6%)
  local copies, waits for them, and re-layouts  13 us (5%)
  Pallas kernels  6.53 us (3%)
  other arithmetic  5.39 us (2%)
  matrix products  4.77 us (2%)
    ppermute x3, waiting for transfers between devices, attend(): piece = lax.ppermute(packed, 'zh', [(i, (i + shift) % 4) for i in range(4)])  82.3 us
    all_to_all x1, blocking collectives, body(): lax.all_to_all(both, ('x', 'y'), split_axis=0, concat_axis=0, tiled=True)  47.1 us
    ppermute x3, starting transfers between devices, attend(): piece = lax.ppermute(packed, 'zh', [(i, (i + shift) % 4) for i in range(4)])  33.6 us
    all_to_all x1, blocking collectives, body(): lax.all_to_all(part, ('core', 'x', 'y'), split_axis=0, concat_axis=0, til...  20.3 us
    all_to_all x4, starting transfers between devices, attend(): piece = lax.all_to_all(piece, 'y', split_axis=0, concat_axis=0, tiled=True)  17 us
    pallas_call x4, Pallas kernels, attention_grads(): pl.pallas_call(attention_kernel, grid_spec=pltpu.PrefetchScalarGridSpec(n...  6.53 us
  transfers between devices with their start and end apart: 8, of which 4 were waited for; matrix products, arithmetic and copies ran while one was open for 5% of the time, Pallas kernels for 3%

profile of v2, /device:TPU:224, one launch (start us, length us, event | category | flops | bytes accessed | tf_op | source)
XLA Modules:
  0.0 248.8 jit_solution(9979828296595498619)
XLA Ops:
  6.5 0.8 dynamic-slice_bitcast_fusion
  8.7 1.2 dynamic_slice.32
  10.6 0.9 convert_multiply_fusion.1
  11.4 1.1 fusion.4
  13.5 1.2 dynamic_slice.35
  14.7 1.3 reduce_max.9
  17.4 147.7 %conditional.1 = (bf16[2,56,1024]{2,1,0:T(8,128)(2,1)}) conditional(s32[]{:T(128)} %convert_element_type.54, () %tuple.11, (s32[]{:T(128)}, bf16[528,128]{1,0:T(8,128)(2,1)S(1)}, bf16[1,52,1024]{2,1,0:T(8,128)(2,1)}, bf16[1,52,1024]{2,1,0:T(8,128)(2,1)}, f32[56]{0:T(128)S(1)}) %tuple.12), branch_computations={%region_2.3_spmd, %region_3.4_spmd} | conditional | flops 234881072 | bytes 16532694 | solution.py:149
  17.5 0.9 broadcast_in_dim.7
  18.3 4.5 %all-to-all-start.3 = ((bf16[4,528,128]{2,1,0:T(8,128)(2,1)}), bf16[4,528,128]{2,1,0:T(8,128)(2,1)S(1)}, u32[]{:S(2)}, u32[]{:S(2)}) async-start(bf16[4,528,128]{2,1,0:T(8,128)(2,1)} %broadcast_in_dim.7), calls=%async_computation.3 | async-start | bytes 1081344 | tf_op jit(solution)/shard_map/cond/branch_1_fun/all_to_all | solution.py:144
  22.8 15.7 %collective-permute-start.2 = (bf16[528,128]{1,0:T(8,128)(2,1)S(1)}, bf16[528,128]{1,0:T(8,128)(2,1)S(1)}, u32[]{:S(2)}, u32[]{:S(2)}) collective-permute-start(bf16[528,128]{1,0:T(8,128)(2,1)S(1)} %get-tuple-element.25), channel_id=1, source_target_pairs={{0,4},{4,8},{8,12},{12,0},{1,5},{5,9},{9,13},{13,1},{2,6},{6,10},{... | collective-permute-start | bytes 405512 | tf_op jit(solution)/shard_map/cond/branch_1_fun/ppermute | solution.py:142
  38.5 24.8 %collective-permute-done.2 = bf16[528,128]{1,0:T(8,128)(2,1)S(1)} collective-permute-done((bf16[528,128]{1,0:T(8,128)(2,1)S(1)}, bf16[528,128]{1,0:T(8,128)(2,1)S(1)}, u32[]{:S(2)}, u32[]{:S(2)}) %collective-permute-start.2) | collective-permute-done | bytes 135200 | tf_op jit(solution)/shard_map/cond/branch_1_fun/ppermute | solution.py:142
  63.3 0.9 broadcast_in_dim.6
  64.2 4.6 %all-to-all-start.2 = ((bf16[4,528,128]{2,1,0:T(8,128)(2,1)}), bf16[4,528,128]{2,1,0:T(8,128)(2,1)S(1)}, u32[]{:S(2)}, u32[]{:S(2)}) async-start(bf16[4,528,128]{2,1,0:T(8,128)(2,1)} %broadcast_in_dim.6), calls=%async_computation.2 | async-start | bytes 1081344 | tf_op jit(solution)/shard_map/cond/branch_1_fun/all_to_all | solution.py:144
  68.8 10.4 %collective-permute-start.1 = (bf16[528,128]{1,0:T(8,128)(2,1)S(1)}, bf16[528,128]{1,0:T(8,128)(2,1)S(1)}, u32[]{:S(2)}, u32[]{:S(2)}) collective-permute-start(bf16[528,128]{1,0:T(8,128)(2,1)S(1)} %get-tuple-element.25), channel_id=1, source_target_pairs={{0,12},{4,0},{8,4},{12,8},{1,13},{5,1},{9,5},{13,9},{2,14},{6,2},{... | collective-permute-start | bytes 405512 | tf_op jit(solution)/shard_map/cond/branch_1_fun/ppermute | solution.py:142
  79.2 24.8 %collective-permute-done.1 = bf16[528,128]{1,0:T(8,128)(2,1)S(1)} collective-permute-done((bf16[528,128]{1,0:T(8,128)(2,1)S(1)}, bf16[528,128]{1,0:T(8,128)(2,1)S(1)}, u32[]{:S(2)}, u32[]{:S(2)}) %collective-permute-start.1) | collective-permute-done | bytes 135200 | tf_op jit(solution)/shard_map/cond/branch_1_fun/ppermute | solution.py:142
  104.1 0.9 broadcast_in_dim.5
  104.9 3.5 %all-to-all-start.1 = ((bf16[4,528,128]{2,1,0:T(8,128)(2,1)}), bf16[4,528,128]{2,1,0:T(8,128)(2,1)S(1)}, u32[]{:S(2)}, u32[]{:S(2)}) async-start(bf16[4,528,128]{2,1,0:T(8,128)(2,1)} %broadcast_in_dim.5), calls=%async_computation.1 | async-start | bytes 1081344 | tf_op jit(solution)/shard_map/cond/branch_1_fun/all_to_all | solution.py:144
  108.4 7.4 %collective-permute-start = (bf16[528,128]{1,0:T(8,128)(2,1)S(1)}, bf16[528,128]{1,0:T(8,128)(2,1)S(1)}, u32[]{:S(2)}, u32[]{:S(2)}) collective-permute-start(bf16[528,128]{1,0:T(8,128)(2,1)S(1)} %get-tuple-element.25), channel_id=1, source_target_pairs={{0,8},{4,12},{8,0},{12,4},{1,9},{5,13},{9,1},{13,5},{2,10},{6,14},... | collective-permute-start | bytes 405512 | tf_op jit(solution)/shard_map/cond/branch_1_fun/ppermute | solution.py:142
  115.9 32.7 %collective-permute-done = bf16[528,128]{1,0:T(8,128)(2,1)S(1)} collective-permute-done((bf16[528,128]{1,0:T(8,128)(2,1)S(1)}, bf16[528,128]{1,0:T(8,128)(2,1)S(1)}, u32[]{:S(2)}, u32[]{:S(2)}) %collective-permute-start) | collective-permute-done | bytes 135200 | tf_op jit(solution)/shard_map/cond/branch_1_fun/ppermute | solution.py:142
  148.5 0.9 broadcast_in_dim.1
  149.4 4.5 %all-to-all-start = ((bf16[4,528,128]{2,1,0:T(8,128)(2,1)}), bf16[4,528,128]{2,1,0:T(8,128)(2,1)S(1)}, u32[]{:S(2)}, u32[]{:S(2)}) async-start(bf16[4,528,128]{2,1,0:T(8,128)(2,1)} %broadcast_in_dim.1), calls=%async_computation | async-start | bytes 1081344 | tf_op jit(solution)/shard_map/cond/branch_1_fun/all_to_all | solution.py:144
  154.8 1.6 branch_1_fun.4.done_ref
  156.4 1.6 branch_1_fun.5.done_ref
  158.0 1.6 branch_1_fun.6.done_ref
  159.7 3.8 %all-to-all-done.pack_ref = bf16[4,528,128]{2,1,0:T(8,128)(2,1)S(1)} async-done(((bf16[4,528,128]{2,1,0:T(8,128)(2,1)}), bf16[4,528,128]{2,1,0:T(8,128)(2,1)S(1)}, u32[]{:S(2)}, u32[]{:S(2)}) %all-to-all-start) | async-done | bytes 540704 | tf_op jit(solution)/shard_map/cond/branch_1_fun/all_to_all | solution.py:144
  163.5 1.6 branch_1_fun.7
  165.1 1.0 slice_bitcast_fusion.1
  166.5 47.1 %all_to_all.26 = bf16[16,56,2048]{2,1,0:T(8,128)(2,1)} all-to-all(bf16[16,56,2048]{2,1,0:T(8,128)(2,1)S(1)} %broadcast_in_dim.20), channel_id=1, replica_groups=mesh['core'=2,'x'=4,'zb'=2,'zq'=4,'zh'=4,'y'=4] {'x','y'}, dimensions={0} | all-to-all | bytes 7340032 | tf_op jit(solution)/shard_map/all_to_all | solution.py:153
  213.7 3.6 %fusion = bf16[1,896,256]{2,1,0:T(8,128)(2,1)S(1)} fusion(bf16[896,2048]{1,0:T(8,128)(2,1)} %bitcast.43, bf16[512,2048]{1,0:T(8,128)(2,1)} %all-gather.2.cloned.1.call-done), kind=kOutput, calls=%fused_computation.2 | convolution fusion | flops 939753472 | bytes 5177344 | tf_op jit(solution)/shard_map/dot_general | solution.py:158
  217.8 1.1 fusion.1
  219.0 20.3 %all_to_all.27 = bf16[32,56,256]{2,1,0:T(8,128)(2,1)S(1)} all-to-all(bf16[32,56,256]{2,1,0:T(8,128)(2,1)S(1)} %bitcast.45), channel_id=1, replica_groups=mesh['core'=2,'x'=4,'zb'=2,'zq'=4,'zh'=4,'y'=4] {'core','x','y'}, dimensions={0} | all-to-all | bytes 1835008 | tf_op jit(solution)/shard_map/all_to_all | solution.py:165
  240.7 1.3 reshape.80
  (40 shorter events, 6.2 us)
Async XLA Ops:
  6.5 6.0 %copy-start = (bf16[1,8,4,64,128]{4,3,2,1,0:T(8,128)(2,1)S(1)}, bf16[1,8,4,64,128]{4,3,2,1,0:T(8,128)(2,1)}, u32[]{:S(2)}) copy-start(bf16[1,8,4,64,128]{4,3,2,1,0:T(8,128)(2,1)} %param.13) | copy-start | bytes 1572868
  6.5 207.1 %all-gather.2.cloned.1.call-start = ((), (), s32[]{:S(2)}) async-start(), calls=%async_computation.6 | async-start | bytes 2162688 | tf_op jit(solution)/shard_map/all_gather | solution.py:101
  17.4 136.5 %copy-start.2 = (bf16[1,52,1024]{2,1,0:T(8,128)(2,1)S(1)}, bf16[1,52,1024]{2,1,0:T(8,128)(2,1)}, u32[]{:S(2)}) copy-start(bf16[1,52,1024]{2,1,0:T(8,128)(2,1)} %get-tuple-element.31) | copy-start | bytes 319492 | tf_op jit(solution)/shard_map/cond
  17.4 136.5 %copy-start.3 = (bf16[1,52,1024]{2,1,0:T(8,128)(2,1)S(1)}, bf16[1,52,1024]{2,1,0:T(8,128)(2,1)}, u32[]{:S(2)}) copy-start(bf16[1,52,1024]{2,1,0:T(8,128)(2,1)} %get-tuple-element.32) | copy-start | bytes 319492 | tf_op jit(solution)/shard_map/cond
  18.3 45.0 %all-to-all-start.3 = ((bf16[4,528,128]{2,1,0:T(8,128)(2,1)}), bf16[4,528,128]{2,1,0:T(8,128)(2,1)S(1)}, u32[]{:S(2)}, u32[]{:S(2)}) async-start(bf16[4,528,128]{2,1,0:T(8,128)(2,1)} %broadcast_in_dim.7), calls=%async_computation.3 | async-start | bytes 1081344 | tf_op jit(solution)/shard_map/cond/branch_1_fun/all_to_all | solution.py:144
  22.8 40.5 %collective-permute-start.2 = (bf16[528,128]{1,0:T(8,128)(2,1)S(1)}, bf16[528,128]{1,0:T(8,128)(2,1)S(1)}, u32[]{:S(2)}, u32[]{:S(2)}) collective-permute-start(bf16[528,128]{1,0:T(8,128)(2,1)S(1)} %get-tuple-element.25), channel_id=1, source_target_pairs={{0,4},{4,8},{8,12},{12,0},{1,5},{5,9},{9,13},{13,1},{2,6},{6,10},{... | collective-permute-start | bytes 405512 | tf_op jit(solution)/shard_map/cond/branch_1_fun/ppermute | solution.py:142
  64.2 39.8 %all-to-all-start.2 = ((bf16[4,528,128]{2,1,0:T(8,128)(2,1)}), bf16[4,528,128]{2,1,0:T(8,128)(2,1)S(1)}, u32[]{:S(2)}, u32[]{:S(2)}) async-start(bf16[4,528,128]{2,1,0:T(8,128)(2,1)} %broadcast_in_dim.6), calls=%async_computation.2 | async-start | bytes 1081344 | tf_op jit(solution)/shard_map/cond/branch_1_fun/all_to_all | solution.py:144
  68.8 35.3 %collective-permute-start.1 = (bf16[528,128]{1,0:T(8,128)(2,1)S(1)}, bf16[528,128]{1,0:T(8,128)(2,1)S(1)}, u32[]{:S(2)}, u32[]{:S(2)}) collective-permute-start(bf16[528,128]{1,0:T(8,128)(2,1)S(1)} %get-tuple-element.25), channel_id=1, source_target_pairs={{0,12},{4,0},{8,4},{12,8},{1,13},{5,1},{9,5},{13,9},{2,14},{6,2},{... | collective-permute-start | bytes 405512 | tf_op jit(solution)/shard_map/cond/branch_1_fun/ppermute | solution.py:142
  104.9 43.6 %all-to-all-start.1 = ((bf16[4,528,128]{2,1,0:T(8,128)(2,1)}), bf16[4,528,128]{2,1,0:T(8,128)(2,1)S(1)}, u32[]{:S(2)}, u32[]{:S(2)}) async-start(bf16[4,528,128]{2,1,0:T(8,128)(2,1)} %broadcast_in_dim.5), calls=%async_computation.1 | async-start | bytes 1081344 | tf_op jit(solution)/shard_map/cond/branch_1_fun/all_to_all | solution.py:144
  108.4 40.1 %collective-permute-start = (bf16[528,128]{1,0:T(8,128)(2,1)S(1)}, bf16[528,128]{1,0:T(8,128)(2,1)S(1)}, u32[]{:S(2)}, u32[]{:S(2)}) collective-permute-start(bf16[528,128]{1,0:T(8,128)(2,1)S(1)} %get-tuple-element.25), channel_id=1, source_target_pairs={{0,8},{4,12},{8,0},{12,4},{1,9},{5,13},{9,1},{13,5},{2,10},{6,14},... | collective-permute-start | bytes 405512 | tf_op jit(solution)/shard_map/cond/branch_1_fun/ppermute | solution.py:142
  149.4 14.1 %all-to-all-start = ((bf16[4,528,128]{2,1,0:T(8,128)(2,1)}), bf16[4,528,128]{2,1,0:T(8,128)(2,1)S(1)}, u32[]{:S(2)}, u32[]{:S(2)}) async-start(bf16[4,528,128]{2,1,0:T(8,128)(2,1)} %broadcast_in_dim.1), calls=%async_computation | async-start | bytes 1081344 | tf_op jit(solution)/shard_map/cond/branch_1_fun/all_to_all | solution.py:144
  213.7 3.6 %copy-start.1 = (bf16[16,56,2048]{2,1,0:T(8,128)(2,1)S(1)}, bf16[16,56,2048]{2,1,0:T(8,128)(2,1)}, u32[]{:S(2)}) copy-start(bf16[16,56,2048]{2,1,0:T(8,128)(2,1)} %all_to_all.26) | copy-start | bytes 11010052
  213.7 4.1 %copy-start.4 = (bf16[512,2048]{1,0:T(8,128)(2,1)S(1)}, bf16[512,2048]{1,0:T(8,128)(2,1)}, u32[]{:S(2)}) copy-start(bf16[512,2048]{1,0:T(8,128)(2,1)} %all-gather.2.cloned.1.call-done) | copy-start | bytes 6291460
Sparse Core Ops, SparseCore 0:
  10.0 174.9 all-gather.1

commit v3 on v1

v3 whole, which is shorter than its diff:
```python
import math

import jax
import jax.numpy as jnp
from jax import lax
from jax.experimental import pallas as pl
from jax.experimental.pallas import tpu as pltpu
from jax.sharding import Mesh, PartitionSpec as P

KVH = 8
HD = 128
TXT = 64
TILE_LEN = 1601
TILE_PAD = 1664
NAMES = ("core", "x", "zb", "zq", "zh", "y")
SIZES = (2, 4, 2, 4, 4, 4)
SCALING = 1.0 / math.sqrt(HD)
META = 2 * TXT
PACK = META + 16
ROWS = 52
GROUP = 8 * TXT
SLICE = 16
NT = (((1,), (1,)), ((), ()))
NN = (((1,), (0,)), ((), ()))
VMEM_LIMIT = 16 * 1024 * 1024


def prepare_kernel(
    gate_ref,
    length_ref,
    query_ref,
    out_ref,
    cot_ref,
    norm_ref,
    key_weight_ref,
    value_weight_ref,
    pack_ref,
    weight_ref,
    query,
    out,
    cot,
    key_weight,
    value_weight,
    sems,
):
    x, zb, zq = (lax.axis_index(name) for name in ("x", "zb", "zq"))
    sample = x * 2 + zb
    feature = pl.multiple_of(x * 128 + (zb * 4 + zq) * SLICE, SLICE)
    copies = [
        pltpu.make_async_copy(source, target, sems.at[i])
        for i, (source, target) in enumerate(
            [
                (key_weight_ref.at[0, pl.ds(feature, SLICE)], key_weight),
                (value_weight_ref.at[0, pl.ds(feature, SLICE)], value_weight),
                (cot_ref.at[0, sample, zq], cot),
                (out_ref.at[0, sample, zq], out),
                (query_ref.at[0, sample, zq], query),
            ]
        )
    ]
    for copy in copies:
        copy.start()
    copies[0].wait()
    copies[1].wait()
    for g in range(KVH):
        weight_ref[:, 2 * g * HD : (2 * g + 1) * HD] = key_weight[:, g * HD : (g + 1) * HD]
        weight_ref[:, (2 * g + 1) * HD : (2 * g + 2) * HD] = value_weight[:, g * HD : (g + 1) * HD]

    head = lax.broadcasted_iota(jnp.int32, (4, HD), 0) == zq
    place = lax.broadcasted_iota(jnp.int32, (TXT, HD), 0)
    lane = lax.broadcasted_iota(jnp.int32, (TXT, HD), 1)
    twice = jnp.where(lane % TXT == place, 1.0, 0.0).astype(jnp.bfloat16)
    norms = lax.dot_general(norm_ref[0, sample], twice, NN, preferred_element_type=jnp.float32)
    norm = jnp.sum(jnp.where(head, norms, 0.0), axis=0, keepdims=True)

    copies[2].wait()
    row_mask = jnp.where(place < length_ref[sample], 1.0, 0.0)
    gate = jnp.tanh(jnp.full((TXT, HD), gate_ref[0], jnp.float32))
    scaled = (gate * cot[...].astype(jnp.float32) * row_mask).astype(jnp.bfloat16)
    pack_ref[TXT : 2 * TXT] = scaled
    copies[3].wait()
    product = scaled.astype(jnp.float32) * out[...].astype(jnp.float32)
    product = jnp.concatenate([product, product], axis=0)
    delta = jnp.sum(product.T, axis=0, keepdims=True)
    row = lax.broadcasted_iota(jnp.int32, (16, HD), 0)
    pack_ref[META : META + 16] = jnp.where(
        row == 0, norm, jnp.where(row == 1, delta, 0.0)
    ).astype(jnp.bfloat16)
    copies[4].wait()
    pack_ref[0:TXT] = query[...]


def prepare(layer_gate, text_lens, query, out, cot, norm, key_weight, value_weight):
    whole = pl.BlockSpec(memory_space=pl.ANY)
    vmem = pl.BlockSpec(memory_space=pltpu.VMEM)
    smem = pl.BlockSpec(memory_space=pltpu.SMEM)
    head = pltpu.VMEM((TXT, HD), jnp.bfloat16)
    rows = pltpu.VMEM((SLICE, KVH * HD), jnp.bfloat16)
    return pl.pallas_call(
        prepare_kernel,
        in_specs=[smem, smem, whole, whole, whole, vmem, whole, whole],
        out_specs=[vmem, vmem],
        out_shape=[
            jax.ShapeDtypeStruct((PACK, HD), jnp.bfloat16),
            jax.ShapeDtypeStruct((SLICE, 2 * KVH * HD), jnp.bfloat16),
        ],
        scratch_shapes=[head, head, head, rows, rows, pltpu.SemaphoreType.DMA((5,))],
        compiler_params=pltpu.CompilerParams(vmem_limit_bytes=VMEM_LIMIT),
        cost_estimate=pl.CostEstimate(flops=1 << 16, bytes_accessed=1 << 18, transcendentals=8192),
    )(layer_gate, text_lens, query, out, cot, norm, key_weight, value_weight)


def attention_kernel(tiles_ref, pack_ref, key_ref, value_ref, out_ref):
    rows = key_ref.shape[0]
    x, zb, zq, zh, y = (lax.axis_index(name) for name in ("x", "zb", "zq", "zh", "y"))
    tiles = tiles_ref[x * 2 + zb]
    row = lax.broadcasted_iota(jnp.int32, (rows, GROUP), 0)
    position = (zq * 16 + zh * 4 + y) * ROWS + row
    second = position >= TILE_PAD
    inside = jnp.where(second, position - TILE_PAD, position) < TILE_LEN
    present = jnp.where(second, 1, 0) < tiles
    mask = jnp.where(inside & present & (row < ROWS), 1.0, 0.0)

    query = pack_ref[:, :, 0, 0:TXT, :].reshape(GROUP, HD)
    grad = pack_ref[:, :, 0, TXT : 2 * TXT, :].reshape(GROUP, HD)
    meta = pack_ref[:, :, 0, META : META + 16, :].astype(jnp.float32)
    left = lax.broadcasted_iota(jnp.int32, (1, HD), 1) < TXT

    def line(which):
        picked = [meta[i // 4, i % 4, which : which + 1] for i in range(8)]
        return jnp.concatenate(
            [jnp.where(left, picked[i], picked[i + 1]) for i in range(0, 8, 2)], axis=1
        )

    scores = lax.dot_general(key_ref[...], query, NT, preferred_element_type=jnp.float32) * SCALING
    attention = jnp.exp(scores - line(0)) * mask
    value_grad = lax.dot_general(
        attention.astype(jnp.bfloat16), grad, NN, preferred_element_type=jnp.float32
    )
    probs = lax.dot_general(value_ref[...], grad, NT, preferred_element_type=jnp.float32)
    grad_scores = (attention * (probs - line(1))).astype(jnp.bfloat16)
    key_grad = lax.dot_general(grad_scores, query, NN, preferred_element_type=jnp.float32) * SCALING
    out_ref[:, 0:HD] = key_grad.astype(jnp.bfloat16)
    out_ref[:, HD : 2 * HD] = value_grad.astype(jnp.bfloat16)


def attention_grads(tiles, packed, keys, values):
    rows = keys.shape[0]
    head = pl.BlockSpec((rows, HD), lambda g: (0, g))
    return pl.pallas_call(
        attention_kernel,
        grid=(KVH,),
        in_specs=[
            pl.BlockSpec(memory_space=pltpu.SMEM),
            pl.BlockSpec((2, 4, 1, PACK, HD), lambda g: (g % 2, 0, g // 2, 0, 0)),
            head,
            head,
        ],
        out_specs=pl.BlockSpec((rows, 2 * HD), lambda g: (0, g)),
        out_shape=jax.ShapeDtypeStruct((rows, 2 * KVH * HD), jnp.bfloat16),
        compiler_params=pltpu.CompilerParams(vmem_limit_bytes=VMEM_LIMIT),
        cost_estimate=pl.CostEstimate(
            flops=8 * rows * KVH * GROUP * HD,
            bytes_accessed=3 << 20,
            transcendentals=rows * KVH * GROUP,
        ),
    )(tiles, packed, keys, values)


def to_all(array, axes, count):
    copies = jnp.broadcast_to(array[None], (count, *array.shape))
    return lax.all_to_all(copies, axes, split_axis=0, concat_axis=0, tiled=True)


def body(
    text_query,
    attn_out,
    grad_out,
    log_norm,
    image_keys,
    image_values,
    k_weight,
    v_weight,
    layer_gate,
    tile_counts,
    text_lens,
):
    rows = image_keys.shape[1]
    padded = -(-rows // 8) * 8
    packed, weight = prepare(
        layer_gate, text_lens, text_query, attn_out, grad_out, log_norm, k_weight, v_weight
    )
    weight = lax.all_gather(weight, ("zh", "zb", "zq"), axis=0, tiled=True)

    keys = jnp.pad(image_keys[0], ((0, padded - rows), (0, 0)))
    values = jnp.pad(image_values[0], ((0, padded - rows), (0, 0)))

    def attend(packed):
        packed = lax.all_gather(packed, "zh", axis=0, tiled=False)
        packed = to_all(packed, "zq", 4)
        packed = to_all(packed, "y", 4)
        return attention_grads(tile_counts, packed, keys, values)

    both = lax.cond(
        jnp.max(text_lens) > 0,
        attend,
        lambda _: jnp.zeros((padded, 2 * KVH * HD), jnp.bfloat16),
        packed,
    )

    both = to_all(both, ("x", "y"), 16).reshape(16 * padded, 2 * KVH * HD)
    halves = weight.reshape(2, 256, 2 * KVH * HD)
    part = jnp.stack(
        [
            lax.dot_general(both, halves[t], NT, preferred_element_type=jnp.float32).astype(
                jnp.bfloat16
            )
            for t in range(2)
        ]
    )
    part = part.reshape(32, padded, 256)
    part = lax.all_to_all(part, ("core", "x", "y"), split_axis=0, concat_axis=0, tiled=True)
    part = part.reshape(2, 4, 4, padded, 2, HD).astype(jnp.float32)
    total = (part[0] + part[1])[:, :, :rows]
    return total.transpose(2, 3, 1, 0, 4).reshape(rows, 2 * 4 * 4 * HD)


def solution(mesh):
    fine = Mesh(mesh.devices.reshape(SIZES), NAMES)
    tensor = ("zh", "y")
    rows = ("x", "zb", "zq", "zh", "y")
    in_specs = (
        P("core", None, tensor, None, None),
        P("core", None, tensor, None, None),
        P("core", None, tensor, None, None),
        P("core", None, tensor, None),
        P("core", rows, None),
        P("core", rows, None),
        P("core", tensor, None),
        P("core", tensor, None),
        P("core"),
        P(),
        P(),
    )
    return jax.shard_map(
        body, mesh=fine, in_specs=in_specs, out_specs=P(rows, "core"), check_vma=False
    )
```

time: 257 us -> 202 us (0.79)
  waiting for transfers between devices: 68.3 us -> 22.6 us
  blocking collectives: 144 us -> 135 us
  other arithmetic: 4.27 us -> 1.05 us
    all_gather x1, waiting for transfers between devices: 50.6 us -> 0.01 us  [body(): weight = lax.all_gather(weight, ('zh', 'zb', 'zq'), axis=0, tiled=True)]
    all_gather x1, blocking collectives: 61.2 us -> 42.3 us  [attend(): packed = lax.all_gather(packed, 'zh', axis=0, tiled=False)]
    all_to_all x1 -> x2, blocking collectives: 42 us -> 58.4 us  [to_all(): return lax.all_to_all(copies, axes, split_axis=0, concat_axis=0, tiled=True)]
    unnamed x12 -> x27, local copies, waits for them, and re-layouts: 0.48 us -> 7.97 us
    all_to_all x1, blocking collectives: 40.4 us -> 34.1 us  [body(): lax.all_to_all(part, ('core', 'x', 'y'), split_axis=0, concat_axis=0, til...]
    reshape x3 -> x0, local copies, waits for them, and re-layouts: 4.82 us -> none  [the longest x1 4.58 us: body(): both = both.reshape(16 * rows, 2 * KVH * HD)]
    all_to_all x1, waiting for transfers between devices: 17.8 us -> 22.5 us  [to_all(): return lax.all_to_all(copies, axes, split_axis=0, concat_axis=0, tiled=True)]
    dynamic_slice x5 -> x0, local copies, waits for them, and re-layouts: 3.36 us -> none  [the longest x1 1.27 us: body(): row_mask = (jnp.arange(TXT) < text_lens[sample]).astype(jnp.float32)]
  transfers between devices with their start and end apart: 2 -> 2, of which waited for: 2 -> 1; matrix products, arithmetic and copies ran while one was open for 3% -> 2% of each run, Pallas kernels for 2% -> 2%
where the time goes in v3:
time: 202 us; the launch traced here: 201 us
  blocking collectives  135 us (67%)
  waiting for transfers between devices  22.6 us (11%)
  between operations  14.9 us (7%)
  local copies, waits for them, and re-layouts  12.2 us (6%)
  Pallas kernels  6.51 us (3%)
  matrix products  4.78 us (2%)
  starting transfers between devices  4.58 us (2%)
    all_to_all x2, blocking collectives, to_all(): return lax.all_to_all(copies, axes, split_axis=0, concat_axis=0, tiled=True)  58.4 us
    all_gather x1, blocking collectives, attend(): packed = lax.all_gather(packed, 'zh', axis=0, tiled=False)  42.3 us
    all_to_all x1, blocking collectives, body(): lax.all_to_all(part, ('core', 'x', 'y'), split_axis=0, concat_axis=0, til...  34.1 us
    all_to_all x1, waiting for transfers between devices, to_all(): return lax.all_to_all(copies, axes, split_axis=0, concat_axis=0, tiled=True)  22.5 us
    unnamed x27, local copies, waits for them, and re-layouts  7.97 us
    pallas_call x1, Pallas kernels, attention_grads(): pl.pallas_call(attention_kernel, grid=(KVH,), in_specs=[pl.BlockSpec(memo...  4.87 us
    dot_general x2, matrix products, body(): lax.dot_general(both, halves[t], NT, preferred_element_type=jnp.float32)  4.78 us
    all_to_all x1, starting transfers between devices, to_all(): return lax.all_to_all(copies, axes, split_axis=0, concat_axis=0, tiled=True)  4.58 us
  transfers between devices with their start and end apart: 2, of which 1 were waited for; matrix products, arithmetic and copies ran while one was open for 2% of the time, Pallas kernels for 2%

profile of v3, /device:TPU:1, one launch (start us, length us, event | category | flops | bytes accessed | tf_op | source)
XLA Modules:
  0.0 201.4 jit_solution(4969792136464234220)
XLA Ops:
  7.2 1.2 copy-done
  8.4 1.2 copy-done.1
  9.7 1.0 copy-done.2
  10.7 1.0 copy-done.3
  11.8 1.0 copy-done.4
  12.8 0.7 copy-done.5
  13.5 0.7 copy-done.6
  14.2 1.6 shard_map.112
  15.8 0.0 all-gather.3.cloned.1.call-update
  15.8 0.7 reduce_max.9
  17.2 0.0 copy-done.11
  17.3 92.3 %conditional.1 = (bf16[56,2048]{1,0:T(8,128)(2,1)S(1)}) conditional(s32[]{:T(128)} %convert_element_type.16, () %tuple.13, (bf16[144,128]{1,0:T(8,128)(2,1)S(1)}, bf16[1,52,1024]{2,1,0:T(8,128)(2,1)S(1)}, bf16[1,52,1024]{2,1,0:T(8,128)(2,1)S(1)}, s32[8]{0:T(128)S(1)}) %tuple.21), branch_computations={%region_1.2_spmd, %region_2.3_spmd} | conditional | flops 234881024 | bytes 15716396 | solution.py:204
  17.3 42.3 %all-gather = bf16[576,128]{1,0:T(8,128)(2,1)S(1)} all-gather(bf16[144,128]{1,0:T(8,128)(2,1)S(1)} %get-tuple-element.23), channel_id=2, replica_groups=mesh['core'=2,'x'=4,'zb'=2,'zq'=4,'zh'=4,'y'=4] {'zh'}, dimensions={0}, use_global_device_ids=true | all-gather | bytes 184320 | tf_op jit(solution)/shard_map/cond/branch_1_fun/all_gather | solution.py:199
  59.6 0.1 broadcast_in_dim.0
  59.7 16.0 %all_to_all.18 = bf16[4,4,144,128]{3,2,1,0:T(8,128)(2,1)S(1)} all-to-all(bf16[4,4,144,128]{3,2,1,0:T(8,128)(2,1)S(1)} %broadcast_in_dim.0), channel_id=1, replica_groups=mesh['core'=2,'x'=4,'zb'=2,'zq'=4,'zh'=4,'y'=4] {'zq'}, dimensions={0} | all-to-all | bytes 1179648 | tf_op jit(solution)/shard_map/cond/branch_1_fun/all_to_all | solution.py:172
  75.7 1.9 broadcast_in_dim.1
  77.5 4.6 %all-to-all-start.1 = ((bf16[4,4,4,144,128]{4,3,2,1,0:T(8,128)(2,1)}), bf16[4,4,4,144,128]{4,3,2,1,0:T(8,128)(2,1)S(1)}, u32[]{:S(2)}, u32[]{:S(2)}) async-start(bf16[4,4,4,144,128]{4,3,2,1,0:T(8,128)(2,1)} %broadcast_in_dim.1), calls=%async_computation.1 | async-start | bytes 4718592 | tf_op jit(solution)/shard_map/cond/branch_1_fun/all_to_all | solution.py:172
  82.1 22.5 %all-to-all-done.1.pack_ref = bf16[4,4,4,144,128]{4,3,2,1,0:T(8,128)(2,1)S(1)} async-done(((bf16[4,4,4,144,128]{4,3,2,1,0:T(8,128)(2,1)}), bf16[4,4,4,144,128]{4,3,2,1,0:T(8,128)(2,1)S(1)}, u32[]{:S(2)}, u32[]{:S(2)}) %all-to-all-start.1) | async-done | bytes 2359328 | tf_op jit(solution)/shard_map/cond/branch_1_fun/all_to_all | solution.py:172
  104.7 4.9 %branch_1_fun.1 = bf16[56,2048]{1,0:T(8,128)(2,1)S(1)} custom-call(s32[8]{0:T(128)S(1)} %get-tuple-element.35.tiles_ref, bf16[4,4,4,144,128]{4,3,2,1,0:T(8,128)(2,1)S(1)} %all-to-all-done.1.pack_ref, bf16[56,1024]{1,0:T(8,128)(2,1)S(1)} %pad.7.key_ref, bf16[56,1024]{1,0:T(8,128)(2,1)S(1)} %pad.8.value_ref), custom_call_target="tpu_custom_call" | custom-call | flops 234881024 | bytes 3145728 | tf_op jit(solution)/shard_map/cond/branch_1_fun/pallas_call | solution.py:150
  109.6 0.4 broadcast_in_dim.6
  110.0 42.4 %all_to_all.19 = bf16[16,56,2048]{2,1,0:T(8,128)(2,1)} all-to-all(bf16[16,56,2048]{2,1,0:T(8,128)(2,1)S(1)} %broadcast_in_dim.6), channel_id=1, replica_groups=mesh['core'=2,'x'=4,'zb'=2,'zq'=4,'zh'=4,'y'=4] {'x','y'}, dimensions={0} | all-to-all | bytes 7340032 | tf_op jit(solution)/shard_map/all_to_all | solution.py:172
  152.4 3.6 %fusion = bf16[1,896,256]{2,1,0:T(8,128)(2,1)S(1)} fusion(bf16[896,2048]{1,0:T(8,128)(2,1)} %bitcast.14, bf16[512,2048]{1,0:T(8,128)(2,1)} %all-gather.3.cloned.1.call-done), kind=kOutput, calls=%fused_computation.2 | convolution fusion | flops 939753472 | bytes 5177344 | tf_op jit(solution)/shard_map/dot_general | solution.py:215
  156.1 0.5 copy-done.12
  156.6 1.1 fusion.1
  157.7 0.1 pad_maximum_fusion
  157.8 34.1 %all_to_all.20 = bf16[32,56,256]{2,1,0:T(8,128)(2,1)S(1)} all-to-all(bf16[32,56,256]{2,1,0:T(8,128)(2,1)S(1)} %bitcast.16), channel_id=1, replica_groups=mesh['core'=2,'x'=4,'zb'=2,'zq'=4,'zh'=4,'y'=4] {'core','x','y'}, dimensions={0} | all-to-all | bytes 1835008 | tf_op jit(solution)/shard_map/all_to_all | solution.py:222
  192.0 0.1 convert_element_type.19
  192.1 0.1 slice_add_fusion
  192.2 0.5 add.12
  192.7 0.1 slice.28
  192.8 0.6 copy.18
  193.3 1.3 reshape.26
  (21 shorter events, 0.1 us)
Async XLA Ops:
  6.5 9.3 %copy-start.7 = (s32[8]{0:T(128)S(1)}, s32[8]{0:T(128)}, u32[]{:S(2)}) copy-start(s32[8]{0:T(128)} %length_ref.1) | copy-start | bytes 100
  6.5 10.7 %copy-start.11 = (s32[8]{0:T(128)S(1)}, s32[8]{0:T(128)}, u32[]{:S(2)}) copy-start(s32[8]{0:T(128)} %param.22) | copy-start | bytes 100
  6.5 145.9 %all-gather.3.cloned.1.call-start = ((), (), s32[]{:S(2)}) async-start(), calls=%async_computation.4 | async-start | bytes 2162688 | tf_op jit(solution)/shard_map/all_gather | solution.py:193
  7.2 1.2 copy-start
  8.4 1.2 copy-start.1
  9.7 1.0 copy-start.2
  10.7 1.0 copy-start.3
  11.8 1.0 copy-start.4
  12.8 0.7 copy-start.5
  13.5 0.7 copy-start.6
  14.1 3.1 %copy-start.9 = (bf16[1,52,1024]{2,1,0:T(8,128)(2,1)S(1)}, bf16[1,52,1024]{2,1,0:T(8,128)(2,1)}, u32[]{:S(2)}) copy-start(bf16[1,52,1024]{2,1,0:T(8,128)(2,1)} %param.17) | copy-start | bytes 319492
  14.2 3.1 %copy-start.10 = (bf16[1,52,1024]{2,1,0:T(8,128)(2,1)S(1)}, bf16[1,52,1024]{2,1,0:T(8,128)(2,1)}, u32[]{:S(2)}) copy-start(bf16[1,52,1024]{2,1,0:T(8,128)(2,1)} %param.18) | copy-start | bytes 319492
  77.5 27.1 %all-to-all-start.1 = ((bf16[4,4,4,144,128]{4,3,2,1,0:T(8,128)(2,1)}), bf16[4,4,4,144,128]{4,3,2,1,0:T(8,128)(2,1)S(1)}, u32[]{:S(2)}, u32[]{:S(2)}) async-start(bf16[4,4,4,144,128]{4,3,2,1,0:T(8,128)(2,1)} %broadcast_in_dim.1), calls=%async_computation.1 | async-start | bytes 4718592 | tf_op jit(solution)/shard_map/cond/branch_1_fun/all_to_all | solution.py:172
  152.4 3.6 %copy-start.8 = (bf16[16,56,2048]{2,1,0:T(8,128)(2,1)S(1)}, bf16[16,56,2048]{2,1,0:T(8,128)(2,1)}, u32[]{:S(2)}) copy-start(bf16[16,56,2048]{2,1,0:T(8,128)(2,1)} %all_to_all.19) | copy-start | bytes 11010052
  152.4 4.1 %copy-start.12 = (bf16[512,2048]{1,0:T(8,128)(2,1)S(1)}, bf16[512,2048]{1,0:T(8,128)(2,1)}, u32[]{:S(2)}) copy-start(bf16[512,2048]{1,0:T(8,128)(2,1)} %all-gather.3.cloned.1.call-done) | copy-start | bytes 6291460
Sparse Core Ops, SparseCore 0:
  15.9 130.5 all-gather.2

commit v4 on v3

v4 whole, which is shorter than its diff:
```python
import math

import jax
import jax.numpy as jnp
from jax import lax
from jax.experimental import pallas as pl
from jax.experimental.pallas import tpu as pltpu
from jax.sharding import Mesh, PartitionSpec as P

KVH = 8
HD = 128
TXT = 64
TILE_LEN = 1601
TILE_PAD = 1664
NAMES = ("core", "x", "zb", "z1", "z0", "zh", "y")
SIZES = (2, 4, 2, 2, 2, 4, 4)
SCALING = 1.0 / math.sqrt(HD)
META = 2 * TXT
PACK = META + 16
ROWS = 52
PADDED = 56
GROUP = 4 * TXT
SLICE = 32
NT = (((1,), (1,)), ((), ()))
NN = (((1,), (0,)), ((), ()))
VMEM_LIMIT = 16 * 1024 * 1024


def prepare_kernel(
    gate_ref,
    length_ref,
    query_ref,
    out_ref,
    cot_ref,
    norm_ref,
    key_weight_ref,
    value_weight_ref,
    pack_ref,
    weight_ref,
    query,
    out,
    cot,
    key_weight,
    value_weight,
    sems,
):
    x, zb, z1, z0 = (lax.axis_index(name) for name in ("x", "zb", "z1", "z0"))
    zq = z1 * 2 + z0
    sample = x * 2 + zb
    feature = pl.multiple_of(x * 128 + (zb * 2 + z1) * SLICE, SLICE)
    copies = [
        pltpu.make_async_copy(source, target, sems.at[i])
        for i, (source, target) in enumerate(
            [
                (key_weight_ref.at[0, pl.ds(feature, SLICE)], key_weight),
                (value_weight_ref.at[0, pl.ds(feature, SLICE)], value_weight),
                (cot_ref.at[0, sample, zq], cot),
                (out_ref.at[0, sample, zq], out),
                (query_ref.at[0, sample, zq], query),
            ]
        )
    ]
    for copy in copies:
        copy.start()
    copies[0].wait()
    copies[1].wait()
    for g in range(KVH):
        place = 2 * (g % 2 * 4 + g // 2) * HD
        weight_ref[:, place : place + HD] = key_weight[:, g * HD : (g + 1) * HD]
        weight_ref[:, place + HD : place + 2 * HD] = value_weight[:, g * HD : (g + 1) * HD]

    head = lax.broadcasted_iota(jnp.int32, (4, HD), 0) == zq
    place = lax.broadcasted_iota(jnp.int32, (TXT, HD), 0)
    lane = lax.broadcasted_iota(jnp.int32, (TXT, HD), 1)
    twice = jnp.where(lane % TXT == place, 1.0, 0.0).astype(jnp.bfloat16)
    norms = lax.dot_general(norm_ref[0, sample], twice, NN, preferred_element_type=jnp.float32)
    norm = jnp.sum(jnp.where(head, norms, 0.0), axis=0, keepdims=True)

    copies[2].wait()
    row_mask = jnp.where(place < length_ref[sample], 1.0, 0.0)
    gate = jnp.tanh(jnp.full((TXT, HD), gate_ref[0], jnp.float32))
    scaled = (gate * cot[...].astype(jnp.float32) * row_mask).astype(jnp.bfloat16)
    pack_ref[TXT : 2 * TXT] = scaled
    copies[3].wait()
    product = scaled.astype(jnp.float32) * out[...].astype(jnp.float32)
    product = jnp.concatenate([product, product], axis=0)
    delta = jnp.sum(product.T, axis=0, keepdims=True)
    row = lax.broadcasted_iota(jnp.int32, (16, HD), 0)
    pack_ref[META : META + 16] = jnp.where(
        row == 0, norm, jnp.where(row == 1, delta, 0.0)
    ).astype(jnp.bfloat16)
    copies[4].wait()
    pack_ref[0:TXT] = query[...]


def prepare(layer_gate, text_lens, query, out, cot, norm, key_weight, value_weight):
    whole = pl.BlockSpec(memory_space=pltpu.HBM)
    vmem = pl.BlockSpec(memory_space=pltpu.VMEM)
    smem = pl.BlockSpec(memory_space=pltpu.SMEM)
    head = pltpu.VMEM((TXT, HD), jnp.bfloat16)
    rows = pltpu.VMEM((SLICE, KVH * HD), jnp.bfloat16)
    return pl.pallas_call(
        prepare_kernel,
        in_specs=[smem, smem, whole, whole, whole, vmem, whole, whole],
        out_specs=[vmem, vmem],
        out_shape=[
            jax.ShapeDtypeStruct((PACK, HD), jnp.bfloat16),
            jax.ShapeDtypeStruct((SLICE, 2 * KVH * HD), jnp.bfloat16),
        ],
        scratch_shapes=[head, head, head, rows, rows, pltpu.SemaphoreType.DMA((5,))],
        compiler_params=pltpu.CompilerParams(vmem_limit_bytes=VMEM_LIMIT),
        cost_estimate=pl.CostEstimate(flops=1 << 16, bytes_accessed=1 << 18, transcendentals=8192),
    )(layer_gate, text_lens, query, out, cot, norm, key_weight, value_weight)


def split_heads_kernel(key_ref, value_ref, out_ref):
    below = jnp.zeros((PADDED - ROWS, HD), jnp.float32)
    for part, ref in enumerate((key_ref, value_ref)):
        for g in range(KVH):
            head = ref[0, :, g * HD : (g + 1) * HD].astype(jnp.float32)
            head = jnp.concatenate([head, below], axis=0).astype(jnp.bfloat16)
            place = (g // 2 * 2 + part) * HD
            out_ref[g % 2 * 2, :, place : place + HD] = head
            out_ref[g % 2 * 2 + 1, :, place : place + HD] = head


def split_heads(keys, values):
    return pl.pallas_call(
        split_heads_kernel,
        out_shape=jax.ShapeDtypeStruct((4, PADDED, KVH * HD), jnp.bfloat16),
        compiler_params=pltpu.CompilerParams(vmem_limit_bytes=VMEM_LIMIT),
        cost_estimate=pl.CostEstimate(flops=0, bytes_accessed=700000, transcendentals=0),
    )(keys, values)


def attention_kernel(block_ref, tiles_ref, pack_ref, heads_ref, out_ref):
    del block_ref
    x, zb, z1, z0, zh = (lax.axis_index(name) for name in ("x", "zb", "z1", "z0", "zh"))
    tiles = tiles_ref[x * 2 + zb]
    query = pack_ref[:, 0, 0:TXT, :].reshape(GROUP, HD)
    grad = pack_ref[:, 0, TXT : 2 * TXT, :].reshape(GROUP, HD)
    meta = pack_ref[:, 0, META : META + 16, :].astype(jnp.float32)
    left = lax.broadcasted_iota(jnp.int32, (1, HD), 1) < TXT

    def line(which):
        picked = [meta[i, which : which + 1] for i in range(4)]
        return jnp.concatenate(
            [jnp.where(left, picked[i], picked[i + 1]) for i in range(0, 4, 2)], axis=1
        )

    norm, delta = line(0), line(1)
    row = lax.broadcasted_iota(jnp.int32, (PADDED, GROUP), 0)
    for y in range(4):
        position = ((z1 * 2 + z0) * 16 + zh * 4 + y) * ROWS + row
        second = position >= TILE_PAD
        inside = jnp.where(second, position - TILE_PAD, position) < TILE_LEN
        present = jnp.where(second, 1, 0) < tiles
        mask = jnp.where(inside & present & (row < ROWS), 1.0, 0.0)
        keys = heads_ref[y, :, 0:HD]
        values = heads_ref[y, :, HD : 2 * HD]
        scores = lax.dot_general(keys, query, NT, preferred_element_type=jnp.float32) * SCALING
        attention = jnp.exp(scores - norm) * mask
        value_grad = lax.dot_general(
            attention.astype(jnp.bfloat16), grad, NN, preferred_element_type=jnp.float32
        )
        probs = lax.dot_general(values, grad, NT, preferred_element_type=jnp.float32)
        grad_scores = (attention * (probs - delta)).astype(jnp.bfloat16)
        key_grad = lax.dot_general(grad_scores, query, NN, preferred_element_type=jnp.float32)
        out_ref[y, :, 0:HD] = (key_grad * SCALING).astype(jnp.bfloat16)
        out_ref[y, :, HD : 2 * HD] = value_grad.astype(jnp.bfloat16)


def attention_grads(block, tiles, packed, heads):
    piece = pl.BlockSpec((4, PADDED, 2 * HD), lambda s, b: (0, 0, (b[0] + 4 - s) % 4))
    return pl.pallas_call(
        attention_kernel,
        grid_spec=pltpu.PrefetchScalarGridSpec(
            num_scalar_prefetch=1,
            grid=(4,),
            in_specs=[
                pl.BlockSpec(memory_space=pltpu.SMEM),
                pl.BlockSpec((4, 1, PACK, HD), lambda s, b: (0, s, 0, 0)),
                piece,
            ],
            out_specs=piece,
        ),
        out_shape=jax.ShapeDtypeStruct((4, PADDED, KVH * HD), jnp.bfloat16),
        compiler_params=pltpu.CompilerParams(vmem_limit_bytes=VMEM_LIMIT),
        cost_estimate=pl.CostEstimate(
            flops=8 * 4 * PADDED * 4 * GROUP * HD,
            bytes_accessed=2 << 20,
            transcendentals=4 * PADDED * 4 * GROUP,
        ),
    )(block, tiles, packed, heads)


def project_kernel(grads_ref, weight_ref, out_ref):
    wide = KVH * HD
    for t in range(2):
        for h in range(2):
            rows = slice(h * 2 * PADDED, (h + 1) * 2 * PADDED)
            total = sum(
                lax.dot_general(
                    grads_ref[0, 2 * p + h],
                    weight_ref[t * 256 : (t + 1) * 256, p * wide : (p + 1) * wide],
                    NT,
                    preferred_element_type=jnp.float32,
                )
                for p in range(2)
            )
            out_ref[t, 0, rows] = total.astype(jnp.bfloat16)


def project(grads, weight):
    features, depth = weight.shape
    rows = 4 * PADDED
    return pl.pallas_call(
        project_kernel,
        grid=(4,),
        in_specs=[
            pl.BlockSpec((1, 4, rows // 2, depth // 2), lambda x: (x, 0, 0, 0)),
            pl.BlockSpec((features, depth), lambda x: (0, 0)),
        ],
        out_specs=pl.BlockSpec((2, 1, rows, features // 2), lambda x: (0, x, 0, 0)),
        out_shape=jax.ShapeDtypeStruct((2, 4, rows, features // 2), jnp.bfloat16),
        compiler_params=pltpu.CompilerParams(vmem_limit_bytes=VMEM_LIMIT),
        cost_estimate=pl.CostEstimate(
            flops=8 * rows * features * depth, bytes_accessed=7 << 20, transcendentals=0
        ),
    )(grads, weight)


def to_all(array, axes, count):
    copies = jnp.broadcast_to(array[None], (count, *array.shape))
    return lax.all_to_all(copies, axes, split_axis=0, concat_axis=0, tiled=True)


def body(
    text_query,
    attn_out,
    grad_out,
    log_norm,
    image_keys,
    image_values,
    k_weight,
    v_weight,
    layer_gate,
    tile_counts,
    text_lens,
):
    packed, weight = prepare(
        layer_gate, text_lens, text_query, attn_out, grad_out, log_norm, k_weight, v_weight
    )
    weight = lax.all_gather(weight, ("zh", "zb", "z1"), axis=0, tiled=True)
    zh = lax.axis_index("zh").astype(jnp.int32).reshape(1)
    own = lax.axis_index("y") % 2

    def attend(packed):
        heads = split_heads(image_keys, image_values)
        heads = lax.all_to_all(heads, "y", split_axis=0, concat_axis=0, tiled=True)
        pieces = [packed] + [
            lax.ppermute(packed, "zh", [(i, (i + shift) % 4) for i in range(4)])
            for shift in (1, 2, 3)
        ]
        packed = to_all(jnp.stack(pieces), ("z1", "z0"), 4)
        part = attention_grads(zh, tile_counts, packed, heads)
        part = part.reshape(2, 2 * PADDED, KVH * HD)
        kept = lax.dynamic_index_in_dim(part, own, 0, keepdims=False)
        given = lax.dynamic_index_in_dim(part, 1 - own, 0, keepdims=False)
        taken = lax.ppermute(given, "y", [(0, 1), (1, 0), (2, 3), (3, 2)])
        return (kept.astype(jnp.float32) + taken.astype(jnp.float32)).astype(jnp.bfloat16)

    grads = lax.cond(
        jnp.max(text_lens) > 0,
        attend,
        lambda _: jnp.zeros((2 * PADDED, KVH * HD), jnp.bfloat16),
        packed,
    )

    grads = to_all(grads, ("x", "y"), 16).reshape(4, 4, 2 * PADDED, KVH * HD)
    part = project(grads, weight).reshape(32, PADDED, 256)
    part = lax.all_to_all(part, ("core", "x", "y"), split_axis=0, concat_axis=0, tiled=True)
    part = part.reshape(2, 4, 4, PADDED, 2, HD).astype(jnp.float32)
    total = (part[0] + part[1])[:, :, :ROWS]
    return total.transpose(2, 3, 1, 0, 4).reshape(ROWS, 2 * 4 * 4 * HD)


def solution(mesh):
    fine = Mesh(mesh.devices.reshape(SIZES), NAMES)
    tensor = ("zh", "y")
    rows = ("x", "zb", "z1", "z0", "zh", "y")
    in_specs = (
        P("core", None, tensor, None, None),
        P("core", None, tensor, None, None),
        P("core", None, tensor, None, None),
        P("core", None, tensor, None),
        P("core", rows, None),
        P("core", rows, None),
        P("core", tensor, None),
        P("core", tensor, None),
        P("core"),
        P(),
        P(),
    )
    return jax.shard_map(
        body, mesh=fine, in_specs=in_specs, out_specs=P(rows, "core"), check_vma=False
    )
```

time: 202 us -> 210 us (1.040)
  blocking collectives: 135 us -> 71.3 us
  starting transfers between devices: 4.58 us -> 56.4 us
  waiting for transfers between devices: 22.6 us -> 36.3 us
  Pallas kernels: 6.51 us -> 14.8 us
  matrix products: 4.78 us -> 0 us
  local copies, waits for them, and re-layouts: 12.2 us -> 14.3 us
    ppermute x0 -> x4, starting transfers between devices: none -> 46.7 us  [the longest x3 42.7 us: attend(): lax.ppermute(packed, 'zh', [(i, (i + shift) % 4) for i in range(4)])]
    all_gather x1 -> x0, blocking collectives: 42.3 us -> none  [attend(): packed = lax.all_gather(packed, 'zh', axis=0, tiled=False)]
    ppermute x0 -> x4, waiting for transfers between devices: none -> 12.4 us  [the longest x3 8.63 us: attend(): lax.ppermute(packed, 'zh', [(i, (i + shift) % 4) for i in range(4)])]
    all_to_all x1, blocking collectives: 34.1 us -> 23.5 us  [body(): lax.all_to_all(part, ('core', 'x', 'y'), split_axis=0, concat_axis=0, til...]
    all_to_all x2 -> x1, blocking collectives: 58.4 us -> 47.8 us  [to_all(): return lax.all_to_all(copies, axes, split_axis=0, concat_axis=0, tiled=True)]
    pallas_call x1 -> x3, Pallas kernels: 4.87 us -> 13 us  [the longest x1 6.4 us: attention_grads(): pl.pallas_call(attention_kernel, grid_spec=pltpu.PrefetchScalarGridSpec(n...]
    all_to_all x0 -> x1, starting transfers between devices: none -> 5.01 us  [attend(): heads = lax.all_to_all(heads, 'y', split_axis=0, concat_axis=0, tiled=True)]
    dot_general x2 -> x0, matrix products: 4.78 us -> none  [body(): lax.dot_general(both, halves[t], NT, preferred_element_type=jnp.float32)]
  transfers between devices with their start and end apart: 2 -> 7, of which waited for: 1 -> 3; matrix products, arithmetic and copies ran while one was open for 2% -> 1% of each run, Pallas kernels for 2% -> 3%
where the time goes in v4:
time: 210 us; the launch traced here: 209 us
  blocking collectives  71.3 us (34%)
  starting transfers between devices  56.4 us (27%)
  waiting for transfers between devices  36.3 us (17%)
  Pallas kernels  14.8 us (7%)
  between operations  14.8 us (7%)
  local copies, waits for them, and re-layouts  14.3 us (7%)
    all_to_all x1, blocking collectives, to_all(): return lax.all_to_all(copies, axes, split_axis=0, concat_axis=0, tiled=True)  47.8 us
    ppermute x3, starting transfers between devices, attend(): lax.ppermute(packed, 'zh', [(i, (i + shift) % 4) for i in range(4)])  42.7 us
    all_to_all x1, waiting for transfers between devices, to_all(): return lax.all_to_all(copies, axes, split_axis=0, concat_axis=0, tiled=True)  23.9 us
    all_to_all x1, blocking collectives, body(): lax.all_to_all(part, ('core', 'x', 'y'), split_axis=0, concat_axis=0, til...  23.5 us
    unnamed x27, local copies, waits for them, and re-layouts  11.1 us
    ppermute x3, waiting for transfers between devices, attend(): lax.ppermute(packed, 'zh', [(i, (i + shift) % 4) for i in range(4)])  8.63 us
    pallas_call x1, Pallas kernels, attention_grads(): pl.pallas_call(attention_kernel, grid_spec=pltpu.PrefetchScalarGridSpec(n...  6.4 us
    pallas_call x1, Pallas kernels, project(): pl.pallas_call(project_kernel, grid=(4,), in_specs=[pl.BlockSpec((1, 4, r...  5.73 us
  transfers between devices with their start and end apart: 7, of which 3 were waited for; matrix products, arithmetic and copies ran while one was open for 1% of the time, Pallas kernels for 3%

profile of v4, /device:TPU:1, one launch (start us, length us, event | category | flops | bytes accessed | tf_op | source)
XLA Modules:
  0.0 209.0 jit_solution(17067459170201357908)
XLA Ops:
  7.2 1.2 copy-done.1
  8.4 1.2 copy-done.2
  9.7 1.0 copy-done.3
  10.7 1.0 copy-done.4
  11.8 1.0 copy-done.5
  12.8 0.7 copy-done.6
  13.5 0.7 copy-done.7
  14.2 1.8 shard_map.112
  16.0 0.6 reduce_max.9
  17.3 101.1 %conditional.1 = (bf16[112,1024]{1,0:T(8,128)(2,1)S(1)}) conditional(s32[]{:T(128)} %convert_element_type.19, () %tuple.11, (bf16[144,128]{1,0:T(8,128)(2,1)S(1)}, bf16[1,52,1024]{2,1,0:T(8,128)(2,1)S(1)}, bf16[1,52,1024]{2,1,0:T(8,128)(2,1)S(1)}, s32[]{:T(128)}, s32[8]{0:T(128)S(1)}, /*index=5*/pred[]{:T(512)}, s32[]{:T(128)}, s32[]{:T(128)}, (), (), ...), branch_computations={%region_1.2_spmd, %region_2.3_spmd} | conditional | flops 235560960 | bytes 9482211 | solution.py:273
  17.3 0.9 branch_1_fun.2
  18.2 5.0 %all-to-all-start.1 = ((bf16[4,56,1024]{2,1,0:T(8,128)(2,1)}), bf16[4,56,1024]{2,1,0:T(8,128)(2,1)S(1)}, u32[]{:S(2)}, u32[]{:S(2)}) async-start(bf16[4,56,1024]{2,1,0:T(8,128)(2,1)} %branch_1_fun.2), calls=%async_computation.1 | async-start | bytes 917504 | tf_op jit(solution)/shard_map/cond/branch_1_fun/all_to_all | solution.py:260
  23.2 15.4 %collective-permute-start = (bf16[144,128]{1,0:T(8,128)(2,1)S(1)}, bf16[144,128]{1,0:T(8,128)(2,1)S(1)}, u32[]{:S(2)}, u32[]{:S(2)}) collective-permute-start(bf16[144,128]{1,0:T(8,128)(2,1)S(1)} %get-tuple-element.22), channel_id=1, source_target_pairs={{0,4},{4,8},{8,12},{12,0},{1,5},{5,9},{9,13},{13,1},{2,6},{6,10},{... | collective-permute-start | bytes 110600 | tf_op jit(solution)/shard_map/cond/branch_1_fun/ppermute | solution.py:262
  38.6 19.1 %collective-permute-start.1 = (bf16[144,128]{1,0:T(8,128)(2,1)S(1)}, bf16[144,128]{1,0:T(8,128)(2,1)S(1)}, u32[]{:S(2)}, u32[]{:S(2)}) collective-permute-start(bf16[144,128]{1,0:T(8,128)(2,1)S(1)} %get-tuple-element.22), channel_id=1, source_target_pairs={{0,8},{4,12},{8,0},{12,4},{1,9},{5,13},{9,1},{13,5},{2,10},{6,14},... | collective-permute-start | bytes 110600 | tf_op jit(solution)/shard_map/cond/branch_1_fun/ppermute | solution.py:262
  57.7 8.2 %collective-permute-start.2 = (bf16[144,128]{1,0:T(8,128)(2,1)S(1)}, bf16[144,128]{1,0:T(8,128)(2,1)S(1)}, u32[]{:S(2)}, u32[]{:S(2)}) collective-permute-start(bf16[144,128]{1,0:T(8,128)(2,1)S(1)} %get-tuple-element.22), channel_id=1, source_target_pairs={{0,12},{4,0},{8,4},{12,8},{1,13},{5,1},{9,5},{13,9},{2,14},{6,2},{... | collective-permute-start | bytes 110600 | tf_op jit(solution)/shard_map/cond/branch_1_fun/ppermute | solution.py:262
  65.9 8.6 %collective-permute-done.2 = bf16[144,128]{1,0:T(8,128)(2,1)S(1)} collective-permute-done((bf16[144,128]{1,0:T(8,128)(2,1)S(1)}, bf16[144,128]{1,0:T(8,128)(2,1)S(1)}, u32[]{:S(2)}, u32[]{:S(2)}) %collective-permute-start.2) | collective-permute-done | bytes 36896 | tf_op jit(solution)/shard_map/cond/branch_1_fun/ppermute | solution.py:262
  74.6 0.9 broadcast_in_dim.0
  75.5 4.7 %all-to-all-start = ((bf16[4,4,144,128]{3,2,1,0:T(8,128)(2,1)}), bf16[4,4,144,128]{3,2,1,0:T(8,128)(2,1)S(1)}, u32[]{:S(2)}, u32[]{:S(2)}) async-start(bf16[4,4,144,128]{3,2,1,0:T(8,128)(2,1)} %broadcast_in_dim.0), calls=%async_computation | async-start | bytes 1179648 | tf_op jit(solution)/shard_map/cond/branch_1_fun/all_to_all | solution.py:235
  80.1 23.9 %all-to-all-done.pack_ref = bf16[4,4,144,128]{3,2,1,0:T(8,128)(2,1)S(1)} async-done(((bf16[4,4,144,128]{3,2,1,0:T(8,128)(2,1)}), bf16[4,4,144,128]{3,2,1,0:T(8,128)(2,1)S(1)}, u32[]{:S(2)}, u32[]{:S(2)}) %all-to-all-start) | async-done | bytes 589856 | tf_op jit(solution)/shard_map/cond/branch_1_fun/all_to_all | solution.py:235
  104.0 6.4 %branch_1_fun.3 = bf16[4,56,1024]{2,1,0:T(8,128)(2,1)S(1)} custom-call(s32[1]{0:T(128)} %bitcast.block_ref, s32[8]{0:T(128)S(1)} %get-tuple-element.39.tiles_ref, bf16[4,4,144,128]{3,2,1,0:T(8,128)(2,1)S(1)} %all-to-all-done.pack_ref, bf16[4,56,1024]{2,1,0:T(8,128)(2,1)S(1)} %all-to-all-done.1.heads_ref), custom_call_target="tpu_custom_call" | custom-call | flops 234881024 | bytes 2097152 | tf_op jit(solution)/shard_map/cond/branch_1_fun/pallas_call | solution.py:175
  110.5 4.0 %collective-permute-start.3 = (bf16[112,1024]{1,0:T(8,128)(2,1)S(1)}, bf16[112,1024]{1,0:T(8,128)(2,1)S(1)}, u32[]{:S(2)}, u32[]{:S(2)}) collective-permute-start(bf16[112,1024]{1,0:T(8,128)(2,1)S(1)} %dynamic-slice_bitcast_fusion), channel_id=1, source_target_pairs={{0,1},{1,0},{2,3},{3,2},{4,5},{5,4},{6,7},{7,6},{8,9},{9,8},{10,11... | collective-permute-start | bytes 688136 | tf_op jit(solution)/shard_map/cond/branch_1_fun/ppermute | solution.py:270
  114.5 3.8 %collective-permute-done.3 = bf16[112,1024]{1,0:T(8,128)(2,1)S(1)} collective-permute-done((bf16[112,1024]{1,0:T(8,128)(2,1)S(1)}, bf16[112,1024]{1,0:T(8,128)(2,1)S(1)}, u32[]{:S(2)}, u32[]{:S(2)}) %collective-permute-start.3) | collective-permute-done | bytes 229408 | tf_op jit(solution)/shard_map/cond/branch_1_fun/ppermute | solution.py:270
  118.4 0.5 broadcast_in_dim.8
  118.8 47.8 %all_to_all.18 = bf16[16,112,1024]{2,1,0:T(8,128)(2,1)} all-to-all(bf16[16,112,1024]{2,1,0:T(8,128)(2,1)S(1)} %broadcast_in_dim.8), channel_id=1, replica_groups=mesh['core'=2,'x'=4,'zb'=2,'z1'=2,'z0'=2,'zh'=4,'y'=4] {'x','y'}, dimensions={0} | all-to-all | bytes 7340032 | tf_op jit(solution)/shard_map/all_to_all | solution.py:235
  166.7 2.0 copy-done
  168.7 1.6 copy-done.9
  170.3 5.7 %shard_map.113 = bf16[2,4,224,256]{3,2,1,0:T(8,128)(2,1)S(1)} custom-call(bf16[4,4,112,1024]{3,2,1,0:T(8,128)(2,1)S(1)} %bitcast.16, bf16[512,2048]{1,0:T(8,128)(2,1)S(1)} %copy-done.9), custom_call_target="tpu_custom_call" | custom-call | flops 1879048192 | bytes 7340032 | tf_op jit(solution)/shard_map/pallas_call | solution.py:217
  176.0 23.5 %all_to_all.19 = bf16[32,56,256]{2,1,0:T(8,128)(2,1)S(1)} all-to-all(bf16[32,56,256]{2,1,0:T(8,128)(2,1)S(1)} %bitcast.19), channel_id=1, replica_groups=mesh['core'=2,'x'=4,'zb'=2,'z1'=2,'z0'=2,'zh'=4,'y'=4] {'core','x','y'}, dimensions={0} | all-to-all | bytes 1835008 | tf_op jit(solution)/shard_map/all_to_all | solution.py:282
  199.5 0.1 convert_element_type.20
  199.8 0.5 add.24
  200.3 0.6 copy.18
  200.9 1.3 reshape.29
  (28 shorter events, 0.3 us)
Async XLA Ops:
  6.5 9.4 %copy-start.8 = (s32[8]{0:T(128)S(1)}, s32[8]{0:T(128)}, u32[]{:S(2)}) copy-start(s32[8]{0:T(128)} %length_ref.1) | copy-start | bytes 100
  6.5 10.7 %copy-start.12 = (s32[8]{0:T(128)S(1)}, s32[8]{0:T(128)}, u32[]{:S(2)}) copy-start(s32[8]{0:T(128)} %param.22) | copy-start | bytes 100
  6.5 160.1 %all-gather.2.cloned.1.call-start = ((), (), s32[]{:S(2)}) async-start(), calls=%async_computation.4 | async-start | bytes 2228224 | tf_op jit(solution)/shard_map/all_gather | solution.py:254
  7.2 1.2 copy-start.1
  8.4 1.2 copy-start.2
  9.7 1.0 copy-start.3
  10.7 1.0 copy-start.4
  11.8 1.0 copy-start.5
  12.8 0.7 copy-start.6
  13.5 0.7 copy-start.7
  14.1 3.1 %copy-start.10 = (bf16[1,52,1024]{2,1,0:T(8,128)(2,1)S(1)}, bf16[1,52,1024]{2,1,0:T(8,128)(2,1)}, u32[]{:S(2)}) copy-start(bf16[1,52,1024]{2,1,0:T(8,128)(2,1)} %param.17) | copy-start | bytes 319492
  14.2 3.1 %copy-start.11 = (bf16[1,52,1024]{2,1,0:T(8,128)(2,1)S(1)}, bf16[1,52,1024]{2,1,0:T(8,128)(2,1)}, u32[]{:S(2)}) copy-start(bf16[1,52,1024]{2,1,0:T(8,128)(2,1)} %param.18) | copy-start | bytes 319492
  18.2 56.4 %all-to-all-start.1 = ((bf16[4,56,1024]{2,1,0:T(8,128)(2,1)}), bf16[4,56,1024]{2,1,0:T(8,128)(2,1)S(1)}, u32[]{:S(2)}, u32[]{:S(2)}) async-start(bf16[4,56,1024]{2,1,0:T(8,128)(2,1)} %branch_1_fun.2), calls=%async_computation.1 | async-start | bytes 917504 | tf_op jit(solution)/shard_map/cond/branch_1_fun/all_to_all | solution.py:260
  23.2 42.7 %collective-permute-start = (bf16[144,128]{1,0:T(8,128)(2,1)S(1)}, bf16[144,128]{1,0:T(8,128)(2,1)S(1)}, u32[]{:S(2)}, u32[]{:S(2)}) collective-permute-start(bf16[144,128]{1,0:T(8,128)(2,1)S(1)} %get-tuple-element.22), channel_id=1, source_target_pairs={{0,4},{4,8},{8,12},{12,0},{1,5},{5,9},{9,13},{13,1},{2,6},{6,10},{... | collective-permute-start | bytes 110600 | tf_op jit(solution)/shard_map/cond/branch_1_fun/ppermute | solution.py:262
  38.6 27.3 %collective-permute-start.1 = (bf16[144,128]{1,0:T(8,128)(2,1)S(1)}, bf16[144,128]{1,0:T(8,128)(2,1)S(1)}, u32[]{:S(2)}, u32[]{:S(2)}) collective-permute-start(bf16[144,128]{1,0:T(8,128)(2,1)S(1)} %get-tuple-element.22), channel_id=1, source_target_pairs={{0,8},{4,12},{8,0},{12,4},{1,9},{5,13},{9,1},{13,5},{2,10},{6,14},... | collective-permute-start | bytes 110600 | tf_op jit(solution)/shard_map/cond/branch_1_fun/ppermute | solution.py:262
  57.7 16.8 %collective-permute-start.2 = (bf16[144,128]{1,0:T(8,128)(2,1)S(1)}, bf16[144,128]{1,0:T(8,128)(2,1)S(1)}, u32[]{:S(2)}, u32[]{:S(2)}) collective-permute-start(bf16[144,128]{1,0:T(8,128)(2,1)S(1)} %get-tuple-element.22), channel_id=1, source_target_pairs={{0,12},{4,0},{8,4},{12,8},{1,13},{5,1},{9,5},{13,9},{2,14},{6,2},{... | collective-permute-start | bytes 110600 | tf_op jit(solution)/shard_map/cond/branch_1_fun/ppermute | solution.py:262
  75.5 28.6 %all-to-all-start = ((bf16[4,4,144,128]{3,2,1,0:T(8,128)(2,1)}), bf16[4,4,144,128]{3,2,1,0:T(8,128)(2,1)S(1)}, u32[]{:S(2)}, u32[]{:S(2)}) async-start(bf16[4,4,144,128]{3,2,1,0:T(8,128)(2,1)} %broadcast_in_dim.0), calls=%async_computation | async-start | bytes 1179648 | tf_op jit(solution)/shard_map/cond/branch_1_fun/all_to_all | solution.py:235
  110.5 7.8 %collective-permute-start.3 = (bf16[112,1024]{1,0:T(8,128)(2,1)S(1)}, bf16[112,1024]{1,0:T(8,128)(2,1)S(1)}, u32[]{:S(2)}, u32[]{:S(2)}) collective-permute-start(bf16[112,1024]{1,0:T(8,128)(2,1)S(1)} %dynamic-slice_bitcast_fusion), channel_id=1, source_target_pairs={{0,1},{1,0},{2,3},{3,2},{4,5},{5,4},{6,7},{7,6},{8,9},{9,8},{10,11... | collective-permute-start | bytes 688136 | tf_op jit(solution)/shard_map/cond/branch_1_fun/ppermute | solution.py:270
  166.7 2.0 copy-start
  168.7 1.6 copy-start.9
Sparse Core Ops, SparseCore 0:
  16.1 120.7 all-gather.1

commit v5 on v4

--- a/solution.py
+++ b/solution.py
@@ -24,6 +24,7 @@
 NT = (((1,), (1,)), ((), ()))
 NN = (((1,), (0,)), ((), ()))
 VMEM_LIMIT = 16 * 1024 * 1024
+WHOLE_VMEM = 60 * 1024 * 1024
 
 
 def prepare_kernel(
@@ -108,7 +109,7 @@
             jax.ShapeDtypeStruct((SLICE, 2 * KVH * HD), jnp.bfloat16),
         ],
         scratch_shapes=[head, head, head, rows, rows, pltpu.SemaphoreType.DMA((5,))],
-        compiler_params=pltpu.CompilerParams(vmem_limit_bytes=VMEM_LIMIT),
+        compiler_params=pltpu.CompilerParams(vmem_limit_bytes=WHOLE_VMEM),
         cost_estimate=pl.CostEstimate(flops=1 << 16, bytes_accessed=1 << 18, transcendentals=8192),
     )(layer_gate, text_lens, query, out, cot, norm, key_weight, value_weight)
 
@@ -133,8 +134,7 @@
     )(keys, values)
 
 
-def attention_kernel(block_ref, tiles_ref, pack_ref, heads_ref, out_ref):
-    del block_ref
+def attention_kernel(tiles_ref, pack_ref, heads_ref, out_ref):
     x, zb, z1, z0, zh = (lax.axis_index(name) for name in ("x", "zb", "z1", "z0", "zh"))
     tiles = tiles_ref[x * 2 + zb]
     query = pack_ref[:, 0, 0:TXT, :].reshape(GROUP, HD)
@@ -170,20 +170,17 @@
         out_ref[y, :, HD : 2 * HD] = value_grad.astype(jnp.bfloat16)
 
 
-def attention_grads(block, tiles, packed, heads):
-    piece = pl.BlockSpec((4, PADDED, 2 * HD), lambda s, b: (0, 0, (b[0] + 4 - s) % 4))
+def attention_grads(tiles, packed, heads):
+    piece = pl.BlockSpec((4, PADDED, 2 * HD), lambda s: (0, 0, s))
     return pl.pallas_call(
         attention_kernel,
-        grid_spec=pltpu.PrefetchScalarGridSpec(
-            num_scalar_prefetch=1,
-            grid=(4,),
-            in_specs=[
-                pl.BlockSpec(memory_space=pltpu.SMEM),
-                pl.BlockSpec((4, 1, PACK, HD), lambda s, b: (0, s, 0, 0)),
-                piece,
-            ],
-            out_specs=piece,
-        ),
+        grid=(4,),
+        in_specs=[
+            pl.BlockSpec(memory_space=pltpu.SMEM),
+            pl.BlockSpec((4, 1, PACK, HD), lambda s: (0, s, 0, 0)),
+            piece,
+        ],
+        out_specs=piece,
         out_shape=jax.ShapeDtypeStruct((4, PADDED, KVH * HD), jnp.bfloat16),
         compiler_params=pltpu.CompilerParams(vmem_limit_bytes=VMEM_LIMIT),
         cost_estimate=pl.CostEstimate(
@@ -191,7 +188,7 @@
             bytes_accessed=2 << 20,
             transcendentals=4 * PADDED * 4 * GROUP,
         ),
-    )(block, tiles, packed, heads)
+    )(tiles, packed, heads)
 
 
 def project_kernel(grads_ref, weight_ref, out_ref):
@@ -223,7 +220,7 @@
         ],
         out_specs=pl.BlockSpec((2, 1, rows, features // 2), lambda x: (0, x, 0, 0)),
         out_shape=jax.ShapeDtypeStruct((2, 4, rows, features // 2), jnp.bfloat16),
-        compiler_params=pltpu.CompilerParams(vmem_limit_bytes=VMEM_LIMIT),
+        compiler_params=pltpu.CompilerParams(vmem_limit_bytes=WHOLE_VMEM),
         cost_estimate=pl.CostEstimate(
             flops=8 * rows * features * depth, bytes_accessed=7 << 20, transcendentals=0
         ),
@@ -252,18 +249,14 @@
         layer_gate, text_lens, text_query, attn_out, grad_out, log_norm, k_weight, v_weight
     )
     weight = lax.all_gather(weight, ("zh", "zb", "z1"), axis=0, tiled=True)
-    zh = lax.axis_index("zh").astype(jnp.int32).reshape(1)
     own = lax.axis_index("y") % 2
 
     def attend(packed):
         heads = split_heads(image_keys, image_values)
         heads = lax.all_to_all(heads, "y", split_axis=0, concat_axis=0, tiled=True)
-        pieces = [packed] + [
-            lax.ppermute(packed, "zh", [(i, (i + shift) % 4) for i in range(4)])
-            for shift in (1, 2, 3)
-        ]
-        packed = to_all(jnp.stack(pieces), ("z1", "z0"), 4)
-        part = attention_grads(zh, tile_counts, packed, heads)
+        packed = lax.all_gather(packed, "zh", axis=0, tiled=True)
+        packed = to_all(packed, ("z1", "z0"), 4).reshape(4, 4, PACK, HD)
+        part = attention_grads(tile_counts, packed, heads)
         part = part.reshape(2, 2 * PADDED, KVH * HD)
         kept = lax.dynamic_index_in_dim(part, own, 0, keepdims=False)
         given = lax.dynamic_index_in_dim(part, 1 - own, 0, keepdims=False)

time: 210 us -> 192 us (0.914)
  starting transfers between devices: 56.4 us -> 11.1 us
  blocking collectives: 71.3 us -> 112 us
  local copies, waits for them, and re-layouts: 14.3 us -> 3.74 us
  waiting for transfers between devices: 36.3 us -> 30.5 us
  Pallas kernels: 14.8 us -> 18 us
    ppermute x3 -> x0, starting transfers between devices: 42.7 us -> none  [attend(): lax.ppermute(packed, 'zh', [(i, (i + shift) % 4) for i in range(4)])]
    all_gather x0 -> x1, blocking collectives: none -> 42.3 us  [attend(): packed = lax.all_gather(packed, 'zh', axis=0, tiled=True)]
    unnamed x27 -> x9, local copies, waits for them, and re-layouts: 11.1 us -> 0.57 us
    ppermute x3 -> x0, waiting for transfers between devices: 8.63 us -> none  [attend(): lax.ppermute(packed, 'zh', [(i, (i + shift) % 4) for i in range(4)])]
    pallas_call x1, Pallas kernels: 5.73 us -> 8.31 us  [project(): pl.pallas_call(project_kernel, grid=(4,), in_specs=[pl.BlockSpec((1, 4, r...]
    ppermute x1, starting transfers between devices: 4.02 us -> 1.92 us  [attend(): taken = lax.ppermute(given, 'y', [(0, 1), (1, 0), (2, 3), (3, 2)])]
  transfers between devices with their start and end apart: 7 -> 4, of which waited for: 3 -> 2; matrix products, arithmetic and copies ran while one was open for 1% -> 1% of each run, Pallas kernels for 3% -> 4%
where the time goes in v5:
time: 192 us
  blocking collectives  112 us (58%)
  waiting for transfers between devices  30.5 us (16%)
  Pallas kernels  18 us (9%)
  between operations  14.9 us (8%)
  starting transfers between devices  11.1 us (6%)
  local copies, waits for them, and re-layouts  3.74 us (2%)
    all_to_all x1, blocking collectives, to_all(): return lax.all_to_all(copies, axes, split_axis=0, concat_axis=0, tiled=True)  46.3 us
    all_gather x1, blocking collectives, attend(): packed = lax.all_gather(packed, 'zh', axis=0, tiled=True)  42.3 us
    all_to_all x1, waiting for transfers between devices, to_all(): return lax.all_to_all(copies, axes, split_axis=0, concat_axis=0, tiled=True)  25.3 us
    all_to_all x1, blocking collectives, body(): lax.all_to_all(part, ('core', 'x', 'y'), split_axis=0, concat_axis=0, til...  23.7 us
    pallas_call x1, Pallas kernels, project(): pl.pallas_call(project_kernel, grid=(4,), in_specs=[pl.BlockSpec((1, 4, r...  8.31 us
    pallas_call x1, Pallas kernels, attention_grads(): pl.pallas_call(attention_kernel, grid=(4,), in_specs=[pl.BlockSpec(memory...  6.3 us
    ppermute x1, waiting for transfers between devices, attend(): taken = lax.ppermute(given, 'y', [(0, 1), (1, 0), (2, 3), (3, 2)])  5.23 us
    all_to_all x1, starting transfers between devices, attend(): heads = lax.all_to_all(heads, 'y', split_axis=0, concat_axis=0, tiled=True)  5.01 us
  transfers between devices with their start and end apart: 4, of which 2 were waited for; matrix products, arithmetic and copies ran while one was open for 1% of the time, Pallas kernels for 4%

profile of v5, /device:TPU:1, one launch (start us, length us, event | category | flops | bytes accessed | tf_op | source)
XLA Modules:
  0.0 191.6 jit_solution(12085135134207349494)
XLA Ops:
  6.5 0.0 copy-start.2
  6.5 0.0 copy-start
  6.5 0.0 all-gather.2.cloned.1.call-start
  7.3 2.6 %shard_map.112 = (bf16[144,128]{1,0:T(8,128)(2,1)S(1)}, bf16[32,2048]{1,0:T(8,128)(2,1)}) custom-call(f32[1]{0:T(128)S(6)} %copy.21.gate_ref, s32[8]{0:T(128)} %length_ref.1, bf16[1,8,4,64,128]{4,3,2,1,0:T(8,128)(2,1)} %query_ref.1, bf16[1,8,4,64,128]{4,3,2,1,0:T(8,128)(2,1)} %out_ref.1, bf16[1,8,4,64,128]{4,3,2,1,0:T(8,128)(2,1)} %cot_ref.1, ...), custom_call_target="tpu_custom_call" | custom-call | flops 65536 | bytes 262144 | tf_op jit(solution)/shard_map/pallas_call | solution.py:103
  9.9 0.0 all-gather.2.cloned.1.call-update
  9.9 0.0 copy-done.2
  9.9 0.6 reduce_max.9
  11.2 0.0 copy-done
  11.2 0.0 copy-done.1
  11.2 0.0 copy-done.3
  11.2 92.0 %conditional.1 = (bf16[112,1024]{1,0:T(8,128)(2,1)S(1)}) conditional(s32[]{:T(128)} %convert_element_type.19, () %tuple.11, (bf16[144,128]{1,0:T(8,128)(2,1)S(1)}, bf16[1,52,1024]{2,1,0:T(8,128)(2,1)S(1)}, bf16[1,52,1024]{2,1,0:T(8,128)(2,1)S(1)}, s32[8]{0:T(128)S(1)}, pred[]{:T(512)}, /*index=5*/s32[]{:T(128)}, s32[]{:T(128)}, (), (), s32[]{:T(128)}, ...), branch_computations={%region_1.2_spmd, %region_2.3_spmd} | conditional | flops 235339776 | bytes 8929131 | solution.py:266
  11.2 0.9 branch_1_fun.2
  12.1 5.0 %all-to-all-start.1 = ((bf16[4,56,1024]{2,1,0:T(8,128)(2,1)}), bf16[4,56,1024]{2,1,0:T(8,128)(2,1)S(1)}, u32[]{:S(2)}, u32[]{:S(2)}) async-start(bf16[4,56,1024]{2,1,0:T(8,128)(2,1)} %branch_1_fun.2), calls=%async_computation.1 | async-start | bytes 917504 | tf_op jit(solution)/shard_map/cond/branch_1_fun/all_to_all | solution.py:256
  17.1 42.3 %all_gather.4 = bf16[576,128]{1,0:T(8,128)(2,1)S(1)} all-gather(bf16[144,128]{1,0:T(8,128)(2,1)S(1)} %get-tuple-element.19), channel_id=1, replica_groups=mesh['core'=2,'x'=4,'zb'=2,'z1'=2,'z0'=2,'zh'=4,'y'=4] {'zh'}, dimensions={0}, use_global_device_ids=true | all-gather | bytes 184320 | tf_op jit(solution)/shard_map/cond/branch_1_fun/all_gather | solution.py:257
  59.4 0.0 all-to-all-done.1.heads_ref
  59.4 0.9 broadcast_in_dim.0
  60.3 4.1 %all-to-all-start = ((bf16[4,576,128]{2,1,0:T(8,128)(2,1)}), bf16[4,576,128]{2,1,0:T(8,128)(2,1)S(1)}, u32[]{:S(2)}, u32[]{:S(2)}) async-start(bf16[4,576,128]{2,1,0:T(8,128)(2,1)} %broadcast_in_dim.0), calls=%async_computation | async-start | bytes 1179648 | tf_op jit(solution)/shard_map/cond/branch_1_fun/all_to_all | solution.py:232
  64.4 25.3 %all-to-all-done = bf16[4,576,128]{2,1,0:T(8,128)(2,1)S(1)} async-done(((bf16[4,576,128]{2,1,0:T(8,128)(2,1)}), bf16[4,576,128]{2,1,0:T(8,128)(2,1)S(1)}, u32[]{:S(2)}, u32[]{:S(2)}) %all-to-all-start) | async-done | bytes 589856 | tf_op jit(solution)/shard_map/cond/branch_1_fun/all_to_all | solution.py:232
  89.7 6.3 %branch_1_fun.3 = bf16[4,56,1024]{2,1,0:T(8,128)(2,1)S(1)} custom-call(s32[8]{0:T(128)S(1)} %get-tuple-element.35.tiles_ref, bf16[4,4,144,128]{3,2,1,0:T(8,128)(2,1)S(1)} %bitcast.12, bf16[4,56,1024]{2,1,0:T(8,128)(2,1)S(1)} %all-to-all-done.1.heads_ref), custom_call_target="tpu_custom_call" | custom-call | flops 234881024 | bytes 2097152 | tf_op jit(solution)/shard_map/cond/branch_1_fun/pallas_call | solution.py:175
  96.0 1.9 %collective-permute-start = (bf16[112,1024]{1,0:T(8,128)(2,1)S(1)}, bf16[112,1024]{1,0:T(8,128)(2,1)S(1)}, u32[]{:S(2)}, u32[]{:S(2)}) collective-permute-start(bf16[112,1024]{1,0:T(8,128)(2,1)S(1)} %dynamic-slice_bitcast_fusion), channel_id=1, source_target_pairs={{0,1},{1,0},{2,3},{3,2},{4,5},{5,4},{6,7},{7,6},{8,9},{9,8},{10,11... | collective-permute-start | bytes 688136 | tf_op jit(solution)/shard_map/cond/branch_1_fun/ppermute | solution.py:263
  98.0 5.2 %collective-permute-done = bf16[112,1024]{1,0:T(8,128)(2,1)S(1)} collective-permute-done((bf16[112,1024]{1,0:T(8,128)(2,1)S(1)}, bf16[112,1024]{1,0:T(8,128)(2,1)S(1)}, u32[]{:S(2)}, u32[]{:S(2)}) %collective-permute-start) | collective-permute-done | bytes 229408 | tf_op jit(solution)/shard_map/cond/branch_1_fun/ppermute | solution.py:263
  103.2 0.1 fusion
  103.3 0.5 broadcast_in_dim.8
  103.7 46.3 %all_to_all.18 = bf16[16,112,1024]{2,1,0:T(8,128)(2,1)} all-to-all(bf16[16,112,1024]{2,1,0:T(8,128)(2,1)S(1)} %broadcast_in_dim.8), channel_id=1, replica_groups=mesh['core'=2,'x'=4,'zb'=2,'z1'=2,'z0'=2,'zh'=4,'y'=4] {'x','y'}, dimensions={0} | all-to-all | bytes 7340032 | tf_op jit(solution)/shard_map/all_to_all | solution.py:232
  150.1 8.3 %shard_map.113 = bf16[2,4,224,256]{3,2,1,0:T(8,128)(2,1)} custom-call(bf16[4,4,112,1024]{3,2,1,0:T(8,128)(2,1)} %bitcast.15, bf16[512,2048]{1,0:T(8,128)(2,1)} %all-gather.2.cloned.1.call-done.weight_ref), custom_call_target="tpu_custom_call" | custom-call | flops 1879048192 | bytes 7340032 | tf_op jit(solution)/shard_map/pallas_call | solution.py:214
  158.4 23.7 %all_to_all.19 = bf16[32,56,256]{2,1,0:T(8,128)(2,1)S(1)} all-to-all(bf16[32,56,256]{2,1,0:T(8,128)(2,1)} %bitcast.17), channel_id=1, replica_groups=mesh['core'=2,'x'=4,'zb'=2,'z1'=2,'z0'=2,'zh'=4,'y'=4] {'core','x','y'}, dimensions={0} | all-to-all | bytes 1835008 | tf_op jit(solution)/shard_map/all_to_all | solution.py:275
  182.1 0.1 convert_element_type.20
  182.2 0.1 slice_add_fusion
  182.3 0.5 add.24
  182.8 0.1 slice.16
  182.9 0.6 copy.18
  183.4 1.3 reshape.28
  (4 shorter events, 0.0 us)
Async XLA Ops:
  6.5 3.4 %copy-start.2 = (s32[8]{0:T(128)S(1)}, s32[8]{0:T(128)}, u32[]{:S(2)}) copy-start(s32[8]{0:T(128)} %length_ref.1) | copy-start | bytes 100
  6.5 4.7 %copy-start = (bf16[1,52,1024]{2,1,0:T(8,128)(2,1)S(1)}, bf16[1,52,1024]{2,1,0:T(8,128)(2,1)}, u32[]{:S(2)}) copy-start(bf16[1,52,1024]{2,1,0:T(8,128)(2,1)} %param.17) | copy-start | bytes 319492
  6.5 4.7 %copy-start.1 = (bf16[1,52,1024]{2,1,0:T(8,128)(2,1)S(1)}, bf16[1,52,1024]{2,1,0:T(8,128)(2,1)}, u32[]{:S(2)}) copy-start(bf16[1,52,1024]{2,1,0:T(8,128)(2,1)} %param.18) | copy-start | bytes 319492
  6.5 4.7 %copy-start.3 = (s32[8]{0:T(128)S(1)}, s32[8]{0:T(128)}, u32[]{:S(2)}) copy-start(s32[8]{0:T(128)} %param.22) | copy-start | bytes 100
  6.5 143.5 %all-gather.2.cloned.1.call-start = ((), (), s32[]{:S(2)}) async-start(), calls=%async_computation.4 | async-start | bytes 2228224 | tf_op jit(solution)/shard_map/all_gather | solution.py:251
  12.1 47.3 %all-to-all-start.1 = ((bf16[4,56,1024]{2,1,0:T(8,128)(2,1)}), bf16[4,56,1024]{2,1,0:T(8,128)(2,1)S(1)}, u32[]{:S(2)}, u32[]{:S(2)}) async-start(bf16[4,56,1024]{2,1,0:T(8,128)(2,1)} %branch_1_fun.2), calls=%async_computation.1 | async-start | bytes 917504 | tf_op jit(solution)/shard_map/cond/branch_1_fun/all_to_all | solution.py:256
  60.3 29.4 %all-to-all-start = ((bf16[4,576,128]{2,1,0:T(8,128)(2,1)}), bf16[4,576,128]{2,1,0:T(8,128)(2,1)S(1)}, u32[]{:S(2)}, u32[]{:S(2)}) async-start(bf16[4,576,128]{2,1,0:T(8,128)(2,1)} %broadcast_in_dim.0), calls=%async_computation | async-start | bytes 1179648 | tf_op jit(solution)/shard_map/cond/branch_1_fun/all_to_all | solution.py:232
  96.0 7.2 %collective-permute-start = (bf16[112,1024]{1,0:T(8,128)(2,1)S(1)}, bf16[112,1024]{1,0:T(8,128)(2,1)S(1)}, u32[]{:S(2)}, u32[]{:S(2)}) collective-permute-start(bf16[112,1024]{1,0:T(8,128)(2,1)S(1)} %dynamic-slice_bitcast_fusion), channel_id=1, source_target_pairs={{0,1},{1,0},{2,3},{3,2},{4,5},{5,4},{6,7},{7,6},{8,9},{9,8},{10,11... | collective-permute-start | bytes 688136 | tf_op jit(solution)/shard_map/cond/branch_1_fun/ppermute | solution.py:263
Sparse Core Ops, SparseCore 0:
  10.0 111.3 all-gather.1

commit v6 on v5

--- a/solution.py
+++ b/solution.py
@@ -38,6 +38,7 @@
     value_weight_ref,
     pack_ref,
     weight_ref,
+    longest_ref,
     query,
     out,
     cot,
@@ -63,6 +64,10 @@
     ]
     for copy in copies:
         copy.start()
+    longest = length_ref[0]
+    for i in range(1, 8):
+        longest = jnp.maximum(longest, length_ref[i])
+    longest_ref[0] = longest
     copies[0].wait()
     copies[1].wait()
     for g in range(KVH):
@@ -103,10 +108,11 @@
     return pl.pallas_call(
         prepare_kernel,
         in_specs=[smem, smem, whole, whole, whole, vmem, whole, whole],
-        out_specs=[vmem, vmem],
+        out_specs=[vmem, vmem, smem],
         out_shape=[
             jax.ShapeDtypeStruct((PACK, HD), jnp.bfloat16),
             jax.ShapeDtypeStruct((SLICE, 2 * KVH * HD), jnp.bfloat16),
+            jax.ShapeDtypeStruct((1,), jnp.int32),
         ],
         scratch_shapes=[head, head, head, rows, rows, pltpu.SemaphoreType.DMA((5,))],
         compiler_params=pltpu.CompilerParams(vmem_limit_bytes=WHOLE_VMEM),
@@ -149,25 +155,31 @@
         )
 
     norm, delta = line(0), line(1)
-    row = lax.broadcasted_iota(jnp.int32, (PADDED, GROUP), 0)
-    for y in range(4):
-        position = ((z1 * 2 + z0) * 16 + zh * 4 + y) * ROWS + row
-        second = position >= TILE_PAD
-        inside = jnp.where(second, position - TILE_PAD, position) < TILE_LEN
-        present = jnp.where(second, 1, 0) < tiles
-        mask = jnp.where(inside & present & (row < ROWS), 1.0, 0.0)
-        keys = heads_ref[y, :, 0:HD]
-        values = heads_ref[y, :, HD : 2 * HD]
-        scores = lax.dot_general(keys, query, NT, preferred_element_type=jnp.float32) * SCALING
-        attention = jnp.exp(scores - norm) * mask
-        value_grad = lax.dot_general(
-            attention.astype(jnp.bfloat16), grad, NN, preferred_element_type=jnp.float32
-        )
-        probs = lax.dot_general(values, grad, NT, preferred_element_type=jnp.float32)
-        grad_scores = (attention * (probs - delta)).astype(jnp.bfloat16)
-        key_grad = lax.dot_general(grad_scores, query, NN, preferred_element_type=jnp.float32)
-        out_ref[y, :, 0:HD] = (key_grad * SCALING).astype(jnp.bfloat16)
-        out_ref[y, :, HD : 2 * HD] = value_grad.astype(jnp.bfloat16)
+    line_rows = 4 * PADDED
+    wide_row = lax.broadcasted_iota(jnp.int32, (line_rows, GROUP), 0)
+    y = sum(jnp.where(wide_row >= i * PADDED, 1, 0) for i in (1, 2, 3))
+    row = wide_row - y * PADDED
+    position = ((z1 * 2 + z0) * 16 + zh * 4 + y) * ROWS + row
+    second = position >= TILE_PAD
+    inside = jnp.where(second, position - TILE_PAD, position) < TILE_LEN
+    present = jnp.where(second, 1, 0) < tiles
+    mask = jnp.where(inside & present & (row < ROWS), 1.0, 0.0)
+
+    def lines(block):
+        return block.astype(jnp.float32).reshape(line_rows, HD).astype(jnp.bfloat16)
+
+    keys = lines(heads_ref[:, :, 0:HD])
+    values = lines(heads_ref[:, :, HD : 2 * HD])
+    scores = lax.dot_general(keys, query, NT, preferred_element_type=jnp.float32) * SCALING
+    attention = jnp.exp(scores - norm) * mask
+    value_grad = lax.dot_general(
+        attention.astype(jnp.bfloat16), grad, NN, preferred_element_type=jnp.float32
+    )
+    probs = lax.dot_general(values, grad, NT, preferred_element_type=jnp.float32)
+    grad_scores = (attention * (probs - delta)).astype(jnp.bfloat16)
+    key_grad = lax.dot_general(grad_scores, query, NN, preferred_element_type=jnp.float32) * SCALING
+    out_ref[:, :, 0:HD] = key_grad.reshape(4, PADDED, HD).astype(jnp.bfloat16)
+    out_ref[:, :, HD : 2 * HD] = value_grad.reshape(4, PADDED, HD).astype(jnp.bfloat16)
 
 
 def attention_grads(tiles, packed, heads):
@@ -193,19 +205,17 @@
 
 def project_kernel(grads_ref, weight_ref, out_ref):
     wide = KVH * HD
-    for t in range(2):
-        for h in range(2):
-            rows = slice(h * 2 * PADDED, (h + 1) * 2 * PADDED)
-            total = sum(
-                lax.dot_general(
-                    grads_ref[0, 2 * p + h],
-                    weight_ref[t * 256 : (t + 1) * 256, p * wide : (p + 1) * wide],
-                    NT,
-                    preferred_element_type=jnp.float32,
-                )
-                for p in range(2)
-            )
-            out_ref[t, 0, rows] = total.astype(jnp.bfloat16)
+    total = sum(
+        lax.dot_general(
+            grads_ref[0, 2 * p : 2 * p + 2].reshape(4 * PADDED, wide),
+            weight_ref[:, p * wide : (p + 1) * wide],
+            NT,
+            preferred_element_type=jnp.float32,
+        )
+        for p in range(2)
+    ).astype(jnp.bfloat16)
+    out_ref[0, 0] = total[:, 0:256]
+    out_ref[1, 0] = total[:, 256:512]
 
 
 def project(grads, weight):
@@ -245,7 +255,7 @@
     tile_counts,
     text_lens,
 ):
-    packed, weight = prepare(
+    packed, weight, longest = prepare(
         layer_gate, text_lens, text_query, attn_out, grad_out, log_norm, k_weight, v_weight
     )
     weight = lax.all_gather(weight, ("zh", "zb", "z1"), axis=0, tiled=True)
@@ -255,7 +265,8 @@
         heads = split_heads(image_keys, image_values)
         heads = lax.all_to_all(heads, "y", split_axis=0, concat_axis=0, tiled=True)
         packed = lax.all_gather(packed, "zh", axis=0, tiled=True)
-        packed = to_all(packed, ("z1", "z0"), 4).reshape(4, 4, PACK, HD)
+        packed = lax.all_gather(packed, ("z1", "z0"), axis=0, tiled=True)
+        packed = packed.reshape(4, 4, PACK, HD)
         part = attention_grads(tile_counts, packed, heads)
         part = part.reshape(2, 2 * PADDED, KVH * HD)
         kept = lax.dynamic_index_in_dim(part, own, 0, keepdims=False)
@@ -264,7 +275,7 @@
         return (kept.astype(jnp.float32) + taken.astype(jnp.float32)).astype(jnp.bfloat16)
 
     grads = lax.cond(
-        jnp.max(text_lens) > 0,
+        longest[0] > 0,
         attend,
         lambda _: jnp.zeros((2 * PADDED, KVH * HD), jnp.bfloat16),
         packed,

time: 192 us -> 179 us (0.932)
  waiting for transfers between devices: 30.5 us -> 3.81 us
  blocking collectives: 112 us -> 132 us
  Pallas kernels: 18 us -> 12.6 us
    all_to_all x1 -> x0, waiting for transfers between devices: 25.3 us -> none  [to_all(): return lax.all_to_all(copies, axes, split_axis=0, concat_axis=0, tiled=True)]
    all_gather x0 -> x1, blocking collectives: none -> 17.9 us  [attend(): packed = lax.all_gather(packed, ('z1', 'z0'), axis=0, tiled=True)]
    ppermute x1, starting transfers between devices: 1.92 us -> 7.55 us  [attend(): taken = lax.ppermute(given, 'y', [(0, 1), (1, 0), (2, 3), (3, 2)])]
    all_to_all x1 -> x0, starting transfers between devices: 4.14 us -> none  [to_all(): return lax.all_to_all(copies, axes, split_axis=0, concat_axis=0, tiled=True)]
    pallas_call x1, Pallas kernels: 6.3 us -> 2.83 us  [attention_grads(): pl.pallas_call(attention_kernel, grid=(4,), in_specs=[pl.BlockSpec(memory...]
    all_to_all x1, blocking collectives: 23.7 us -> 26.6 us  [body(): lax.all_to_all(part, ('core', 'x', 'y'), split_axis=0, concat_axis=0, til...]
    pallas_call x1, Pallas kernels: 8.31 us -> 6.28 us  [project(): pl.pallas_call(project_kernel, grid=(4,), in_specs=[pl.BlockSpec((1, 4, r...]
  transfers between devices with their start and end apart: 4 -> 3, of which waited for: 2 -> 1; matrix products, arithmetic and copies ran while one was open for 1% -> 0% of each run, Pallas kernels for 4% -> 2%
where the time goes in v6:
time: 179 us
  blocking collectives  132 us (74%)
  between operations  14.8 us (8%)
  starting transfers between devices  12.6 us (7%)
  Pallas kernels  12.6 us (7%)
  waiting for transfers between devices  3.81 us (2%)
  local copies, waits for them, and re-layouts  2.84 us (2%)
    all_to_all x1, blocking collectives, to_all(): return lax.all_to_all(copies, axes, split_axis=0, concat_axis=0, tiled=True)  45 us
    all_gather x1, blocking collectives, attend(): packed = lax.all_gather(packed, 'zh', axis=0, tiled=True)  42.4 us
    all_to_all x1, blocking collectives, body(): lax.all_to_all(part, ('core', 'x', 'y'), split_axis=0, concat_axis=0, til...  26.6 us
    all_gather x1, blocking collectives, attend(): packed = lax.all_gather(packed, ('z1', 'z0'), axis=0, tiled=True)  17.9 us
    ppermute x1, starting transfers between devices, attend(): taken = lax.ppermute(given, 'y', [(0, 1), (1, 0), (2, 3), (3, 2)])  7.55 us
    pallas_call x1, Pallas kernels, project(): pl.pallas_call(project_kernel, grid=(4,), in_specs=[pl.BlockSpec((1, 4, r...  6.28 us
    all_to_all x1, starting transfers between devices, attend(): heads = lax.all_to_all(heads, 'y', split_axis=0, concat_axis=0, tiled=True)  5.01 us
    ppermute x1, waiting for transfers between devices, attend(): taken = lax.ppermute(given, 'y', [(0, 1), (1, 0), (2, 3), (3, 2)])  3.79 us
  transfers between devices with their start and end apart: 3, of which 1 were waited for; matrix products, arithmetic and copies ran while one was open for 0% of the time, Pallas kernels for 2%

profile of v6, /device:TPU:1, one launch (start us, length us, event | category | flops | bytes accessed | tf_op | source)
XLA Modules:
  0.0 178.9 jit_solution(2360419516728239573)
XLA Ops:
  6.5 0.0 copy-start
  6.5 0.0 copy-start.1
  6.5 0.0 copy-start.2
  6.5 0.0 all-gather.2.cloned.1.call-start
  7.2 2.6 %shard_map.112 = (bf16[144,128]{1,0:T(8,128)(2,1)S(1)}, bf16[32,2048]{1,0:T(8,128)(2,1)}, s32[1]{0:T(128)}) custom-call(f32[1]{0:T(128)S(6)} %copy.21.gate_ref, s32[8]{0:T(128)} %length_ref.1, bf16[1,8,4,64,128]{4,3,2,1,0:T(8,128)(2,1)} %query_ref.1, bf16[1,8,4,64,128]{4,3,2,1,0:T(8,128)(2,1)} %out_ref.1, bf16[1,8,4,64,128]{4,3,2,1,0:T(8,128)(2,1)} %cot_ref.1, ...), custom_call_target="tpu_custom_call" | custom-call | flops 65536 | bytes 262144 | tf_op jit(solution)/shard_map/pallas_call | solution.py:108
  9.8 0.0 all-gather.2.cloned.1.call-update
  10.5 0.0 copy-done
  10.5 0.0 copy-done.1
  10.5 0.0 copy-done.2
  10.5 80.5 %conditional.1 = (bf16[112,1024]{1,0:T(8,128)(2,1)S(1)}) conditional(s32[]{:T(128)} %bitcast.5, () %tuple.11, (bf16[144,128]{1,0:T(8,128)(2,1)S(1)}, bf16[1,52,1024]{2,1,0:T(8,128)(2,1)S(1)}, bf16[1,52,1024]{2,1,0:T(8,128)(2,1)S(1)}, s32[8]{0:T(128)S(1)}, pred[]{:T(512)}, /*index=5*/s32[]{:T(128)}, s32[]{:T(128)}, (), (), s32[]{:T(128)}, ...), branch_computations={%region_0.1_spmd, %region_1.2_spmd} | conditional | flops 235339776 | bytes 7159627 | solution.py:277
  10.5 0.9 branch_1_fun.2
  11.4 5.0 %all-to-all-start = ((bf16[4,56,1024]{2,1,0:T(8,128)(2,1)}), bf16[4,56,1024]{2,1,0:T(8,128)(2,1)S(1)}, u32[]{:S(2)}, u32[]{:S(2)}) async-start(bf16[4,56,1024]{2,1,0:T(8,128)(2,1)} %branch_1_fun.2), calls=%async_computation | async-start | bytes 917504 | tf_op jit(solution)/shard_map/cond/branch_1_fun/all_to_all | solution.py:266
  16.4 42.4 %all_gather.6 = bf16[576,128]{1,0:T(8,128)(2,1)S(1)} all-gather(bf16[144,128]{1,0:T(8,128)(2,1)S(1)} %get-tuple-element.19), channel_id=1, replica_groups=mesh['core'=2,'x'=4,'zb'=2,'z1'=2,'z0'=2,'zh'=4,'y'=4] {'zh'}, dimensions={0}, use_global_device_ids=true | all-gather | bytes 184320 | tf_op jit(solution)/shard_map/cond/branch_1_fun/all_gather | solution.py:267
  58.9 17.9 %all_gather.7 = bf16[2304,128]{1,0:T(8,128)(2,1)S(1)} all-gather(bf16[576,128]{1,0:T(8,128)(2,1)S(1)} %all_gather.6), channel_id=1, replica_groups=mesh['core'=2,'x'=4,'zb'=2,'z1'=2,'z0'=2,'zh'=4,'y'=4] {'z1','z0'}, dimensions={0}, use_global_device_ids=true | all-gather | bytes 737280 | tf_op jit(solution)/shard_map/cond/branch_1_fun/all_gather | solution.py:268
  76.7 0.0 all-to-all-done.heads_ref
  76.7 2.8 %branch_1_fun.3 = bf16[4,56,1024]{2,1,0:T(8,128)(2,1)S(1)} custom-call(s32[8]{0:T(128)S(1)} %get-tuple-element.37.tiles_ref, bf16[4,4,144,128]{3,2,1,0:T(8,128)(2,1)S(1)} %bitcast.13, bf16[4,56,1024]{2,1,0:T(8,128)(2,1)S(1)} %all-to-all-done.heads_ref), custom_call_target="tpu_custom_call" | custom-call | flops 234881024 | bytes 2097152 | tf_op jit(solution)/shard_map/cond/branch_1_fun/pallas_call | solution.py:187
  79.6 7.6 %collective-permute-start = (bf16[112,1024]{1,0:T(8,128)(2,1)S(1)}, bf16[112,1024]{1,0:T(8,128)(2,1)S(1)}, u32[]{:S(2)}, u32[]{:S(2)}) collective-permute-start(bf16[112,1024]{1,0:T(8,128)(2,1)S(1)} %dynamic-slice_bitcast_fusion), channel_id=1, source_target_pairs={{0,1},{1,0},{2,3},{3,2},{4,5},{5,4},{6,7},{7,6},{8,9},{9,8},{10,11... | collective-permute-start | bytes 688136 | tf_op jit(solution)/shard_map/cond/branch_1_fun/ppermute | solution.py:274
  87.2 3.8 %collective-permute-done = bf16[112,1024]{1,0:T(8,128)(2,1)S(1)} collective-permute-done((bf16[112,1024]{1,0:T(8,128)(2,1)S(1)}, bf16[112,1024]{1,0:T(8,128)(2,1)S(1)}, u32[]{:S(2)}, u32[]{:S(2)}) %collective-permute-start) | collective-permute-done | bytes 229408 | tf_op jit(solution)/shard_map/cond/branch_1_fun/ppermute | solution.py:274
  91.0 0.1 fusion
  91.0 0.5 broadcast_in_dim.2
  91.5 45.0 %all_to_all.14 = bf16[16,112,1024]{2,1,0:T(8,128)(2,1)} all-to-all(bf16[16,112,1024]{2,1,0:T(8,128)(2,1)S(1)} %broadcast_in_dim.2), channel_id=1, replica_groups=mesh['core'=2,'x'=4,'zb'=2,'z1'=2,'z0'=2,'zh'=4,'y'=4] {'x','y'}, dimensions={0} | all-to-all | bytes 7340032 | tf_op jit(solution)/shard_map/all_to_all | solution.py:242
  136.5 0.0 all-gather.2.cloned.1.call-done.weight_ref
  136.5 6.3 %shard_map.113 = bf16[2,4,224,256]{3,2,1,0:T(8,128)(2,1)} custom-call(bf16[4,4,112,1024]{3,2,1,0:T(8,128)(2,1)} %bitcast.16, bf16[512,2048]{1,0:T(8,128)(2,1)} %all-gather.2.cloned.1.call-done.weight_ref), custom_call_target="tpu_custom_call" | custom-call | flops 1879048192 | bytes 7340032 | tf_op jit(solution)/shard_map/pallas_call | solution.py:224
  142.8 26.6 %all_to_all.15 = bf16[32,56,256]{2,1,0:T(8,128)(2,1)S(1)} all-to-all(bf16[32,56,256]{2,1,0:T(8,128)(2,1)} %bitcast.18), channel_id=1, replica_groups=mesh['core'=2,'x'=4,'zb'=2,'z1'=2,'z0'=2,'zh'=4,'y'=4] {'core','x','y'}, dimensions={0} | all-to-all | bytes 1835008 | tf_op jit(solution)/shard_map/all_to_all | solution.py:286
  169.4 0.1 convert_element_type.24
  169.5 0.1 slice_add_fusion
  169.7 0.5 add.24
  170.1 0.1 slice.16
  170.2 0.6 copy.18
  170.8 1.3 reshape.31
  (1 shorter events, 0.0 us)
Async XLA Ops:
  6.5 4.0 %copy-start = (bf16[1,52,1024]{2,1,0:T(8,128)(2,1)S(1)}, bf16[1,52,1024]{2,1,0:T(8,128)(2,1)}, u32[]{:S(2)}) copy-start(bf16[1,52,1024]{2,1,0:T(8,128)(2,1)} %param.17) | copy-start | bytes 319492
  6.5 4.0 %copy-start.1 = (bf16[1,52,1024]{2,1,0:T(8,128)(2,1)S(1)}, bf16[1,52,1024]{2,1,0:T(8,128)(2,1)}, u32[]{:S(2)}) copy-start(bf16[1,52,1024]{2,1,0:T(8,128)(2,1)} %param.18) | copy-start | bytes 319492
  6.5 4.0 %copy-start.2 = (s32[8]{0:T(128)S(1)}, s32[8]{0:T(128)}, u32[]{:S(2)}) copy-start(s32[8]{0:T(128)} %param.22) | copy-start | bytes 100
  6.5 130.0 %all-gather.2.cloned.1.call-start = ((), (), s32[]{:S(2)}) async-start(), calls=%async_computation.3 | async-start | bytes 2228224 | tf_op jit(solution)/shard_map/all_gather | solution.py:261
  11.4 65.3 %all-to-all-start = ((bf16[4,56,1024]{2,1,0:T(8,128)(2,1)}), bf16[4,56,1024]{2,1,0:T(8,128)(2,1)S(1)}, u32[]{:S(2)}, u32[]{:S(2)}) async-start(bf16[4,56,1024]{2,1,0:T(8,128)(2,1)} %branch_1_fun.2), calls=%async_computation | async-start | bytes 917504 | tf_op jit(solution)/shard_map/cond/branch_1_fun/all_to_all | solution.py:266
  79.6 11.4 %collective-permute-start = (bf16[112,1024]{1,0:T(8,128)(2,1)S(1)}, bf16[112,1024]{1,0:T(8,128)(2,1)S(1)}, u32[]{:S(2)}, u32[]{:S(2)}) collective-permute-start(bf16[112,1024]{1,0:T(8,128)(2,1)S(1)} %dynamic-slice_bitcast_fusion), channel_id=1, source_target_pairs={{0,1},{1,0},{2,3},{3,2},{4,5},{5,4},{6,7},{7,6},{8,9},{9,8},{10,11... | collective-permute-start | bytes 688136 | tf_op jit(solution)/shard_map/cond/branch_1_fun/ppermute | solution.py:274
Sparse Core Ops, SparseCore 0:
  10.0 109.7 all-gather.1

commit v7 on v6

--- a/solution.py
+++ b/solution.py
@@ -47,7 +47,7 @@
     sems,
 ):
     x, zb, z1, z0 = (lax.axis_index(name) for name in ("x", "zb", "z1", "z0"))
-    zq = z1 * 2 + z0
+    heads = pl.ds(2 * z0, 2)
     sample = x * 2 + zb
     feature = pl.multiple_of(x * 128 + (zb * 2 + z1) * SLICE, SLICE)
     copies = [
@@ -56,9 +56,9 @@
             [
                 (key_weight_ref.at[0, pl.ds(feature, SLICE)], key_weight),
                 (value_weight_ref.at[0, pl.ds(feature, SLICE)], value_weight),
-                (cot_ref.at[0, sample, zq], cot),
-                (out_ref.at[0, sample, zq], out),
-                (query_ref.at[0, sample, zq], query),
+                (cot_ref.at[0, sample, heads], cot),
+                (out_ref.at[0, sample, heads], out),
+                (query_ref.at[0, sample, heads], query),
             ]
         )
     ]
@@ -75,42 +75,41 @@
         weight_ref[:, place : place + HD] = key_weight[:, g * HD : (g + 1) * HD]
         weight_ref[:, place + HD : place + 2 * HD] = value_weight[:, g * HD : (g + 1) * HD]
 
-    head = lax.broadcasted_iota(jnp.int32, (4, HD), 0) == zq
+    head = lax.broadcasted_iota(jnp.int32, (4, HD), 0)
     place = lax.broadcasted_iota(jnp.int32, (TXT, HD), 0)
     lane = lax.broadcasted_iota(jnp.int32, (TXT, HD), 1)
     twice = jnp.where(lane % TXT == place, 1.0, 0.0).astype(jnp.bfloat16)
     norms = lax.dot_general(norm_ref[0, sample], twice, NN, preferred_element_type=jnp.float32)
-    norm = jnp.sum(jnp.where(head, norms, 0.0), axis=0, keepdims=True)
-
-    copies[2].wait()
     row_mask = jnp.where(place < length_ref[sample], 1.0, 0.0)
     gate = jnp.tanh(jnp.full((TXT, HD), gate_ref[0], jnp.float32))
-    scaled = (gate * cot[...].astype(jnp.float32) * row_mask).astype(jnp.bfloat16)
-    pack_ref[TXT : 2 * TXT] = scaled
-    copies[3].wait()
-    product = scaled.astype(jnp.float32) * out[...].astype(jnp.float32)
-    product = jnp.concatenate([product, product], axis=0)
-    delta = jnp.sum(product.T, axis=0, keepdims=True)
     row = lax.broadcasted_iota(jnp.int32, (16, HD), 0)
-    pack_ref[META : META + 16] = jnp.where(
-        row == 0, norm, jnp.where(row == 1, delta, 0.0)
-    ).astype(jnp.bfloat16)
-    copies[4].wait()
-    pack_ref[0:TXT] = query[...]
+    for copy in copies[2:]:
+        copy.wait()
+    for i in range(2):
+        scaled = (gate * cot[i].astype(jnp.float32) * row_mask).astype(jnp.bfloat16)
+        product = scaled.astype(jnp.float32) * out[i].astype(jnp.float32)
+        product = jnp.concatenate([product, product], axis=0)
+        delta = jnp.sum(product.T, axis=0, keepdims=True)
+        norm = jnp.sum(jnp.where(head == 2 * z0 + i, norms, 0.0), axis=0, keepdims=True)
+        pack_ref[i, 0:TXT] = query[i]
+        pack_ref[i, TXT : 2 * TXT] = scaled
+        pack_ref[i, META : META + 16] = jnp.where(
+            row == 0, norm, jnp.where(row == 1, delta, 0.0)
+        ).astype(jnp.bfloat16)
 
 
 def prepare(layer_gate, text_lens, query, out, cot, norm, key_weight, value_weight):
     whole = pl.BlockSpec(memory_space=pltpu.HBM)
     vmem = pl.BlockSpec(memory_space=pltpu.VMEM)
     smem = pl.BlockSpec(memory_space=pltpu.SMEM)
-    head = pltpu.VMEM((TXT, HD), jnp.bfloat16)
+    head = pltpu.VMEM((2, TXT, HD), jnp.bfloat16)
     rows = pltpu.VMEM((SLICE, KVH * HD), jnp.bfloat16)
     return pl.pallas_call(
         prepare_kernel,
         in_specs=[smem, smem, whole, whole, whole, vmem, whole, whole],
         out_specs=[vmem, vmem, smem],
         out_shape=[
-            jax.ShapeDtypeStruct((PACK, HD), jnp.bfloat16),
+            jax.ShapeDtypeStruct((2, PACK, HD), jnp.bfloat16),
             jax.ShapeDtypeStruct((SLICE, 2 * KVH * HD), jnp.bfloat16),
             jax.ShapeDtypeStruct((1,), jnp.int32),
         ],
@@ -140,16 +139,17 @@
     )(keys, values)
 
 
-def attention_kernel(tiles_ref, pack_ref, heads_ref, out_ref):
+def attention_kernel(tiles_ref, own_ref, other_ref, heads_ref, out_ref):
     x, zb, z1, z0, zh = (lax.axis_index(name) for name in ("x", "zb", "z1", "z0", "zh"))
     tiles = tiles_ref[x * 2 + zb]
-    query = pack_ref[:, 0, 0:TXT, :].reshape(GROUP, HD)
-    grad = pack_ref[:, 0, TXT : 2 * TXT, :].reshape(GROUP, HD)
-    meta = pack_ref[:, 0, META : META + 16, :].astype(jnp.float32)
+    packs = (own_ref, other_ref)
+    query = jnp.concatenate([ref[0, i, 0:TXT] for ref in packs for i in range(2)], axis=0)
+    grad = jnp.concatenate([ref[0, i, TXT : 2 * TXT] for ref in packs for i in range(2)], axis=0)
+    meta = [ref[0, i, META : META + 16].astype(jnp.float32) for ref in packs for i in range(2)]
     left = lax.broadcasted_iota(jnp.int32, (1, HD), 1) < TXT
 
     def line(which):
-        picked = [meta[i, which : which + 1] for i in range(4)]
+        picked = [meta[i][which : which + 1] for i in range(4)]
         return jnp.concatenate(
             [jnp.where(left, picked[i], picked[i + 1]) for i in range(0, 4, 2)], axis=1
         )
@@ -182,14 +182,16 @@
     out_ref[:, :, HD : 2 * HD] = value_grad.reshape(4, PADDED, HD).astype(jnp.bfloat16)
 
 
-def attention_grads(tiles, packed, heads):
+def attention_grads(tiles, own, other, heads):
+    pack = pl.BlockSpec((1, 2, PACK, HD), lambda s: (s, 0, 0, 0))
     piece = pl.BlockSpec((4, PADDED, 2 * HD), lambda s: (0, 0, s))
     return pl.pallas_call(
         attention_kernel,
         grid=(4,),
         in_specs=[
             pl.BlockSpec(memory_space=pltpu.SMEM),
-            pl.BlockSpec((4, 1, PACK, HD), lambda s: (0, s, 0, 0)),
+            pack,
+            pack,
             piece,
         ],
         out_specs=piece,
@@ -200,7 +202,7 @@
             bytes_accessed=2 << 20,
             transcendentals=4 * PADDED * 4 * GROUP,
         ),
-    )(tiles, packed, heads)
+    )(tiles, own, other, heads)
 
 
 def project_kernel(grads_ref, weight_ref, out_ref):
@@ -264,10 +266,9 @@
     def attend(packed):
         heads = split_heads(image_keys, image_values)
         heads = lax.all_to_all(heads, "y", split_axis=0, concat_axis=0, tiled=True)
-        packed = lax.all_gather(packed, "zh", axis=0, tiled=True)
-        packed = lax.all_gather(packed, ("z1", "z0"), axis=0, tiled=True)
-        packed = packed.reshape(4, 4, PACK, HD)
-        part = attention_grads(tile_counts, packed, heads)
+        packed = lax.all_gather(packed, "zh", axis=0, tiled=False)
+        other = lax.ppermute(packed, "z0", [(0, 1), (1, 0)])
+        part = attention_grads(tile_counts, packed, other, heads)
         part = part.reshape(2, 2 * PADDED, KVH * HD)
         kept = lax.dynamic_index_in_dim(part, own, 0, keepdims=False)
         given = lax.dynamic_index_in_dim(part, 1 - own, 0, keepdims=False)

time: 179 us -> 185 us (1.034)
  waiting for transfers between devices: 3.81 us -> 17.6 us
  blocking collectives: 132 us -> 122 us
  starting transfers between devices: 12.6 us -> 15.2 us
    ppermute x0 -> x1, waiting for transfers between devices: none -> 13.8 us  [attend(): other = lax.ppermute(packed, 'z0', [(0, 1), (1, 0)])]
    all_gather x2 -> x1, blocking collectives: 60.3 us -> 49.8 us  [attend(): packed = lax.all_gather(packed, 'zh', axis=0, tiled=False)]
    ppermute x0 -> x1, starting transfers between devices: none -> 5.09 us  [attend(): other = lax.ppermute(packed, 'z0', [(0, 1), (1, 0)])]
    all_to_all x1, blocking collectives: 45 us -> 48.1 us  [to_all(): return lax.all_to_all(copies, axes, split_axis=0, concat_axis=0, tiled=True)]
    all_to_all x1, blocking collectives: 26.6 us -> 23.7 us  [body(): lax.all_to_all(part, ('core', 'x', 'y'), split_axis=0, concat_axis=0, til...]
    ppermute x1, starting transfers between devices: 7.55 us -> 5.07 us  [attend(): taken = lax.ppermute(given, 'y', [(0, 1), (1, 0), (2, 3), (3, 2)])]
  transfers between devices with their start and end apart: 3 -> 4, of which waited for: 1 -> 2; matrix products, arithmetic and copies ran while one was open for 0% -> 0% of each run, Pallas kernels for 2% -> 2%
where the time goes in v7:
time: 185 us
  blocking collectives  122 us (66%)
  waiting for transfers between devices  17.6 us (10%)
  starting transfers between devices  15.2 us (8%)
  between operations  14.8 us (8%)
  Pallas kernels  12.4 us (7%)
  local copies, waits for them, and re-layouts  2.84 us (2%)
    all_gather x1, blocking collectives, attend(): packed = lax.all_gather(packed, 'zh', axis=0, tiled=False)  49.8 us
    all_to_all x1, blocking collectives, to_all(): return lax.all_to_all(copies, axes, split_axis=0, concat_axis=0, tiled=True)  48.1 us
    all_to_all x1, blocking collectives, body(): lax.all_to_all(part, ('core', 'x', 'y'), split_axis=0, concat_axis=0, til...  23.7 us
    ppermute x1, waiting for transfers between devices, attend(): other = lax.ppermute(packed, 'z0', [(0, 1), (1, 0)])  13.8 us
    pallas_call x1, Pallas kernels, project(): pl.pallas_call(project_kernel, grid=(4,), in_specs=[pl.BlockSpec((1, 4, r...  6.28 us
    ppermute x1, starting transfers between devices, attend(): other = lax.ppermute(packed, 'z0', [(0, 1), (1, 0)])  5.09 us
    ppermute x1, starting transfers between devices, attend(): taken = lax.ppermute(given, 'y', [(0, 1), (1, 0), (2, 3), (3, 2)])  5.07 us
    all_to_all x1, starting transfers between devices, attend(): heads = lax.all_to_all(heads, 'y', split_axis=0, concat_axis=0, tiled=True)  5.01 us
  transfers between devices with their start and end apart: 4, of which 2 were waited for; matrix products, arithmetic and copies ran while one was open for 0% of the time, Pallas kernels for 2%

profile of v7, /device:TPU:1, one launch (start us, length us, event | category | flops | bytes accessed | tf_op | source)
XLA Modules:
  0.0 184.9 jit_solution(17063215750796325247)
XLA Ops:
  6.5 0.0 copy-start
  6.5 0.0 copy-start.1
  6.5 0.0 copy-start.2
  6.5 0.0 all-gather.3.cloned.1.call-start
  7.2 2.5 %shard_map.112 = (bf16[2,144,128]{2,1,0:T(8,128)(2,1)S(1)}, bf16[32,2048]{1,0:T(8,128)(2,1)}, s32[1]{0:T(128)}) custom-call(f32[1]{0:T(128)S(6)} %copy.22.gate_ref, s32[8]{0:T(128)} %length_ref.1, bf16[1,8,4,64,128]{4,3,2,1,0:T(8,128)(2,1)} %query_ref.1, bf16[1,8,4,64,128]{4,3,2,1,0:T(8,128)(2,1)} %out_ref.1, bf16[1,8,4,64,128]{4,3,2,1,0:T(8,128)(2,1)} %cot_ref.1, ...), custom_call_target="tpu_custom_call" | custom-call | flops 65536 | bytes 262144 | tf_op jit(solution)/shard_map/pallas_call | solution.py:107
  9.7 0.0 all-gather.3.cloned.1.call-update
  10.4 0.0 copy-done
  10.4 0.0 copy-done.1
  10.4 0.0 copy-done.2
  10.4 86.4 %conditional.1 = (bf16[112,1024]{1,0:T(8,128)(2,1)S(1)}) conditional(s32[]{:T(128)} %bitcast.5, () %tuple.11, (bf16[2,144,128]{2,1,0:T(8,128)(2,1)S(1)}, bf16[1,52,1024]{2,1,0:T(8,128)(2,1)S(1)}, bf16[1,52,1024]{2,1,0:T(8,128)(2,1)S(1)}, s32[8]{0:T(128)S(1)}, pred[]{:T(512)}, /*index=5*/s32[]{:T(128)}, s32[]{:T(128)}, (), (), s32[]{:T(128)}, ...), branch_computations={%region_0.1_spmd, %region_1.2_spmd} | conditional | flops 235339776 | bytes 7786355 | solution.py:278
  10.4 0.9 branch_1_fun.2
  11.3 5.0 %all-to-all-start = ((bf16[4,56,1024]{2,1,0:T(8,128)(2,1)}), bf16[4,56,1024]{2,1,0:T(8,128)(2,1)S(1)}, u32[]{:S(2)}, u32[]{:S(2)}) async-start(bf16[4,56,1024]{2,1,0:T(8,128)(2,1)} %branch_1_fun.2), calls=%async_computation | async-start | bytes 917504 | tf_op jit(solution)/shard_map/cond/branch_1_fun/all_to_all | solution.py:268
  16.3 49.8 %all-gather = bf16[8,144,128]{2,1,0:T(8,128)(2,1)S(1)} all-gather(bf16[2,144,128]{2,1,0:T(8,128)(2,1)S(1)} %get-tuple-element.19), channel_id=2, replica_groups=mesh['core'=2,'x'=4,'zb'=2,'z1'=2,'z0'=2,'zh'=4,'y'=4] {'zh'}, dimensions={0}, use_global_device_ids=true | all-gather | bytes 368640 | tf_op jit(solution)/shard_map/cond/branch_1_fun/all_gather | solution.py:269
  66.1 5.1 %collective-permute-start = (bf16[4,2,144,128]{3,2,1,0:T(8,128)(2,1)S(1)}, bf16[4,2,144,128]{3,2,1,0:T(8,128)(2,1)S(1)}, u32[]{:S(2)}, u32[]{:S(2)}) collective-permute-start(bf16[4,2,144,128]{3,2,1,0:T(8,128)(2,1)S(1)} %bitcast.15), channel_id=1, source_target_pairs={{0,16},{16,0},{1,17},{17,1},{2,18},{18,2},{3,19},{19,3},{4,20},{20... | collective-permute-start | bytes 884744 | tf_op jit(solution)/shard_map/cond/branch_1_fun/ppermute | solution.py:270
  71.2 13.8 %collective-permute-done.other_ref = bf16[4,2,144,128]{3,2,1,0:T(8,128)(2,1)S(1)} collective-permute-done((bf16[4,2,144,128]{3,2,1,0:T(8,128)(2,1)S(1)}, bf16[4,2,144,128]{3,2,1,0:T(8,128)(2,1)S(1)}, u32[]{:S(2)}, u32[]{:S(2)}) %collective-permute-start) | collective-permute-done | bytes 294944 | tf_op jit(solution)/shard_map/cond/branch_1_fun/ppermute | solution.py:270
  85.0 0.0 all-to-all-done.heads_ref
  85.0 2.8 %branch_1_fun.3 = bf16[4,56,1024]{2,1,0:T(8,128)(2,1)S(1)} custom-call(s32[8]{0:T(128)S(1)} %get-tuple-element.37.tiles_ref, bf16[4,2,144,128]{3,2,1,0:T(8,128)(2,1)S(1)} %bitcast.16, bf16[4,2,144,128]{3,2,1,0:T(8,128)(2,1)S(1)} %collective-permute-done.other_ref, bf16[4,56,1024]{2,1,0:T(8,128)(2,1)S(1)} %all-to-all-done.heads_ref), custom_call_target="tpu_custom_call" | custom-call | flops 234881024 | bytes 2097152 | tf_op jit(solution)/shard_map/cond/branch_1_fun/pallas_call | solution.py:188
  87.9 5.1 %collective-permute-start.1 = (bf16[112,1024]{1,0:T(8,128)(2,1)S(1)}, bf16[112,1024]{1,0:T(8,128)(2,1)S(1)}, u32[]{:S(2)}, u32[]{:S(2)}) collective-permute-start(bf16[112,1024]{1,0:T(8,128)(2,1)S(1)} %dynamic-slice_bitcast_fusion), channel_id=1, source_target_pairs={{0,1},{1,0},{2,3},{3,2},{4,5},{5,4},{6,7},{7,6},{8,9},{9,8},{10,11... | collective-permute-start | bytes 688136 | tf_op jit(solution)/shard_map/cond/branch_1_fun/ppermute | solution.py:275
  93.0 3.8 %collective-permute-done.1 = bf16[112,1024]{1,0:T(8,128)(2,1)S(1)} collective-permute-done((bf16[112,1024]{1,0:T(8,128)(2,1)S(1)}, bf16[112,1024]{1,0:T(8,128)(2,1)S(1)}, u32[]{:S(2)}, u32[]{:S(2)}) %collective-permute-start.1) | collective-permute-done | bytes 229408 | tf_op jit(solution)/shard_map/cond/branch_1_fun/ppermute | solution.py:275
  96.8 0.1 fusion
  96.8 0.5 broadcast_in_dim.2
  97.3 48.1 %all_to_all.14 = bf16[16,112,1024]{2,1,0:T(8,128)(2,1)} all-to-all(bf16[16,112,1024]{2,1,0:T(8,128)(2,1)S(1)} %broadcast_in_dim.2), channel_id=1, replica_groups=mesh['core'=2,'x'=4,'zb'=2,'z1'=2,'z0'=2,'zh'=4,'y'=4] {'x','y'}, dimensions={0} | all-to-all | bytes 7340032 | tf_op jit(solution)/shard_map/all_to_all | solution.py:244
  145.4 0.0 all-gather.3.cloned.1.call-done.weight_ref
  145.4 6.3 %shard_map.113 = bf16[2,4,224,256]{3,2,1,0:T(8,128)(2,1)} custom-call(bf16[4,4,112,1024]{3,2,1,0:T(8,128)(2,1)} %bitcast.17, bf16[512,2048]{1,0:T(8,128)(2,1)} %all-gather.3.cloned.1.call-done.weight_ref), custom_call_target="tpu_custom_call" | custom-call | flops 1879048192 | bytes 7340032 | tf_op jit(solution)/shard_map/pallas_call | solution.py:226
  151.7 23.7 %all_to_all.15 = bf16[32,56,256]{2,1,0:T(8,128)(2,1)S(1)} all-to-all(bf16[32,56,256]{2,1,0:T(8,128)(2,1)} %bitcast.19), channel_id=1, replica_groups=mesh['core'=2,'x'=4,'zb'=2,'z1'=2,'z0'=2,'zh'=4,'y'=4] {'core','x','y'}, dimensions={0} | all-to-all | bytes 1835008 | tf_op jit(solution)/shard_map/all_to_all | solution.py:287
  175.4 0.1 convert_element_type.24
  175.5 0.1 slice_add_fusion
  175.7 0.5 add.24
  176.2 0.1 slice.16
  176.2 0.6 copy.19
  176.8 1.3 reshape.28
  (1 shorter events, 0.0 us)
Async XLA Ops:
  6.5 3.8 %copy-start = (bf16[1,52,1024]{2,1,0:T(8,128)(2,1)S(1)}, bf16[1,52,1024]{2,1,0:T(8,128)(2,1)}, u32[]{:S(2)}) copy-start(bf16[1,52,1024]{2,1,0:T(8,128)(2,1)} %param.17) | copy-start | bytes 319492
  6.5 3.8 %copy-start.1 = (bf16[1,52,1024]{2,1,0:T(8,128)(2,1)S(1)}, bf16[1,52,1024]{2,1,0:T(8,128)(2,1)}, u32[]{:S(2)}) copy-start(bf16[1,52,1024]{2,1,0:T(8,128)(2,1)} %param.18) | copy-start | bytes 319492
  6.5 3.9 %copy-start.2 = (s32[8]{0:T(128)S(1)}, s32[8]{0:T(128)}, u32[]{:S(2)}) copy-start(s32[8]{0:T(128)} %param.22) | copy-start | bytes 100
  6.5 138.9 %all-gather.3.cloned.1.call-start = ((), (), s32[]{:S(2)}) async-start(), calls=%async_computation.3 | async-start | bytes 2228224 | tf_op jit(solution)/shard_map/all_gather | solution.py:263
  11.3 73.8 %all-to-all-start = ((bf16[4,56,1024]{2,1,0:T(8,128)(2,1)}), bf16[4,56,1024]{2,1,0:T(8,128)(2,1)S(1)}, u32[]{:S(2)}, u32[]{:S(2)}) async-start(bf16[4,56,1024]{2,1,0:T(8,128)(2,1)} %branch_1_fun.2), calls=%async_computation | async-start | bytes 917504 | tf_op jit(solution)/shard_map/cond/branch_1_fun/all_to_all | solution.py:268
  66.1 18.9 %collective-permute-start = (bf16[4,2,144,128]{3,2,1,0:T(8,128)(2,1)S(1)}, bf16[4,2,144,128]{3,2,1,0:T(8,128)(2,1)S(1)}, u32[]{:S(2)}, u32[]{:S(2)}) collective-permute-start(bf16[4,2,144,128]{3,2,1,0:T(8,128)(2,1)S(1)} %bitcast.15), channel_id=1, source_target_pairs={{0,16},{16,0},{1,17},{17,1},{2,18},{18,2},{3,19},{19,3},{4,20},{20... | collective-permute-start | bytes 884744 | tf_op jit(solution)/shard_map/cond/branch_1_fun/ppermute | solution.py:270
  87.9 8.9 %collective-permute-start.1 = (bf16[112,1024]{1,0:T(8,128)(2,1)S(1)}, bf16[112,1024]{1,0:T(8,128)(2,1)S(1)}, u32[]{:S(2)}, u32[]{:S(2)}) collective-permute-start(bf16[112,1024]{1,0:T(8,128)(2,1)S(1)} %dynamic-slice_bitcast_fusion), channel_id=1, source_target_pairs={{0,1},{1,0},{2,3},{3,2},{4,5},{5,4},{6,7},{7,6},{8,9},{9,8},{10,11... | collective-permute-start | bytes 688136 | tf_op jit(solution)/shard_map/cond/branch_1_fun/ppermute | solution.py:275
Sparse Core Ops, SparseCore 0:
  10.0 108.8 all-gather.2

commit v8 on v6

--- a/solution.py
+++ b/solution.py
@@ -203,7 +203,7 @@
     )(tiles, packed, heads)
 
 
-def project_kernel(grads_ref, weight_ref, out_ref):
+def project_kernel(grads_ref, weight_ref, kept_ref, given_ref):
     wide = KVH * HD
     total = sum(
         lax.dot_general(
@@ -213,14 +213,17 @@
             preferred_element_type=jnp.float32,
         )
         for p in range(2)
-    ).astype(jnp.bfloat16)
-    out_ref[0, 0] = total[:, 0:256]
-    out_ref[1, 0] = total[:, 256:512]
+    )
+    first = lax.axis_index("core") == 0
+    low, high = total[:, 0:256], total[:, 256:512]
+    kept_ref[0] = jnp.where(first, low, high)
+    given_ref[0] = jnp.where(first, high, low).astype(jnp.bfloat16)
 
 
 def project(grads, weight):
     features, depth = weight.shape
     rows = 4 * PADDED
+    half = pl.BlockSpec((1, rows, features // 2), lambda x: (x, 0, 0))
     return pl.pallas_call(
         project_kernel,
         grid=(4,),
@@ -228,13 +231,34 @@
             pl.BlockSpec((1, 4, rows // 2, depth // 2), lambda x: (x, 0, 0, 0)),
             pl.BlockSpec((features, depth), lambda x: (0, 0)),
         ],
-        out_specs=pl.BlockSpec((2, 1, rows, features // 2), lambda x: (0, x, 0, 0)),
-        out_shape=jax.ShapeDtypeStruct((2, 4, rows, features // 2), jnp.bfloat16),
+        out_specs=[half, half],
+        out_shape=[
+            jax.ShapeDtypeStruct((4, rows, features // 2), jnp.float32),
+            jax.ShapeDtypeStruct((4, rows, features // 2), jnp.bfloat16),
+        ],
         compiler_params=pltpu.CompilerParams(vmem_limit_bytes=WHOLE_VMEM),
         cost_estimate=pl.CostEstimate(
             flops=8 * rows * features * depth, bytes_accessed=7 << 20, transcendentals=0
         ),
     )(grads, weight)
+
+
+def in_columns_kernel(part_ref, out_ref):
+    for z in range(2):
+        for y in range(4):
+            for x in range(4):
+                place = (z * 16 + y * 4 + x) * HD
+                block = part_ref[x * 4 + y, :, z * HD : (z + 1) * HD].astype(jnp.float32)
+                out_ref[:, place : place + HD] = block[0:ROWS]
+
+
+def in_columns(part):
+    return pl.pallas_call(
+        in_columns_kernel,
+        out_shape=jax.ShapeDtypeStruct((ROWS, 2 * 4 * 4 * HD), jnp.float32),
+        compiler_params=pltpu.CompilerParams(vmem_limit_bytes=VMEM_LIMIT),
+        cost_estimate=pl.CostEstimate(flops=0, bytes_accessed=1400000, transcendentals=0),
+    )(part)
 
 
 def to_all(array, axes, count):
@@ -282,11 +306,11 @@
     )
 
     grads = to_all(grads, ("x", "y"), 16).reshape(4, 4, 2 * PADDED, KVH * HD)
-    part = project(grads, weight).reshape(32, PADDED, 256)
-    part = lax.all_to_all(part, ("core", "x", "y"), split_axis=0, concat_axis=0, tiled=True)
-    part = part.reshape(2, 4, 4, PADDED, 2, HD).astype(jnp.float32)
-    total = (part[0] + part[1])[:, :, :ROWS]
-    return total.transpose(2, 3, 1, 0, 4).reshape(ROWS, 2 * 4 * 4 * HD)
+    kept, given = project(grads, weight)
+    taken = lax.ppermute(given, "core", [(0, 1), (1, 0)])
+    part = (kept + taken.astype(jnp.float32)).astype(jnp.bfloat16).reshape(16, PADDED, 256)
+    part = lax.all_to_all(part, ("x", "y"), split_axis=0, concat_axis=0, tiled=True)
+    return in_columns(part)
 
 
 def solution(mesh):

time: 179 us -> 177 us (0.989)
  blocking collectives: 132 us -> 118 us
  starting transfers between devices: 12.6 us -> 22.8 us
  local copies, waits for them, and re-layouts: 2.84 us -> 0.49 us
    all_to_all x1, blocking collectives: 26.6 us -> 13.4 us  [body(): lax.all_to_all(part, ('x', 'y'), split_axis=0, concat_axis=0, tiled=True)]
    ppermute x0 -> x1, starting transfers between devices: none -> 9.92 us  [body(): taken = lax.ppermute(given, 'core', [(0, 1), (1, 0)])]
  transfers between devices with their start and end apart: 3 -> 4, of which waited for: 1 -> 2; matrix products, arithmetic and copies ran while one was open for 0% -> 0% of each run, Pallas kernels for 2% -> 2%
where the time goes in v8:
time: 177 us; the launch traced here: 176 us
  blocking collectives  118 us (67%)
  starting transfers between devices  22.8 us (13%)
  between operations  14.8 us (8%)
  Pallas kernels  13.6 us (8%)
  waiting for transfers between devices  5.44 us (3%)
    all_to_all x1, blocking collectives, to_all(): return lax.all_to_all(copies, axes, split_axis=0, concat_axis=0, tiled=True)  44.2 us
    all_gather x1, blocking collectives, attend(): packed = lax.all_gather(packed, 'zh', axis=0, tiled=True)  42.4 us
    all_gather x1, blocking collectives, attend(): packed = lax.all_gather(packed, ('z1', 'z0'), axis=0, tiled=True)  17.8 us
    all_to_all x1, blocking collectives, body(): lax.all_to_all(part, ('x', 'y'), split_axis=0, concat_axis=0, tiled=True)  13.4 us
    ppermute x1, starting transfers between devices, body(): taken = lax.ppermute(given, 'core', [(0, 1), (1, 0)])  9.92 us
    ppermute x1, starting transfers between devices, attend(): taken = lax.ppermute(given, 'y', [(0, 1), (1, 0), (2, 3), (3, 2)])  7.87 us
    pallas_call x1, Pallas kernels, project(): pl.pallas_call(project_kernel, grid=(4,), in_specs=[pl.BlockSpec((1, 4, r...  6.35 us
    all_to_all x1, starting transfers between devices, attend(): heads = lax.all_to_all(heads, 'y', split_axis=0, concat_axis=0, tiled=True)  5.01 us
  transfers between devices with their start and end apart: 4, of which 2 were waited for; matrix products, arithmetic and copies ran while one was open for 0% of the time, Pallas kernels for 2%

profile of v8, /device:TPU:1, one launch (start us, length us, event | category | flops | bytes accessed | tf_op | source)
XLA Modules:
  0.0 176.4 jit_solution(3532696156494195567)
XLA Ops:
  6.5 0.0 copy-start
  6.5 0.0 copy-start.1
  6.5 0.0 copy-start.2
  6.5 0.0 all-gather.2.cloned.1.call-start
  7.2 2.6 %shard_map.112 = (bf16[144,128]{1,0:T(8,128)(2,1)S(1)}, bf16[32,2048]{1,0:T(8,128)(2,1)}, s32[1]{0:T(128)}) custom-call(f32[1]{0:T(128)S(6)} %copy.17.gate_ref, s32[8]{0:T(128)} %length_ref.1, bf16[1,8,4,64,128]{4,3,2,1,0:T(8,128)(2,1)} %query_ref.1, bf16[1,8,4,64,128]{4,3,2,1,0:T(8,128)(2,1)} %out_ref.1, bf16[1,8,4,64,128]{4,3,2,1,0:T(8,128)(2,1)} %cot_ref.1, ...), custom_call_target="tpu_custom_call" | custom-call | flops 65536 | bytes 262144 | tf_op jit(solution)/shard_map/pallas_call | solution.py:108
  9.8 0.0 all-gather.2.cloned.1.call-update
  10.5 0.0 copy-done
  10.5 0.0 copy-done.1
  10.5 0.0 copy-done.2
  10.5 80.8 %conditional.1 = (bf16[112,1024]{1,0:T(8,128)(2,1)S(1)}) conditional(s32[]{:T(128)} %bitcast.5, () %tuple.11, (bf16[144,128]{1,0:T(8,128)(2,1)S(1)}, bf16[1,52,1024]{2,1,0:T(8,128)(2,1)S(1)}, bf16[1,52,1024]{2,1,0:T(8,128)(2,1)S(1)}, s32[8]{0:T(128)S(1)}, pred[]{:T(512)}, /*index=5*/s32[]{:T(128)}, s32[]{:T(128)}, (), (), s32[]{:T(128)}, ...), branch_computations={%region_0.1_spmd, %region_1.2_spmd} | conditional | flops 235339776 | bytes 7159627 | solution.py:301
  10.5 0.9 branch_1_fun.2
  11.4 5.0 %all-to-all-start = ((bf16[4,56,1024]{2,1,0:T(8,128)(2,1)}), bf16[4,56,1024]{2,1,0:T(8,128)(2,1)S(1)}, u32[]{:S(2)}, u32[]{:S(2)}) async-start(bf16[4,56,1024]{2,1,0:T(8,128)(2,1)} %branch_1_fun.2), calls=%async_computation | async-start | bytes 917504 | tf_op jit(solution)/shard_map/cond/branch_1_fun/all_to_all | solution.py:290
  16.4 42.4 %all_gather.6 = bf16[576,128]{1,0:T(8,128)(2,1)S(1)} all-gather(bf16[144,128]{1,0:T(8,128)(2,1)S(1)} %get-tuple-element.19), channel_id=1, replica_groups=mesh['core'=2,'x'=4,'zb'=2,'z1'=2,'z0'=2,'zh'=4,'y'=4] {'zh'}, dimensions={0}, use_global_device_ids=true | all-gather | bytes 184320 | tf_op jit(solution)/shard_map/cond/branch_1_fun/all_gather | solution.py:291
  58.8 17.8 %all_gather.7 = bf16[2304,128]{1,0:T(8,128)(2,1)S(1)} all-gather(bf16[576,128]{1,0:T(8,128)(2,1)S(1)} %all_gather.6), channel_id=1, replica_groups=mesh['core'=2,'x'=4,'zb'=2,'z1'=2,'z0'=2,'zh'=4,'y'=4] {'z1','z0'}, dimensions={0}, use_global_device_ids=true | all-gather | bytes 737280 | tf_op jit(solution)/shard_map/cond/branch_1_fun/all_gather | solution.py:292
  76.7 0.0 all-to-all-done.heads_ref
  76.7 2.8 %branch_1_fun.3 = bf16[4,56,1024]{2,1,0:T(8,128)(2,1)S(1)} custom-call(s32[8]{0:T(128)S(1)} %get-tuple-element.41.tiles_ref, bf16[4,4,144,128]{3,2,1,0:T(8,128)(2,1)S(1)} %bitcast.10, bf16[4,56,1024]{2,1,0:T(8,128)(2,1)S(1)} %all-to-all-done.heads_ref), custom_call_target="tpu_custom_call" | custom-call | flops 234881024 | bytes 2097152 | tf_op jit(solution)/shard_map/cond/branch_1_fun/pallas_call | solution.py:187
  79.6 7.9 %collective-permute-start = (bf16[112,1024]{1,0:T(8,128)(2,1)S(1)}, bf16[112,1024]{1,0:T(8,128)(2,1)S(1)}, u32[]{:S(2)}, u32[]{:S(2)}) collective-permute-start(bf16[112,1024]{1,0:T(8,128)(2,1)S(1)} %dynamic-slice_bitcast_fusion), channel_id=1, source_target_pairs={{0,1},{1,0},{2,3},{3,2},{4,5},{5,4},{6,7},{7,6},{8,9},{9,8},{10,11... | collective-permute-start | bytes 688136 | tf_op jit(solution)/shard_map/cond/branch_1_fun/ppermute | solution.py:298
  87.4 3.8 %collective-permute-done = bf16[112,1024]{1,0:T(8,128)(2,1)S(1)} collective-permute-done((bf16[112,1024]{1,0:T(8,128)(2,1)S(1)}, bf16[112,1024]{1,0:T(8,128)(2,1)S(1)}, u32[]{:S(2)}, u32[]{:S(2)}) %collective-permute-start) | collective-permute-done | bytes 229408 | tf_op jit(solution)/shard_map/cond/branch_1_fun/ppermute | solution.py:298
  91.2 0.1 fusion
  91.3 0.5 broadcast_in_dim.2
  91.8 44.2 %all_to_all.14 = bf16[16,112,1024]{2,1,0:T(8,128)(2,1)} all-to-all(bf16[16,112,1024]{2,1,0:T(8,128)(2,1)S(1)} %broadcast_in_dim.2), channel_id=1, replica_groups=mesh['core'=2,'x'=4,'zb'=2,'z1'=2,'z0'=2,'zh'=4,'y'=4] {'x','y'}, dimensions={0} | all-to-all | bytes 7340032 | tf_op jit(solution)/shard_map/all_to_all | solution.py:266
  136.0 0.0 all-gather.2.cloned.1.call-done.weight_ref
  136.0 6.4 %shard_map.113 = (f32[4,224,256]{2,1,0:T(8,128)}, bf16[4,224,256]{2,1,0:T(8,128)(2,1)}) custom-call(bf16[4,4,112,1024]{3,2,1,0:T(8,128)(2,1)} %bitcast.13, bf16[512,2048]{1,0:T(8,128)(2,1)} %all-gather.2.cloned.1.call-done.weight_ref), custom_call_target="tpu_custom_call" | custom-call | flops 1879048192 | bytes 7340032 | tf_op jit(solution)/shard_map/pallas_call | solution.py:227
  142.4 9.9 %collective-permute-start.1 = (bf16[4,224,256]{2,1,0:T(8,128)(2,1)}, bf16[4,224,256]{2,1,0:T(8,128)(2,1)S(1)}, u32[]{:S(2)}, u32[]{:S(2)}) collective-permute-start(bf16[4,224,256]{2,1,0:T(8,128)(2,1)} %get-tuple-element.32), channel_id=1, source_target_pairs={{0,512},{512,0},{1,513},{513,1},{2,514},{514,2},{3,515},{515,3},{4... | collective-permute-start | bytes 1376264 | tf_op jit(solution)/shard_map/ppermute | solution.py:310
  152.3 1.6 collective-permute-done.1
  153.9 1.3 add_convert_fusion
  155.2 13.4 %all_to_all.15.part_ref = bf16[16,56,256]{2,1,0:T(8,128)(2,1)S(1)} all-to-all(bf16[16,56,256]{2,1,0:T(8,128)(2,1)S(1)} %bitcast.14), channel_id=1, replica_groups=mesh['core'=2,'x'=4,'zb'=2,'z1'=2,'z0'=2,'zh'=4,'y'=4] {'x','y'}, dimensions={0} | all-to-all | bytes 917504 | tf_op jit(solution)/shard_map/all_to_all | solution.py:312
  168.6 1.0 shard_map.114
  (1 shorter events, 0.0 us)
Async XLA Ops:
  6.5 4.0 %copy-start = (bf16[1,52,1024]{2,1,0:T(8,128)(2,1)S(1)}, bf16[1,52,1024]{2,1,0:T(8,128)(2,1)}, u32[]{:S(2)}) copy-start(bf16[1,52,1024]{2,1,0:T(8,128)(2,1)} %param.17) | copy-start | bytes 319492
  6.5 4.0 %copy-start.1 = (bf16[1,52,1024]{2,1,0:T(8,128)(2,1)S(1)}, bf16[1,52,1024]{2,1,0:T(8,128)(2,1)}, u32[]{:S(2)}) copy-start(bf16[1,52,1024]{2,1,0:T(8,128)(2,1)} %param.18) | copy-start | bytes 319492
  6.5 4.0 %copy-start.2 = (s32[8]{0:T(128)S(1)}, s32[8]{0:T(128)}, u32[]{:S(2)}) copy-start(s32[8]{0:T(128)} %param.22) | copy-start | bytes 100
  6.5 129.5 %all-gather.2.cloned.1.call-start = ((), (), s32[]{:S(2)}) async-start(), calls=%async_computation.3 | async-start | bytes 2228224 | tf_op jit(solution)/shard_map/all_gather | solution.py:285
  11.4 65.3 %all-to-all-start = ((bf16[4,56,1024]{2,1,0:T(8,128)(2,1)}), bf16[4,56,1024]{2,1,0:T(8,128)(2,1)S(1)}, u32[]{:S(2)}, u32[]{:S(2)}) async-start(bf16[4,56,1024]{2,1,0:T(8,128)(2,1)} %branch_1_fun.2), calls=%async_computation | async-start | bytes 917504 | tf_op jit(solution)/shard_map/cond/branch_1_fun/all_to_all | solution.py:290
  79.6 11.7 %collective-permute-start = (bf16[112,1024]{1,0:T(8,128)(2,1)S(1)}, bf16[112,1024]{1,0:T(8,128)(2,1)S(1)}, u32[]{:S(2)}, u32[]{:S(2)}) collective-permute-start(bf16[112,1024]{1,0:T(8,128)(2,1)S(1)} %dynamic-slice_bitcast_fusion), channel_id=1, source_target_pairs={{0,1},{1,0},{2,3},{3,2},{4,5},{5,4},{6,7},{7,6},{8,9},{9,8},{10,11... | collective-permute-start | bytes 688136 | tf_op jit(solution)/shard_map/cond/branch_1_fun/ppermute | solution.py:298
  142.4 11.6 %collective-permute-start.1 = (bf16[4,224,256]{2,1,0:T(8,128)(2,1)}, bf16[4,224,256]{2,1,0:T(8,128)(2,1)S(1)}, u32[]{:S(2)}, u32[]{:S(2)}) collective-permute-start(bf16[4,224,256]{2,1,0:T(8,128)(2,1)} %get-tuple-element.32), channel_id=1, source_target_pairs={{0,512},{512,0},{1,513},{513,1},{2,514},{514,2},{3,515},{515,3},{4... | collective-permute-start | bytes 1376264 | tf_op jit(solution)/shard_map/ppermute | solution.py:310
Sparse Core Ops, SparseCore 0:
  10.0 109.1 all-gather.1

commit v9 on v8

--- a/solution.py
+++ b/solution.py
@@ -121,11 +121,9 @@
 
 
 def split_heads_kernel(key_ref, value_ref, out_ref):
-    below = jnp.zeros((PADDED - ROWS, HD), jnp.float32)
     for part, ref in enumerate((key_ref, value_ref)):
         for g in range(KVH):
-            head = ref[0, :, g * HD : (g + 1) * HD].astype(jnp.float32)
-            head = jnp.concatenate([head, below], axis=0).astype(jnp.bfloat16)
+            head = ref[0, :, g * HD : (g + 1) * HD]
             place = (g // 2 * 2 + part) * HD
             out_ref[g % 2 * 2, :, place : place + HD] = head
             out_ref[g % 2 * 2 + 1, :, place : place + HD] = head
@@ -134,7 +132,7 @@
 def split_heads(keys, values):
     return pl.pallas_call(
         split_heads_kernel,
-        out_shape=jax.ShapeDtypeStruct((4, PADDED, KVH * HD), jnp.bfloat16),
+        out_shape=jax.ShapeDtypeStruct((4, ROWS, KVH * HD), jnp.bfloat16),
         compiler_params=pltpu.CompilerParams(vmem_limit_bytes=VMEM_LIMIT),
         cost_estimate=pl.CostEstimate(flops=0, bytes_accessed=700000, transcendentals=0),
     )(keys, values)
@@ -155,18 +153,17 @@
         )
 
     norm, delta = line(0), line(1)
-    line_rows = 4 * PADDED
+    line_rows = 4 * ROWS
     wide_row = lax.broadcasted_iota(jnp.int32, (line_rows, GROUP), 0)
-    y = sum(jnp.where(wide_row >= i * PADDED, 1, 0) for i in (1, 2, 3))
-    row = wide_row - y * PADDED
-    position = ((z1 * 2 + z0) * 16 + zh * 4 + y) * ROWS + row
+    position = ((z1 * 2 + z0) * 16 + zh * 4) * ROWS + wide_row
     second = position >= TILE_PAD
     inside = jnp.where(second, position - TILE_PAD, position) < TILE_LEN
     present = jnp.where(second, 1, 0) < tiles
-    mask = jnp.where(inside & present & (row < ROWS), 1.0, 0.0)
+    mask = jnp.where(inside & present, 1.0, 0.0)
 
     def lines(block):
-        return block.astype(jnp.float32).reshape(line_rows, HD).astype(jnp.bfloat16)
+        wide = block.astype(jnp.float32)
+        return jnp.concatenate([wide[i] for i in range(4)], axis=0).astype(jnp.bfloat16)
 
     keys = lines(heads_ref[:, :, 0:HD])
     values = lines(heads_ref[:, :, HD : 2 * HD])
@@ -178,12 +175,12 @@
     probs = lax.dot_general(values, grad, NT, preferred_element_type=jnp.float32)
     grad_scores = (attention * (probs - delta)).astype(jnp.bfloat16)
     key_grad = lax.dot_general(grad_scores, query, NN, preferred_element_type=jnp.float32) * SCALING
-    out_ref[:, :, 0:HD] = key_grad.reshape(4, PADDED, HD).astype(jnp.bfloat16)
-    out_ref[:, :, HD : 2 * HD] = value_grad.reshape(4, PADDED, HD).astype(jnp.bfloat16)
+    out_ref[:, 0:HD] = key_grad.astype(jnp.bfloat16)
+    out_ref[:, HD : 2 * HD] = value_grad.astype(jnp.bfloat16)
 
 
 def attention_grads(tiles, packed, heads):
-    piece = pl.BlockSpec((4, PADDED, 2 * HD), lambda s: (0, 0, s))
+    piece = pl.BlockSpec((4, ROWS, 2 * HD), lambda s: (0, 0, s))
     return pl.pallas_call(
         attention_kernel,
         grid=(4,),
@@ -192,13 +189,13 @@
             pl.BlockSpec((4, 1, PACK, HD), lambda s: (0, s, 0, 0)),
             piece,
         ],
-        out_specs=piece,
-        out_shape=jax.ShapeDtypeStruct((4, PADDED, KVH * HD), jnp.bfloat16),
+        out_specs=pl.BlockSpec((4 * ROWS, 2 * HD), lambda s: (0, s)),
+        out_shape=jax.ShapeDtypeStruct((4 * ROWS, KVH * HD), jnp.bfloat16),
         compiler_params=pltpu.CompilerParams(vmem_limit_bytes=VMEM_LIMIT),
         cost_estimate=pl.CostEstimate(
-            flops=8 * 4 * PADDED * 4 * GROUP * HD,
+            flops=8 * 4 * ROWS * 4 * GROUP * HD,
             bytes_accessed=2 << 20,
-            transcendentals=4 * PADDED * 4 * GROUP,
+            transcendentals=4 * ROWS * 4 * GROUP,
         ),
     )(tiles, packed, heads)
 
@@ -207,7 +204,7 @@
     wide = KVH * HD
     total = sum(
         lax.dot_general(
-            grads_ref[0, 2 * p : 2 * p + 2].reshape(4 * PADDED, wide),
+            grads_ref[0, p],
             weight_ref[:, p * wide : (p + 1) * wide],
             NT,
             preferred_element_type=jnp.float32,
@@ -216,25 +213,30 @@
     )
     first = lax.axis_index("core") == 0
     low, high = total[:, 0:256], total[:, 256:512]
-    kept_ref[0] = jnp.where(first, low, high)
-    given_ref[0] = jnp.where(first, high, low).astype(jnp.bfloat16)
+    kept = jnp.where(first, low, high)
+    given = jnp.where(first, high, low)
+    below = jnp.zeros((PADDED - ROWS, 256), jnp.float32)
+    for y in range(4):
+        rows = slice(y * ROWS, (y + 1) * ROWS)
+        kept_ref[y] = jnp.concatenate([kept[rows], below], axis=0)
+        given_ref[y] = jnp.concatenate([given[rows], below], axis=0).astype(jnp.bfloat16)
 
 
 def project(grads, weight):
     features, depth = weight.shape
-    rows = 4 * PADDED
-    half = pl.BlockSpec((1, rows, features // 2), lambda x: (x, 0, 0))
+    rows = 4 * ROWS
+    half = pl.BlockSpec((4, PADDED, features // 2), lambda x: (x, 0, 0))
     return pl.pallas_call(
         project_kernel,
         grid=(4,),
         in_specs=[
-            pl.BlockSpec((1, 4, rows // 2, depth // 2), lambda x: (x, 0, 0, 0)),
+            pl.BlockSpec((1, 2, rows, depth // 2), lambda x: (x, 0, 0, 0)),
             pl.BlockSpec((features, depth), lambda x: (0, 0)),
         ],
         out_specs=[half, half],
         out_shape=[
-            jax.ShapeDtypeStruct((4, rows, features // 2), jnp.float32),
-            jax.ShapeDtypeStruct((4, rows, features // 2), jnp.bfloat16),
+            jax.ShapeDtypeStruct((16, PADDED, features // 2), jnp.float32),
+            jax.ShapeDtypeStruct((16, PADDED, features // 2), jnp.bfloat16),
         ],
         compiler_params=pltpu.CompilerParams(vmem_limit_bytes=WHOLE_VMEM),
         cost_estimate=pl.CostEstimate(
@@ -286,13 +288,14 @@
     own = lax.axis_index("y") % 2
 
     def attend(packed):
-        heads = split_heads(image_keys, image_values)
+        packed = lax.all_gather(packed, "zh", axis=0, tiled=True)
+        packed, keys, values = lax.optimization_barrier((packed, image_keys, image_values))
+        heads = split_heads(keys, values)
         heads = lax.all_to_all(heads, "y", split_axis=0, concat_axis=0, tiled=True)
-        packed = lax.all_gather(packed, "zh", axis=0, tiled=True)
         packed = lax.all_gather(packed, ("z1", "z0"), axis=0, tiled=True)
         packed = packed.reshape(4, 4, PACK, HD)
         part = attention_grads(tile_counts, packed, heads)
-        part = part.reshape(2, 2 * PADDED, KVH * HD)
+        part = part.reshape(2, 2 * ROWS, KVH * HD)
         kept = lax.dynamic_index_in_dim(part, own, 0, keepdims=False)
         given = lax.dynamic_index_in_dim(part, 1 - own, 0, keepdims=False)
         taken = lax.ppermute(given, "y", [(0, 1), (1, 0), (2, 3), (3, 2)])
@@ -301,14 +304,14 @@
     grads = lax.cond(
         longest[0] > 0,
         attend,
-        lambda _: jnp.zeros((2 * PADDED, KVH * HD), jnp.bfloat16),
+        lambda _: jnp.zeros((2 * ROWS, KVH * HD), jnp.bfloat16),
         packed,
     )
 
-    grads = to_all(grads, ("x", "y"), 16).reshape(4, 4, 2 * PADDED, KVH * HD)
+    grads = to_all(grads, ("x", "y"), 16).reshape(4, 2, 4 * ROWS, KVH * HD)
     kept, given = project(grads, weight)
     taken = lax.ppermute(given, "core", [(0, 1), (1, 0)])
-    part = (kept + taken.astype(jnp.float32)).astype(jnp.bfloat16).reshape(16, PADDED, 256)
+    part = (kept + taken.astype(jnp.float32)).astype(jnp.bfloat16)
     part = lax.all_to_all(part, ("x", "y"), split_axis=0, concat_axis=0, tiled=True)
     return in_columns(part)
 

time: 177 us -> 170 us (0.960)
  blocking collectives: 118 us -> 109 us
  starting transfers between devices: 22.8 us -> 24.9 us
    all_to_all x1, blocking collectives: 44.2 us -> 35.1 us  [to_all(): return lax.all_to_all(copies, axes, split_axis=0, concat_axis=0, tiled=True)]
    ppermute x1, starting transfers between devices: 9.92 us -> 16.3 us  [body(): taken = lax.ppermute(given, 'core', [(0, 1), (1, 0)])]
    ppermute x1, starting transfers between devices: 7.87 us -> 4.42 us  [attend(): taken = lax.ppermute(given, 'y', [(0, 1), (1, 0), (2, 3), (3, 2)])]
where the time goes in v9:
time: 170 us; the launch traced here: 169 us
  blocking collectives  109 us (64%)
  starting transfers between devices  24.9 us (15%)
  between operations  14.8 us (9%)
  Pallas kernels  13.7 us (8%)
  waiting for transfers between devices  5.27 us (3%)
    all_gather x1, blocking collectives, attend(): packed = lax.all_gather(packed, 'zh', axis=0, tiled=True)  42.3 us
    all_to_all x1, blocking collectives, to_all(): return lax.all_to_all(copies, axes, split_axis=0, concat_axis=0, tiled=True)  35.1 us
    all_gather x1, blocking collectives, attend(): packed = lax.all_gather(packed, ('z1', 'z0'), axis=0, tiled=True)  18.4 us
    ppermute x1, starting transfers between devices, body(): taken = lax.ppermute(given, 'core', [(0, 1), (1, 0)])  16.3 us
    all_to_all x1, blocking collectives, body(): lax.all_to_all(part, ('x', 'y'), split_axis=0, concat_axis=0, tiled=True)  13 us
    pallas_call x1, Pallas kernels, project(): pl.pallas_call(project_kernel, grid=(4,), in_specs=[pl.BlockSpec((1, 2, r...  6.47 us
    ppermute x1, starting transfers between devices, attend(): taken = lax.ppermute(given, 'y', [(0, 1), (1, 0), (2, 3), (3, 2)])  4.42 us
    all_to_all x1, starting transfers between devices, attend(): heads = lax.all_to_all(heads, 'y', split_axis=0, concat_axis=0, tiled=True)  4.18 us
  transfers between devices with their start and end apart: 4, of which 2 were waited for; matrix products, arithmetic and copies ran while one was open for 0% of the time, Pallas kernels for 2%

profile of v9, /device:TPU:1, one launch (start us, length us, event | category | flops | bytes accessed | tf_op | source)
XLA Modules:
  0.0 169.3 jit_solution(17991794022686318663)
XLA Ops:
  6.5 0.0 copy-start
  6.5 0.0 copy-start.1
  6.5 0.0 copy-start.2
  6.5 0.0 all-gather.2.cloned.1.call-start
  7.2 2.6 %shard_map.112 = (bf16[144,128]{1,0:T(8,128)(2,1)S(1)}, bf16[32,2048]{1,0:T(8,128)(2,1)}, s32[1]{0:T(128)}) custom-call(f32[1]{0:T(128)S(6)} %copy.17.gate_ref, s32[8]{0:T(128)} %length_ref.1, bf16[1,8,4,64,128]{4,3,2,1,0:T(8,128)(2,1)} %query_ref.1, bf16[1,8,4,64,128]{4,3,2,1,0:T(8,128)(2,1)} %out_ref.1, bf16[1,8,4,64,128]{4,3,2,1,0:T(8,128)(2,1)} %cot_ref.1, ...), custom_call_target="tpu_custom_call" | custom-call | flops 65536 | bytes 262144 | tf_op jit(solution)/shard_map/pallas_call | solution.py:108
  9.8 0.0 all-gather.2.cloned.1.call-update
  10.5 0.0 copy-done
  10.5 0.0 copy-done.1
  10.5 0.0 copy-done.2
  10.5 76.7 %conditional.1 = (bf16[104,1024]{1,0:T(8,128)(2,1)S(1)}) conditional(s32[]{:T(128)} %bitcast.5, () %tuple.17, (bf16[144,128]{1,0:T(8,128)(2,1)S(1)}, bf16[1,52,1024]{2,1,0:T(8,128)(2,1)S(1)}, bf16[1,52,1024]{2,1,0:T(8,128)(2,1)S(1)}, s32[8]{0:T(128)S(1)}, s32[]{:T(128)}) %tuple.25), branch_computations={%region_0.1_spmd, %region_1.2_spmd} | conditional | flops 218529792 | bytes 6979445 | solution.py:304
  10.5 42.3 %all_gather.6 = bf16[576,128]{1,0:T(8,128)(2,1)S(1)} all-gather(bf16[144,128]{1,0:T(8,128)(2,1)S(1)} %get-tuple-element.42), channel_id=1, replica_groups=mesh['core'=2,'x'=4,'zb'=2,'z1'=2,'z0'=2,'zh'=4,'y'=4] {'zh'}, dimensions={0}, use_global_device_ids=true | all-gather | bytes 184320 | tf_op jit(solution)/shard_map/cond/branch_1_fun/all_gather | solution.py:291
  52.9 0.9 branch_1_fun.2
  53.7 4.2 %all-to-all-start = ((bf16[4,52,1024]{2,1,0:T(8,128)(2,1)}), bf16[4,52,1024]{2,1,0:T(8,128)(2,1)S(1)}, u32[]{:S(2)}, u32[]{:S(2)}) async-start(bf16[4,52,1024]{2,1,0:T(8,128)(2,1)} %branch_1_fun.2), calls=%async_computation | async-start | bytes 917504 | tf_op jit(solution)/shard_map/cond/branch_1_fun/all_to_all | solution.py:294
  57.9 18.4 %all_gather.7 = bf16[2304,128]{1,0:T(8,128)(2,1)S(1)} all-gather(bf16[576,128]{1,0:T(8,128)(2,1)S(1)} %all_gather.6), channel_id=1, replica_groups=mesh['core'=2,'x'=4,'zb'=2,'z1'=2,'z0'=2,'zh'=4,'y'=4] {'z1','z0'}, dimensions={0}, use_global_device_ids=true | all-gather | bytes 737280 | tf_op jit(solution)/shard_map/cond/branch_1_fun/all_gather | solution.py:295
  76.3 0.0 all-to-all-done.heads_ref
  76.3 2.8 %branch_1_fun.3 = bf16[208,1024]{1,0:T(8,128)(2,1)S(1)} custom-call(s32[8]{0:T(128)S(1)} %get-tuple-element.64.tiles_ref, bf16[4,4,144,128]{3,2,1,0:T(8,128)(2,1)S(1)} %bitcast.9, bf16[4,52,1024]{2,1,0:T(8,128)(2,1)S(1)} %all-to-all-done.heads_ref), custom_call_target="tpu_custom_call" | custom-call | flops 218103808 | bytes 2097152 | tf_op jit(solution)/shard_map/cond/branch_1_fun/pallas_call | solution.py:184
  79.1 4.4 %collective-permute-start = (bf16[104,1024]{1,0:T(8,128)(2,1)S(1)}, bf16[104,1024]{1,0:T(8,128)(2,1)S(1)}, u32[]{:S(2)}, u32[]{:S(2)}) collective-permute-start(bf16[104,1024]{1,0:T(8,128)(2,1)S(1)} %dynamic-slice_bitcast_fusion), channel_id=1, source_target_pairs={{0,1},{1,0},{2,3},{3,2},{4,5},{5,4},{6,7},{7,6},{8,9},{9,8},{10,11... | collective-permute-start | bytes 638984 | tf_op jit(solution)/shard_map/cond/branch_1_fun/ppermute | solution.py:301
  83.6 3.6 %collective-permute-done = bf16[104,1024]{1,0:T(8,128)(2,1)S(1)} collective-permute-done((bf16[104,1024]{1,0:T(8,128)(2,1)S(1)}, bf16[104,1024]{1,0:T(8,128)(2,1)S(1)}, u32[]{:S(2)}, u32[]{:S(2)}) %collective-permute-start) | collective-permute-done | bytes 213024 | tf_op jit(solution)/shard_map/cond/branch_1_fun/ppermute | solution.py:301
  87.2 0.1 fusion
  87.3 0.4 broadcast_in_dim.2
  87.7 35.1 %all_to_all.14 = bf16[16,104,1024]{2,1,0:T(8,128)(2,1)} all-to-all(bf16[16,104,1024]{2,1,0:T(8,128)(2,1)S(1)} %broadcast_in_dim.2), channel_id=1, replica_groups=mesh['core'=2,'x'=4,'zb'=2,'z1'=2,'z0'=2,'zh'=4,'y'=4] {'x','y'}, dimensions={0} | all-to-all | bytes 6815744 | tf_op jit(solution)/shard_map/all_to_all | solution.py:268
  122.7 0.0 all-gather.2.cloned.1.call-done.weight_ref
  122.7 6.5 %shard_map.113 = (f32[16,56,256]{2,1,0:T(8,128)}, bf16[16,56,256]{2,1,0:T(8,128)(2,1)}) custom-call(bf16[4,2,208,1024]{3,2,1,0:T(8,128)(2,1)} %bitcast.12, bf16[512,2048]{1,0:T(8,128)(2,1)} %all-gather.2.cloned.1.call-done.weight_ref), custom_call_target="tpu_custom_call" | custom-call | flops 1744830464 | bytes 7340032 | tf_op jit(solution)/shard_map/pallas_call | solution.py:229
  129.2 16.3 %collective-permute-start.1 = (bf16[16,56,256]{2,1,0:T(8,128)(2,1)}, bf16[16,56,256]{2,1,0:T(8,128)(2,1)S(1)}, u32[]{:S(2)}, u32[]{:S(2)}) collective-permute-start(bf16[16,56,256]{2,1,0:T(8,128)(2,1)} %get-tuple-element.58), channel_id=1, source_target_pairs={{0,512},{512,0},{1,513},{513,1},{2,514},{514,2},{3,515},{515,3},{4... | collective-permute-start | bytes 1376264 | tf_op jit(solution)/shard_map/ppermute | solution.py:313
  145.5 1.6 collective-permute-done.1
  147.2 1.3 add_convert_fusion
  148.4 13.0 %all_to_all.15.part_ref = bf16[16,56,256]{2,1,0:T(8,128)(2,1)S(1)} all-to-all(bf16[16,56,256]{2,1,0:T(8,128)(2,1)S(1)} %add_convert_fusion), channel_id=1, replica_groups=mesh['core'=2,'x'=4,'zb'=2,'z1'=2,'z0'=2,'zh'=4,'y'=4] {'x','y'}, dimensions={0} | all-to-all | bytes 917504 | tf_op jit(solution)/shard_map/all_to_all | solution.py:315
  161.5 1.0 shard_map.114
  (1 shorter events, 0.0 us)
Async XLA Ops:
  6.5 4.0 %copy-start = (bf16[1,52,1024]{2,1,0:T(8,128)(2,1)S(1)}, bf16[1,52,1024]{2,1,0:T(8,128)(2,1)}, u32[]{:S(2)}) copy-start(bf16[1,52,1024]{2,1,0:T(8,128)(2,1)} %param.17) | copy-start | bytes 319492
  6.5 4.0 %copy-start.1 = (bf16[1,52,1024]{2,1,0:T(8,128)(2,1)S(1)}, bf16[1,52,1024]{2,1,0:T(8,128)(2,1)}, u32[]{:S(2)}) copy-start(bf16[1,52,1024]{2,1,0:T(8,128)(2,1)} %param.18) | copy-start | bytes 319492
  6.5 4.0 %copy-start.2 = (s32[8]{0:T(128)S(1)}, s32[8]{0:T(128)}, u32[]{:S(2)}) copy-start(s32[8]{0:T(128)} %param.22) | copy-start | bytes 100
  6.5 116.2 %all-gather.2.cloned.1.call-start = ((), (), s32[]{:S(2)}) async-start(), calls=%async_computation.3 | async-start | bytes 2228224 | tf_op jit(solution)/shard_map/all_gather | solution.py:287
  53.7 22.6 %all-to-all-start = ((bf16[4,52,1024]{2,1,0:T(8,128)(2,1)}), bf16[4,52,1024]{2,1,0:T(8,128)(2,1)S(1)}, u32[]{:S(2)}, u32[]{:S(2)}) async-start(bf16[4,52,1024]{2,1,0:T(8,128)(2,1)} %branch_1_fun.2), calls=%async_computation | async-start | bytes 917504 | tf_op jit(solution)/shard_map/cond/branch_1_fun/all_to_all | solution.py:294
  79.1 8.0 %collective-permute-start = (bf16[104,1024]{1,0:T(8,128)(2,1)S(1)}, bf16[104,1024]{1,0:T(8,128)(2,1)S(1)}, u32[]{:S(2)}, u32[]{:S(2)}) collective-permute-start(bf16[104,1024]{1,0:T(8,128)(2,1)S(1)} %dynamic-slice_bitcast_fusion), channel_id=1, source_target_pairs={{0,1},{1,0},{2,3},{3,2},{4,5},{5,4},{6,7},{7,6},{8,9},{9,8},{10,11... | collective-permute-start | bytes 638984 | tf_op jit(solution)/shard_map/cond/branch_1_fun/ppermute | solution.py:301
  129.2 17.9 %collective-permute-start.1 = (bf16[16,56,256]{2,1,0:T(8,128)(2,1)}, bf16[16,56,256]{2,1,0:T(8,128)(2,1)S(1)}, u32[]{:S(2)}, u32[]{:S(2)}) collective-permute-start(bf16[16,56,256]{2,1,0:T(8,128)(2,1)} %get-tuple-element.58), channel_id=1, source_target_pairs={{0,512},{512,0},{1,513},{513,1},{2,514},{514,2},{3,515},{515,3},{4... | collective-permute-start | bytes 1376264 | tf_op jit(solution)/shard_map/ppermute | solution.py:313
Sparse Core Ops, SparseCore 0:
  10.0 109.5 all-gather.1

commit v10 on v9

--- a/solution.py
+++ b/solution.py
@@ -204,7 +204,7 @@
     wide = KVH * HD
     total = sum(
         lax.dot_general(
-            grads_ref[0, p],
+            jnp.concatenate([grads_ref[x, p] for x in range(2)], axis=0),
             weight_ref[:, p * wide : (p + 1) * wide],
             NT,
             preferred_element_type=jnp.float32,
@@ -216,21 +216,21 @@
     kept = jnp.where(first, low, high)
     given = jnp.where(first, high, low)
     below = jnp.zeros((PADDED - ROWS, 256), jnp.float32)
-    for y in range(4):
-        rows = slice(y * ROWS, (y + 1) * ROWS)
-        kept_ref[y] = jnp.concatenate([kept[rows], below], axis=0)
-        given_ref[y] = jnp.concatenate([given[rows], below], axis=0).astype(jnp.bfloat16)
+    for i in range(8):
+        rows = slice(i * ROWS, (i + 1) * ROWS)
+        kept_ref[i] = jnp.concatenate([kept[rows], below], axis=0)
+        given_ref[i] = jnp.concatenate([given[rows], below], axis=0).astype(jnp.bfloat16)
 
 
 def project(grads, weight):
     features, depth = weight.shape
     rows = 4 * ROWS
-    half = pl.BlockSpec((4, PADDED, features // 2), lambda x: (x, 0, 0))
+    half = pl.BlockSpec((8, PADDED, features // 2), lambda x: (x, 0, 0))
     return pl.pallas_call(
         project_kernel,
-        grid=(4,),
+        grid=(2,),
         in_specs=[
-            pl.BlockSpec((1, 2, rows, depth // 2), lambda x: (x, 0, 0, 0)),
+            pl.BlockSpec((2, 2, rows, depth // 2), lambda x: (x, 0, 0, 0)),
             pl.BlockSpec((features, depth), lambda x: (0, 0)),
         ],
         out_specs=[half, half],

time: 170 us -> 168 us (0.988)
  no operation moved by 1% of the time
where the time goes in v10:
time: 168 us
  blocking collectives  109 us (65%)
  starting transfers between devices  24.9 us (15%)
  between operations  14.8 us (9%)
  Pallas kernels  12.4 us (7%)
  waiting for transfers between devices  5.27 us (3%)
    all_gather x1, blocking collectives, attend(): packed = lax.all_gather(packed, 'zh', axis=0, tiled=True)  42.3 us
    all_to_all x1, blocking collectives, to_all(): return lax.all_to_all(copies, axes, split_axis=0, concat_axis=0, tiled=True)  35.1 us
    all_gather x1, blocking collectives, attend(): packed = lax.all_gather(packed, ('z1', 'z0'), axis=0, tiled=True)  18.4 us
    ppermute x1, starting transfers between devices, body(): taken = lax.ppermute(given, 'core', [(0, 1), (1, 0)])  16.3 us
    all_to_all x1, blocking collectives, body(): lax.all_to_all(part, ('x', 'y'), split_axis=0, concat_axis=0, tiled=True)  13 us
    pallas_call x1, Pallas kernels, project(): pl.pallas_call(project_kernel, grid=(2,), in_specs=[pl.BlockSpec((2, 2, r...  5.14 us
    ppermute x1, starting transfers between devices, attend(): taken = lax.ppermute(given, 'y', [(0, 1), (1, 0), (2, 3), (3, 2)])  4.42 us
    all_to_all x1, starting transfers between devices, attend(): heads = lax.all_to_all(heads, 'y', split_axis=0, concat_axis=0, tiled=True)  4.18 us
  transfers between devices with their start and end apart: 4, of which 2 were waited for; matrix products, arithmetic and copies ran while one was open for 0% of the time, Pallas kernels for 2%

profile of v10, /device:TPU:1, one launch (start us, length us, event | category | flops | bytes accessed | tf_op | source)
XLA Modules:
  0.0 168.0 jit_solution(129930140480332317)
XLA Ops:
  6.5 0.0 copy-start
  6.5 0.0 copy-start.1
  6.5 0.0 copy-start.2
  6.5 0.0 all-gather.2.cloned.1.call-start
  7.2 2.6 %shard_map.112 = (bf16[144,128]{1,0:T(8,128)(2,1)S(1)}, bf16[32,2048]{1,0:T(8,128)(2,1)}, s32[1]{0:T(128)}) custom-call(f32[1]{0:T(128)S(6)} %copy.17.gate_ref, s32[8]{0:T(128)} %length_ref.1, bf16[1,8,4,64,128]{4,3,2,1,0:T(8,128)(2,1)} %query_ref.1, bf16[1,8,4,64,128]{4,3,2,1,0:T(8,128)(2,1)} %out_ref.1, bf16[1,8,4,64,128]{4,3,2,1,0:T(8,128)(2,1)} %cot_ref.1, ...), custom_call_target="tpu_custom_call" | custom-call | flops 65536 | bytes 262144 | tf_op jit(solution)/shard_map/pallas_call | solution.py:108
  9.8 0.0 all-gather.2.cloned.1.call-update
  10.5 0.0 copy-done
  10.5 0.0 copy-done.1
  10.5 0.0 copy-done.2
  10.5 76.7 %conditional.1 = (bf16[104,1024]{1,0:T(8,128)(2,1)S(1)}) conditional(s32[]{:T(128)} %bitcast.5, () %tuple.17, (bf16[144,128]{1,0:T(8,128)(2,1)S(1)}, bf16[1,52,1024]{2,1,0:T(8,128)(2,1)S(1)}, bf16[1,52,1024]{2,1,0:T(8,128)(2,1)S(1)}, s32[8]{0:T(128)S(1)}, s32[]{:T(128)}) %tuple.25), branch_computations={%region_0.1_spmd, %region_1.2_spmd} | conditional | flops 218529792 | bytes 6979445 | solution.py:304
  10.5 42.3 %all_gather.6 = bf16[576,128]{1,0:T(8,128)(2,1)S(1)} all-gather(bf16[144,128]{1,0:T(8,128)(2,1)S(1)} %get-tuple-element.42), channel_id=1, replica_groups=mesh['core'=2,'x'=4,'zb'=2,'z1'=2,'z0'=2,'zh'=4,'y'=4] {'zh'}, dimensions={0}, use_global_device_ids=true | all-gather | bytes 184320 | tf_op jit(solution)/shard_map/cond/branch_1_fun/all_gather | solution.py:291
  52.9 0.9 branch_1_fun.2
  53.7 4.2 %all-to-all-start = ((bf16[4,52,1024]{2,1,0:T(8,128)(2,1)}), bf16[4,52,1024]{2,1,0:T(8,128)(2,1)S(1)}, u32[]{:S(2)}, u32[]{:S(2)}) async-start(bf16[4,52,1024]{2,1,0:T(8,128)(2,1)} %branch_1_fun.2), calls=%async_computation | async-start | bytes 917504 | tf_op jit(solution)/shard_map/cond/branch_1_fun/all_to_all | solution.py:294
  57.9 18.4 %all_gather.7 = bf16[2304,128]{1,0:T(8,128)(2,1)S(1)} all-gather(bf16[576,128]{1,0:T(8,128)(2,1)S(1)} %all_gather.6), channel_id=1, replica_groups=mesh['core'=2,'x'=4,'zb'=2,'z1'=2,'z0'=2,'zh'=4,'y'=4] {'z1','z0'}, dimensions={0}, use_global_device_ids=true | all-gather | bytes 737280 | tf_op jit(solution)/shard_map/cond/branch_1_fun/all_gather | solution.py:295
  76.3 0.0 all-to-all-done.heads_ref
  76.3 2.8 %branch_1_fun.3 = bf16[208,1024]{1,0:T(8,128)(2,1)S(1)} custom-call(s32[8]{0:T(128)S(1)} %get-tuple-element.64.tiles_ref, bf16[4,4,144,128]{3,2,1,0:T(8,128)(2,1)S(1)} %bitcast.9, bf16[4,52,1024]{2,1,0:T(8,128)(2,1)S(1)} %all-to-all-done.heads_ref), custom_call_target="tpu_custom_call" | custom-call | flops 218103808 | bytes 2097152 | tf_op jit(solution)/shard_map/cond/branch_1_fun/pallas_call | solution.py:184
  79.1 4.4 %collective-permute-start = (bf16[104,1024]{1,0:T(8,128)(2,1)S(1)}, bf16[104,1024]{1,0:T(8,128)(2,1)S(1)}, u32[]{:S(2)}, u32[]{:S(2)}) collective-permute-start(bf16[104,1024]{1,0:T(8,128)(2,1)S(1)} %dynamic-slice_bitcast_fusion), channel_id=1, source_target_pairs={{0,1},{1,0},{2,3},{3,2},{4,5},{5,4},{6,7},{7,6},{8,9},{9,8},{10,11... | collective-permute-start | bytes 638984 | tf_op jit(solution)/shard_map/cond/branch_1_fun/ppermute | solution.py:301
  83.6 3.6 %collective-permute-done = bf16[104,1024]{1,0:T(8,128)(2,1)S(1)} collective-permute-done((bf16[104,1024]{1,0:T(8,128)(2,1)S(1)}, bf16[104,1024]{1,0:T(8,128)(2,1)S(1)}, u32[]{:S(2)}, u32[]{:S(2)}) %collective-permute-start) | collective-permute-done | bytes 213024 | tf_op jit(solution)/shard_map/cond/branch_1_fun/ppermute | solution.py:301
  87.2 0.1 fusion
  87.3 0.4 broadcast_in_dim.2
  87.7 35.1 %all_to_all.14 = bf16[16,104,1024]{2,1,0:T(8,128)(2,1)} all-to-all(bf16[16,104,1024]{2,1,0:T(8,128)(2,1)S(1)} %broadcast_in_dim.2), channel_id=1, replica_groups=mesh['core'=2,'x'=4,'zb'=2,'z1'=2,'z0'=2,'zh'=4,'y'=4] {'x','y'}, dimensions={0} | all-to-all | bytes 6815744 | tf_op jit(solution)/shard_map/all_to_all | solution.py:268
  122.7 0.0 all-gather.2.cloned.1.call-done.weight_ref
  122.7 5.1 %shard_map.113 = (f32[16,56,256]{2,1,0:T(8,128)}, bf16[16,56,256]{2,1,0:T(8,128)(2,1)}) custom-call(bf16[4,2,208,1024]{3,2,1,0:T(8,128)(2,1)} %bitcast.12, bf16[512,2048]{1,0:T(8,128)(2,1)} %all-gather.2.cloned.1.call-done.weight_ref), custom_call_target="tpu_custom_call" | custom-call | flops 1744830464 | bytes 7340032 | tf_op jit(solution)/shard_map/pallas_call | solution.py:229
  127.9 16.3 %collective-permute-start.1 = (bf16[16,56,256]{2,1,0:T(8,128)(2,1)}, bf16[16,56,256]{2,1,0:T(8,128)(2,1)S(1)}, u32[]{:S(2)}, u32[]{:S(2)}) collective-permute-start(bf16[16,56,256]{2,1,0:T(8,128)(2,1)} %get-tuple-element.58), channel_id=1, source_target_pairs={{0,512},{512,0},{1,513},{513,1},{2,514},{514,2},{3,515},{515,3},{4... | collective-permute-start | bytes 1376264 | tf_op jit(solution)/shard_map/ppermute | solution.py:313
  144.2 1.6 collective-permute-done.1
  145.8 1.3 add_convert_fusion
  147.1 13.0 %all_to_all.15.part_ref = bf16[16,56,256]{2,1,0:T(8,128)(2,1)S(1)} all-to-all(bf16[16,56,256]{2,1,0:T(8,128)(2,1)S(1)} %add_convert_fusion), channel_id=1, replica_groups=mesh['core'=2,'x'=4,'zb'=2,'z1'=2,'z0'=2,'zh'=4,'y'=4] {'x','y'}, dimensions={0} | all-to-all | bytes 917504 | tf_op jit(solution)/shard_map/all_to_all | solution.py:315
  160.1 1.0 shard_map.114
  (1 shorter events, 0.0 us)
Async XLA Ops:
  6.5 4.0 %copy-start = (bf16[1,52,1024]{2,1,0:T(8,128)(2,1)S(1)}, bf16[1,52,1024]{2,1,0:T(8,128)(2,1)}, u32[]{:S(2)}) copy-start(bf16[1,52,1024]{2,1,0:T(8,128)(2,1)} %param.17) | copy-start | bytes 319492
  6.5 4.0 %copy-start.1 = (bf16[1,52,1024]{2,1,0:T(8,128)(2,1)S(1)}, bf16[1,52,1024]{2,1,0:T(8,128)(2,1)}, u32[]{:S(2)}) copy-start(bf16[1,52,1024]{2,1,0:T(8,128)(2,1)} %param.18) | copy-start | bytes 319492
  6.5 4.0 %copy-start.2 = (s32[8]{0:T(128)S(1)}, s32[8]{0:T(128)}, u32[]{:S(2)}) copy-start(s32[8]{0:T(128)} %param.22) | copy-start | bytes 100
  6.5 116.2 %all-gather.2.cloned.1.call-start = ((), (), s32[]{:S(2)}) async-start(), calls=%async_computation.3 | async-start | bytes 2228224 | tf_op jit(solution)/shard_map/all_gather | solution.py:287
  53.7 22.6 %all-to-all-start = ((bf16[4,52,1024]{2,1,0:T(8,128)(2,1)}), bf16[4,52,1024]{2,1,0:T(8,128)(2,1)S(1)}, u32[]{:S(2)}, u32[]{:S(2)}) async-start(bf16[4,52,1024]{2,1,0:T(8,128)(2,1)} %branch_1_fun.2), calls=%async_computation | async-start | bytes 917504 | tf_op jit(solution)/shard_map/cond/branch_1_fun/all_to_all | solution.py:294
  79.1 8.0 %collective-permute-start = (bf16[104,1024]{1,0:T(8,128)(2,1)S(1)}, bf16[104,1024]{1,0:T(8,128)(2,1)S(1)}, u32[]{:S(2)}, u32[]{:S(2)}) collective-permute-start(bf16[104,1024]{1,0:T(8,128)(2,1)S(1)} %dynamic-slice_bitcast_fusion), channel_id=1, source_target_pairs={{0,1},{1,0},{2,3},{3,2},{4,5},{5,4},{6,7},{7,6},{8,9},{9,8},{10,11... | collective-permute-start | bytes 638984 | tf_op jit(solution)/shard_map/cond/branch_1_fun/ppermute | solution.py:301
  127.9 17.9 %collective-permute-start.1 = (bf16[16,56,256]{2,1,0:T(8,128)(2,1)}, bf16[16,56,256]{2,1,0:T(8,128)(2,1)S(1)}, u32[]{:S(2)}, u32[]{:S(2)}) collective-permute-start(bf16[16,56,256]{2,1,0:T(8,128)(2,1)} %get-tuple-element.58), channel_id=1, source_target_pairs={{0,512},{512,0},{1,513},{513,1},{2,514},{514,2},{3,515},{515,3},{4... | collective-permute-start | bytes 1376264 | tf_op jit(solution)/shard_map/ppermute | solution.py:313
Sparse Core Ops, SparseCore 0:
  10.0 109.5 all-gather.1

commit v11 on v10

--- a/solution.py
+++ b/solution.py
@@ -138,7 +138,7 @@
     )(keys, values)
 
 
-def attention_kernel(tiles_ref, pack_ref, heads_ref, out_ref):
+def attention_kernel(half_ref, tiles_ref, pack_ref, heads_ref, out_ref):
     x, zb, z1, z0, zh = (lax.axis_index(name) for name in ("x", "zb", "z1", "z0", "zh"))
     tiles = tiles_ref[x * 2 + zb]
     query = pack_ref[:, 0, 0:TXT, :].reshape(GROUP, HD)
@@ -153,9 +153,9 @@
         )
 
     norm, delta = line(0), line(1)
-    line_rows = 4 * ROWS
+    line_rows = 2 * ROWS
     wide_row = lax.broadcasted_iota(jnp.int32, (line_rows, GROUP), 0)
-    position = ((z1 * 2 + z0) * 16 + zh * 4) * ROWS + wide_row
+    position = ((z1 * 2 + z0) * 16 + zh * 4 + 2 * half_ref[0]) * ROWS + wide_row
     second = position >= TILE_PAD
     inside = jnp.where(second, position - TILE_PAD, position) < TILE_LEN
     present = jnp.where(second, 1, 0) < tiles
@@ -163,7 +163,7 @@
 
     def lines(block):
         wide = block.astype(jnp.float32)
-        return jnp.concatenate([wide[i] for i in range(4)], axis=0).astype(jnp.bfloat16)
+        return jnp.concatenate([wide[0], wide[1]], axis=0).astype(jnp.bfloat16)
 
     keys = lines(heads_ref[:, :, 0:HD])
     values = lines(heads_ref[:, :, HD : 2 * HD])
@@ -179,25 +179,27 @@
     out_ref[:, HD : 2 * HD] = value_grad.astype(jnp.bfloat16)
 
 
-def attention_grads(tiles, packed, heads):
-    piece = pl.BlockSpec((4, ROWS, 2 * HD), lambda s: (0, 0, s))
+def attention_grads(half, tiles, packed, heads):
     return pl.pallas_call(
         attention_kernel,
-        grid=(4,),
-        in_specs=[
-            pl.BlockSpec(memory_space=pltpu.SMEM),
-            pl.BlockSpec((4, 1, PACK, HD), lambda s: (0, s, 0, 0)),
-            piece,
-        ],
-        out_specs=pl.BlockSpec((4 * ROWS, 2 * HD), lambda s: (0, s)),
-        out_shape=jax.ShapeDtypeStruct((4 * ROWS, KVH * HD), jnp.bfloat16),
+        grid_spec=pltpu.PrefetchScalarGridSpec(
+            num_scalar_prefetch=1,
+            grid=(4,),
+            in_specs=[
+                pl.BlockSpec(memory_space=pltpu.SMEM),
+                pl.BlockSpec((4, 1, PACK, HD), lambda s, half: (0, s, 0, 0)),
+                pl.BlockSpec((2, ROWS, 2 * HD), lambda s, half: (half[0], 0, s)),
+            ],
+            out_specs=pl.BlockSpec((2 * ROWS, 2 * HD), lambda s, half: (0, s)),
+        ),
+        out_shape=jax.ShapeDtypeStruct((2 * ROWS, KVH * HD), jnp.bfloat16),
         compiler_params=pltpu.CompilerParams(vmem_limit_bytes=VMEM_LIMIT),
         cost_estimate=pl.CostEstimate(
-            flops=8 * 4 * ROWS * 4 * GROUP * HD,
+            flops=8 * 2 * ROWS * 4 * GROUP * HD,
             bytes_accessed=2 << 20,
-            transcendentals=4 * ROWS * 4 * GROUP,
+            transcendentals=2 * ROWS * 4 * GROUP,
         ),
-    )(tiles, packed, heads)
+    )(half.reshape(1), tiles, packed, heads)
 
 
 def project_kernel(grads_ref, weight_ref, kept_ref, given_ref):
@@ -285,7 +287,7 @@
         layer_gate, text_lens, text_query, attn_out, grad_out, log_norm, k_weight, v_weight
     )
     weight = lax.all_gather(weight, ("zh", "zb", "z1"), axis=0, tiled=True)
-    own = lax.axis_index("y") % 2
+    own = (lax.axis_index("y") % 2).astype(jnp.int32)
 
     def attend(packed):
         packed = lax.all_gather(packed, "zh", axis=0, tiled=True)
@@ -294,11 +296,9 @@
         heads = lax.all_to_all(heads, "y", split_axis=0, concat_axis=0, tiled=True)
         packed = lax.all_gather(packed, ("z1", "z0"), axis=0, tiled=True)
         packed = packed.reshape(4, 4, PACK, HD)
-        part = attention_grads(tile_counts, packed, heads)
-        part = part.reshape(2, 2 * ROWS, KVH * HD)
-        kept = lax.dynamic_index_in_dim(part, own, 0, keepdims=False)
-        given = lax.dynamic_index_in_dim(part, 1 - own, 0, keepdims=False)
+        given = attention_grads(1 - own, tile_counts, packed, heads)
         taken = lax.ppermute(given, "y", [(0, 1), (1, 0), (2, 3), (3, 2)])
+        kept = attention_grads(own, tile_counts, packed, heads)
         return (kept.astype(jnp.float32) + taken.astype(jnp.float32)).astype(jnp.bfloat16)
 
     grads = lax.cond(

time: 168 us -> 168 us (level)
  waiting for transfers between devices: 5.27 us -> 2.65 us
  Pallas kernels: 12.4 us -> 14.8 us
    ppermute x1, waiting for transfers between devices: 3.61 us -> 1 us  [attend(): taken = lax.ppermute(given, 'y', [(0, 1), (1, 0), (2, 3), (3, 2)])]
    pallas_call x1 -> x2, Pallas kernels: 2.8 us -> 5.2 us  [attention_grads(): pl.pallas_call(attention_kernel, grid_spec=pltpu.PrefetchScalarGridSpec(n...]
  transfers between devices with their start and end apart: 4 -> 4, of which waited for: 2 -> 2; matrix products, arithmetic and copies ran while one was open for 0% -> 0% of each run, Pallas kernels for 2% -> 4%
where the time goes in v11:
time: 168 us
  blocking collectives  109 us (65%)
  starting transfers between devices  24.9 us (15%)
  Pallas kernels  14.8 us (9%)
  between operations  14.8 us (9%)
  waiting for transfers between devices  2.65 us (2%)
    all_gather x1, blocking collectives, attend(): packed = lax.all_gather(packed, 'zh', axis=0, tiled=True)  42.3 us
    all_to_all x1, blocking collectives, to_all(): return lax.all_to_all(copies, axes, split_axis=0, concat_axis=0, tiled=True)  35.1 us
    all_gather x1, blocking collectives, attend(): packed = lax.all_gather(packed, ('z1', 'z0'), axis=0, tiled=True)  18.4 us
    ppermute x1, starting transfers between devices, body(): taken = lax.ppermute(given, 'core', [(0, 1), (1, 0)])  16.3 us
    all_to_all x1, blocking collectives, body(): lax.all_to_all(part, ('x', 'y'), split_axis=0, concat_axis=0, tiled=True)  13 us
    pallas_call x2, Pallas kernels, attention_grads(): pl.pallas_call(attention_kernel, grid_spec=pltpu.PrefetchScalarGridSpec(n...  5.2 us
    pallas_call x1, Pallas kernels, project(): pl.pallas_call(project_kernel, grid=(2,), in_specs=[pl.BlockSpec((2, 2, r...  5.14 us
    ppermute x1, starting transfers between devices, attend(): taken = lax.ppermute(given, 'y', [(0, 1), (1, 0), (2, 3), (3, 2)])  4.42 us
  transfers between devices with their start and end apart: 4, of which 2 were waited for; matrix products, arithmetic and copies ran while one was open for 0% of the time, Pallas kernels for 4%

profile of v11, /device:TPU:1, one launch (start us, length us, event | category | flops | bytes accessed | tf_op | source)
XLA Modules:
  0.0 167.7 jit_solution(4204986608908112128)
XLA Ops:
  6.5 0.0 copy-start
  6.5 0.0 copy-start.1
  6.5 0.0 copy-start.2
  6.5 0.0 all-gather.2.cloned.1.call-start
  7.2 2.6 %shard_map.112 = (bf16[144,128]{1,0:T(8,128)(2,1)S(1)}, bf16[32,2048]{1,0:T(8,128)(2,1)}, s32[1]{0:T(128)}) custom-call(f32[1]{0:T(128)S(6)} %copy.17.gate_ref, s32[8]{0:T(128)} %length_ref.1, bf16[1,8,4,64,128]{4,3,2,1,0:T(8,128)(2,1)} %query_ref.1, bf16[1,8,4,64,128]{4,3,2,1,0:T(8,128)(2,1)} %out_ref.1, bf16[1,8,4,64,128]{4,3,2,1,0:T(8,128)(2,1)} %cot_ref.1, ...), custom_call_target="tpu_custom_call" | custom-call | flops 65536 | bytes 262144 | tf_op jit(solution)/shard_map/pallas_call | solution.py:108
  9.8 0.0 all-gather.2.cloned.1.call-update
  10.5 0.0 copy-done
  10.5 0.0 copy-done.1
  10.5 0.0 copy-done.2
  10.5 76.5 %conditional.1 = (bf16[104,1024]{1,0:T(8,128)(2,1)S(1)}) conditional(s32[]{:T(128)} %bitcast.3, () %tuple.17, (s32[]{:T(128)}, bf16[144,128]{1,0:T(8,128)(2,1)S(1)}, bf16[1,52,1024]{2,1,0:T(8,128)(2,1)S(1)}, bf16[1,52,1024]{2,1,0:T(8,128)(2,1)S(1)}, s32[8]{0:T(128)S(1)}) %tuple.25), branch_computations={%region_0.1_spmd, %region_1.2_spmd} | conditional | flops 218529808 | bytes 8650537 | solution.py:304
  10.5 42.3 %all_gather.6 = bf16[576,128]{1,0:T(8,128)(2,1)S(1)} all-gather(bf16[144,128]{1,0:T(8,128)(2,1)S(1)} %get-tuple-element.43), channel_id=1, replica_groups=mesh['core'=2,'x'=4,'zb'=2,'z1'=2,'z0'=2,'zh'=4,'y'=4] {'zh'}, dimensions={0}, use_global_device_ids=true | all-gather | bytes 184320 | tf_op jit(solution)/shard_map/cond/branch_1_fun/all_gather | solution.py:293
  52.9 0.9 branch_1_fun.3
  53.7 4.2 %all-to-all-start = ((bf16[4,52,1024]{2,1,0:T(8,128)(2,1)}), bf16[4,52,1024]{2,1,0:T(8,128)(2,1)S(1)}, u32[]{:S(2)}, u32[]{:S(2)}) async-start(bf16[4,52,1024]{2,1,0:T(8,128)(2,1)} %branch_1_fun.3), calls=%async_computation | async-start | bytes 917504 | tf_op jit(solution)/shard_map/cond/branch_1_fun/all_to_all | solution.py:296
  57.9 18.4 %all_gather.7 = bf16[2304,128]{1,0:T(8,128)(2,1)S(1)} all-gather(bf16[576,128]{1,0:T(8,128)(2,1)S(1)} %all_gather.6), channel_id=1, replica_groups=mesh['core'=2,'x'=4,'zb'=2,'z1'=2,'z0'=2,'zh'=4,'y'=4] {'z1','z0'}, dimensions={0}, use_global_device_ids=true | all-gather | bytes 737280 | tf_op jit(solution)/shard_map/cond/branch_1_fun/all_gather | solution.py:297
  76.3 0.0 all-to-all-done.heads_ref
  76.3 2.6 %branch_1_fun.5 = bf16[104,1024]{1,0:T(8,128)(2,1)S(1)} custom-call(s32[1]{0:T(128)} %bitcast.2.half_ref, s32[8]{0:T(128)S(1)} %get-tuple-element.64.tiles_ref, bf16[4,4,144,128]{3,2,1,0:T(8,128)(2,1)S(1)} %bitcast.5, bf16[4,52,1024]{2,1,0:T(8,128)(2,1)S(1)} %all-to-all-done.heads_ref), custom_call_target="tpu_custom_call" | custom-call | flops 109051904 | bytes 2097152 | tf_op jit(solution)/shard_map/cond/branch_1_fun/pallas_call | solution.py:183
  78.9 4.4 %collective-permute-start = (bf16[104,1024]{1,0:T(8,128)(2,1)S(1)}, bf16[104,1024]{1,0:T(8,128)(2,1)S(1)}, u32[]{:S(2)}, u32[]{:S(2)}) collective-permute-start(bf16[104,1024]{1,0:T(8,128)(2,1)S(1)} %branch_1_fun.5), channel_id=1, source_target_pairs={{0,1},{1,0},{2,3},{3,2},{4,5},{5,4},{6,7},{7,6},{8,9},{9,8},{10,11... | collective-permute-start | bytes 638984 | tf_op jit(solution)/shard_map/cond/branch_1_fun/ppermute | solution.py:300
  83.3 2.6 %branch_1_fun.4 = bf16[104,1024]{1,0:T(8,128)(2,1)S(1)} custom-call(s32[1]{0:T(128)} %bitcast.half_ref, s32[8]{0:T(128)S(1)} %get-tuple-element.64.tiles_ref, bf16[4,4,144,128]{3,2,1,0:T(8,128)(2,1)S(1)} %bitcast.6, bf16[4,52,1024]{2,1,0:T(8,128)(2,1)S(1)} %all-to-all-done.heads_ref), custom_call_target="tpu_custom_call" | custom-call | flops 109051904 | bytes 2097152 | tf_op jit(solution)/shard_map/cond/branch_1_fun/pallas_call | solution.py:183
  86.0 1.0 collective-permute-done
  87.0 0.1 add_convert_fusion
  87.0 0.4 broadcast_in_dim.2
  87.4 35.1 %all_to_all.14 = bf16[16,104,1024]{2,1,0:T(8,128)(2,1)} all-to-all(bf16[16,104,1024]{2,1,0:T(8,128)(2,1)S(1)} %broadcast_in_dim.2), channel_id=1, replica_groups=mesh['core'=2,'x'=4,'zb'=2,'z1'=2,'z0'=2,'zh'=4,'y'=4] {'x','y'}, dimensions={0} | all-to-all | bytes 6815744 | tf_op jit(solution)/shard_map/all_to_all | solution.py:270
  122.5 0.0 all-gather.2.cloned.1.call-done.weight_ref
  122.5 5.1 %shard_map.113 = (f32[16,56,256]{2,1,0:T(8,128)}, bf16[16,56,256]{2,1,0:T(8,128)(2,1)}) custom-call(bf16[4,2,208,1024]{3,2,1,0:T(8,128)(2,1)} %bitcast.7, bf16[512,2048]{1,0:T(8,128)(2,1)} %all-gather.2.cloned.1.call-done.weight_ref), custom_call_target="tpu_custom_call" | custom-call | flops 1744830464 | bytes 7340032 | tf_op jit(solution)/shard_map/pallas_call | solution.py:231
  127.6 16.3 %collective-permute-start.1 = (bf16[16,56,256]{2,1,0:T(8,128)(2,1)}, bf16[16,56,256]{2,1,0:T(8,128)(2,1)S(1)}, u32[]{:S(2)}, u32[]{:S(2)}) collective-permute-start(bf16[16,56,256]{2,1,0:T(8,128)(2,1)} %get-tuple-element.58), channel_id=1, source_target_pairs={{0,512},{512,0},{1,513},{513,1},{2,514},{514,2},{3,515},{515,3},{4... | collective-permute-start | bytes 1376264 | tf_op jit(solution)/shard_map/ppermute | solution.py:313
  143.9 1.6 collective-permute-done.1
  145.6 1.3 add_convert_fusion.1
  146.9 13.0 %all_to_all.15.part_ref = bf16[16,56,256]{2,1,0:T(8,128)(2,1)S(1)} all-to-all(bf16[16,56,256]{2,1,0:T(8,128)(2,1)S(1)} %add_convert_fusion.1), channel_id=1, replica_groups=mesh['core'=2,'x'=4,'zb'=2,'z1'=2,'z0'=2,'zh'=4,'y'=4] {'x','y'}, dimensions={0} | all-to-all | bytes 917504 | tf_op jit(solution)/shard_map/all_to_all | solution.py:315
  159.9 1.0 shard_map.114
Async XLA Ops:
  6.5 4.0 %copy-start = (bf16[1,52,1024]{2,1,0:T(8,128)(2,1)S(1)}, bf16[1,52,1024]{2,1,0:T(8,128)(2,1)}, u32[]{:S(2)}) copy-start(bf16[1,52,1024]{2,1,0:T(8,128)(2,1)} %param.17) | copy-start | bytes 319492
  6.5 4.0 %copy-start.1 = (bf16[1,52,1024]{2,1,0:T(8,128)(2,1)S(1)}, bf16[1,52,1024]{2,1,0:T(8,128)(2,1)}, u32[]{:S(2)}) copy-start(bf16[1,52,1024]{2,1,0:T(8,128)(2,1)} %param.18) | copy-start | bytes 319492
  6.5 4.0 %copy-start.2 = (s32[8]{0:T(128)S(1)}, s32[8]{0:T(128)}, u32[]{:S(2)}) copy-start(s32[8]{0:T(128)} %param.22) | copy-start | bytes 100
  6.5 116.0 %all-gather.2.cloned.1.call-start = ((), (), s32[]{:S(2)}) async-start(), calls=%async_computation.3 | async-start | bytes 2228224 | tf_op jit(solution)/shard_map/all_gather | solution.py:289
  53.7 22.6 %all-to-all-start = ((bf16[4,52,1024]{2,1,0:T(8,128)(2,1)}), bf16[4,52,1024]{2,1,0:T(8,128)(2,1)S(1)}, u32[]{:S(2)}, u32[]{:S(2)}) async-start(bf16[4,52,1024]{2,1,0:T(8,128)(2,1)} %branch_1_fun.3), calls=%async_computation | async-start | bytes 917504 | tf_op jit(solution)/shard_map/cond/branch_1_fun/all_to_all | solution.py:296
  78.9 8.0 %collective-permute-start = (bf16[104,1024]{1,0:T(8,128)(2,1)S(1)}, bf16[104,1024]{1,0:T(8,128)(2,1)S(1)}, u32[]{:S(2)}, u32[]{:S(2)}) collective-permute-start(bf16[104,1024]{1,0:T(8,128)(2,1)S(1)} %branch_1_fun.5), channel_id=1, source_target_pairs={{0,1},{1,0},{2,3},{3,2},{4,5},{5,4},{6,7},{7,6},{8,9},{9,8},{10,11... | collective-permute-start | bytes 638984 | tf_op jit(solution)/shard_map/cond/branch_1_fun/ppermute | solution.py:300
  127.6 17.9 %collective-permute-start.1 = (bf16[16,56,256]{2,1,0:T(8,128)(2,1)}, bf16[16,56,256]{2,1,0:T(8,128)(2,1)S(1)}, u32[]{:S(2)}, u32[]{:S(2)}) collective-permute-start(bf16[16,56,256]{2,1,0:T(8,128)(2,1)} %get-tuple-element.58), channel_id=1, source_target_pairs={{0,512},{512,0},{1,513},{513,1},{2,514},{514,2},{3,515},{515,3},{4... | collective-permute-start | bytes 1376264 | tf_op jit(solution)/shard_map/ppermute | solution.py:313
Sparse Core Ops, SparseCore 0:
  10.0 108.6 all-gather.1

commit v12 on v11

--- a/solution.py
+++ b/solution.py
@@ -141,19 +141,8 @@
 def attention_kernel(half_ref, tiles_ref, pack_ref, heads_ref, out_ref):
     x, zb, z1, z0, zh = (lax.axis_index(name) for name in ("x", "zb", "z1", "z0", "zh"))
     tiles = tiles_ref[x * 2 + zb]
-    query = pack_ref[:, 0, 0:TXT, :].reshape(GROUP, HD)
-    grad = pack_ref[:, 0, TXT : 2 * TXT, :].reshape(GROUP, HD)
-    meta = pack_ref[:, 0, META : META + 16, :].astype(jnp.float32)
+    line_rows = 2 * ROWS
     left = lax.broadcasted_iota(jnp.int32, (1, HD), 1) < TXT
-
-    def line(which):
-        picked = [meta[i, which : which + 1] for i in range(4)]
-        return jnp.concatenate(
-            [jnp.where(left, picked[i], picked[i + 1]) for i in range(0, 4, 2)], axis=1
-        )
-
-    norm, delta = line(0), line(1)
-    line_rows = 2 * ROWS
     wide_row = lax.broadcasted_iota(jnp.int32, (line_rows, GROUP), 0)
     position = ((z1 * 2 + z0) * 16 + zh * 4 + 2 * half_ref[0]) * ROWS + wide_row
     second = position >= TILE_PAD
@@ -161,22 +150,34 @@
     present = jnp.where(second, 1, 0) < tiles
     mask = jnp.where(inside & present, 1.0, 0.0)
 
-    def lines(block):
-        wide = block.astype(jnp.float32)
-        return jnp.concatenate([wide[0], wide[1]], axis=0).astype(jnp.bfloat16)
-
-    keys = lines(heads_ref[:, :, 0:HD])
-    values = lines(heads_ref[:, :, HD : 2 * HD])
-    scores = lax.dot_general(keys, query, NT, preferred_element_type=jnp.float32) * SCALING
-    attention = jnp.exp(scores - norm) * mask
-    value_grad = lax.dot_general(
-        attention.astype(jnp.bfloat16), grad, NN, preferred_element_type=jnp.float32
-    )
-    probs = lax.dot_general(values, grad, NT, preferred_element_type=jnp.float32)
-    grad_scores = (attention * (probs - delta)).astype(jnp.bfloat16)
-    key_grad = lax.dot_general(grad_scores, query, NN, preferred_element_type=jnp.float32) * SCALING
-    out_ref[:, 0:HD] = key_grad.astype(jnp.bfloat16)
-    out_ref[:, HD : 2 * HD] = value_grad.astype(jnp.bfloat16)
+    for s in range(2):
+        query = pack_ref[:, s, 0:TXT, :].reshape(GROUP, HD)
+        grad = pack_ref[:, s, TXT : 2 * TXT, :].reshape(GROUP, HD)
+        meta = pack_ref[:, s, META : META + 16, :].astype(jnp.float32)
+
+        def line(which):
+            picked = [meta[i, which : which + 1] for i in range(4)]
+            return jnp.concatenate(
+                [jnp.where(left, picked[i], picked[i + 1]) for i in range(0, 4, 2)], axis=1
+            )
+
+        def lines(block):
+            wide = block.astype(jnp.float32)
+            return jnp.concatenate([wide[0], wide[1]], axis=0).astype(jnp.bfloat16)
+
+        key, value = slice(2 * s * HD, (2 * s + 1) * HD), slice((2 * s + 1) * HD, (2 * s + 2) * HD)
+        keys = lines(heads_ref[:, :, key])
+        values = lines(heads_ref[:, :, value])
+        scores = lax.dot_general(keys, query, NT, preferred_element_type=jnp.float32) * SCALING
+        attention = jnp.exp(scores - line(0)) * mask
+        value_grad = lax.dot_general(
+            attention.astype(jnp.bfloat16), grad, NN, preferred_element_type=jnp.float32
+        )
+        probs = lax.dot_general(values, grad, NT, preferred_element_type=jnp.float32)
+        grad_scores = (attention * (probs - line(1))).astype(jnp.bfloat16)
+        key_grad = lax.dot_general(grad_scores, query, NN, preferred_element_type=jnp.float32)
+        out_ref[:, key] = (key_grad * SCALING).astype(jnp.bfloat16)
+        out_ref[:, value] = value_grad.astype(jnp.bfloat16)
 
 
 def attention_grads(half, tiles, packed, heads):
@@ -184,13 +185,13 @@
         attention_kernel,
         grid_spec=pltpu.PrefetchScalarGridSpec(
             num_scalar_prefetch=1,
-            grid=(4,),
+            grid=(2,),
             in_specs=[
                 pl.BlockSpec(memory_space=pltpu.SMEM),
-                pl.BlockSpec((4, 1, PACK, HD), lambda s, half: (0, s, 0, 0)),
-                pl.BlockSpec((2, ROWS, 2 * HD), lambda s, half: (half[0], 0, s)),
+                pl.BlockSpec((4, 2, PACK, HD), lambda s, half: (0, s, 0, 0)),
+                pl.BlockSpec((2, ROWS, 4 * HD), lambda s, half: (half[0], 0, s)),
             ],
-            out_specs=pl.BlockSpec((2 * ROWS, 2 * HD), lambda s, half: (0, s)),
+            out_specs=pl.BlockSpec((2 * ROWS, 4 * HD), lambda s, half: (0, s)),
         ),
         out_shape=jax.ShapeDtypeStruct((2 * ROWS, KVH * HD), jnp.bfloat16),
         compiler_params=pltpu.CompilerParams(vmem_limit_bytes=VMEM_LIMIT),

time: 168 us -> 167 us (level)
  Pallas kernels: 14.8 us -> 13 us
    pallas_call x2, Pallas kernels: 5.2 us -> 3.45 us  [attention_grads(): pl.pallas_call(attention_kernel, grid_spec=pltpu.PrefetchScalarGridSpec(n...]
  transfers between devices with their start and end apart: 4 -> 4, of which waited for: 2 -> 2; matrix products, arithmetic and copies ran while one was open for 0% -> 0% of each run, Pallas kernels for 4% -> 3%
where the time goes in v12:
time: 167 us
  blocking collectives  109 us (65%)
  starting transfers between devices  24.9 us (15%)
  between operations  14.8 us (9%)
  Pallas kernels  13 us (8%)
  waiting for transfers between devices  3.44 us (2%)
    all_gather x1, blocking collectives, attend(): packed = lax.all_gather(packed, 'zh', axis=0, tiled=True)  42.3 us
    all_to_all x1, blocking collectives, to_all(): return lax.all_to_all(copies, axes, split_axis=0, concat_axis=0, tiled=True)  35.1 us
    all_gather x1, blocking collectives, attend(): packed = lax.all_gather(packed, ('z1', 'z0'), axis=0, tiled=True)  18.4 us
    ppermute x1, starting transfers between devices, body(): taken = lax.ppermute(given, 'core', [(0, 1), (1, 0)])  16.3 us
    all_to_all x1, blocking collectives, body(): lax.all_to_all(part, ('x', 'y'), split_axis=0, concat_axis=0, tiled=True)  13 us
    pallas_call x1, Pallas kernels, project(): pl.pallas_call(project_kernel, grid=(2,), in_specs=[pl.BlockSpec((2, 2, r...  5.14 us
    ppermute x1, starting transfers between devices, attend(): taken = lax.ppermute(given, 'y', [(0, 1), (1, 0), (2, 3), (3, 2)])  4.42 us
    all_to_all x1, starting transfers between devices, attend(): heads = lax.all_to_all(heads, 'y', split_axis=0, concat_axis=0, tiled=True)  4.18 us
  transfers between devices with their start and end apart: 4, of which 2 were waited for; matrix products, arithmetic and copies ran while one was open for 0% of the time, Pallas kernels for 3%

profile of v12, /device:TPU:1, one launch (start us, length us, event | category | flops | bytes accessed | tf_op | source)
XLA Modules:
  0.0 166.8 jit_solution(12477834528580963545)
XLA Ops:
  6.5 0.0 copy-start
  6.5 0.0 copy-start.1
  6.5 0.0 copy-start.2
  6.5 0.0 all-gather.2.cloned.1.call-start
  7.2 2.6 %shard_map.112 = (bf16[144,128]{1,0:T(8,128)(2,1)S(1)}, bf16[32,2048]{1,0:T(8,128)(2,1)}, s32[1]{0:T(128)}) custom-call(f32[1]{0:T(128)S(6)} %copy.17.gate_ref, s32[8]{0:T(128)} %length_ref.1, bf16[1,8,4,64,128]{4,3,2,1,0:T(8,128)(2,1)} %query_ref.1, bf16[1,8,4,64,128]{4,3,2,1,0:T(8,128)(2,1)} %out_ref.1, bf16[1,8,4,64,128]{4,3,2,1,0:T(8,128)(2,1)} %cot_ref.1, ...), custom_call_target="tpu_custom_call" | custom-call | flops 65536 | bytes 262144 | tf_op jit(solution)/shard_map/pallas_call | solution.py:108
  9.8 0.0 all-gather.2.cloned.1.call-update
  10.5 0.0 copy-done
  10.5 0.0 copy-done.1
  10.5 0.0 copy-done.2
  10.5 75.5 %conditional.1 = (bf16[104,1024]{1,0:T(8,128)(2,1)S(1)}) conditional(s32[]{:T(128)} %bitcast.3, () %tuple.17, (s32[]{:T(128)}, bf16[144,128]{1,0:T(8,128)(2,1)S(1)}, bf16[1,52,1024]{2,1,0:T(8,128)(2,1)S(1)}, bf16[1,52,1024]{2,1,0:T(8,128)(2,1)S(1)}, s32[8]{0:T(128)S(1)}) %tuple.25), branch_computations={%region_0.1_spmd, %region_1.2_spmd} | conditional | flops 218529808 | bytes 8650537 | solution.py:305
  10.5 42.3 %all_gather.6 = bf16[576,128]{1,0:T(8,128)(2,1)S(1)} all-gather(bf16[144,128]{1,0:T(8,128)(2,1)S(1)} %get-tuple-element.43), channel_id=1, replica_groups=mesh['core'=2,'x'=4,'zb'=2,'z1'=2,'z0'=2,'zh'=4,'y'=4] {'zh'}, dimensions={0}, use_global_device_ids=true | all-gather | bytes 184320 | tf_op jit(solution)/shard_map/cond/branch_1_fun/all_gather | solution.py:294
  52.9 0.9 branch_1_fun.3
  53.7 4.2 %all-to-all-start = ((bf16[4,52,1024]{2,1,0:T(8,128)(2,1)}), bf16[4,52,1024]{2,1,0:T(8,128)(2,1)S(1)}, u32[]{:S(2)}, u32[]{:S(2)}) async-start(bf16[4,52,1024]{2,1,0:T(8,128)(2,1)} %branch_1_fun.3), calls=%async_computation | async-start | bytes 917504 | tf_op jit(solution)/shard_map/cond/branch_1_fun/all_to_all | solution.py:297
  57.9 18.4 %all_gather.7 = bf16[2304,128]{1,0:T(8,128)(2,1)S(1)} all-gather(bf16[576,128]{1,0:T(8,128)(2,1)S(1)} %all_gather.6), channel_id=1, replica_groups=mesh['core'=2,'x'=4,'zb'=2,'z1'=2,'z0'=2,'zh'=4,'y'=4] {'z1','z0'}, dimensions={0}, use_global_device_ids=true | all-gather | bytes 737280 | tf_op jit(solution)/shard_map/cond/branch_1_fun/all_gather | solution.py:298
  76.3 0.0 all-to-all-done.heads_ref
  76.3 1.7 %branch_1_fun.5 = bf16[104,1024]{1,0:T(8,128)(2,1)S(1)} custom-call(s32[1]{0:T(128)} %bitcast.2.half_ref, s32[8]{0:T(128)S(1)} %get-tuple-element.64.tiles_ref, bf16[4,4,144,128]{3,2,1,0:T(8,128)(2,1)S(1)} %bitcast.5, bf16[4,52,1024]{2,1,0:T(8,128)(2,1)S(1)} %all-to-all-done.heads_ref), custom_call_target="tpu_custom_call" | custom-call | flops 109051904 | bytes 2097152 | tf_op jit(solution)/shard_map/cond/branch_1_fun/pallas_call | solution.py:184
  78.0 4.4 %collective-permute-start = (bf16[104,1024]{1,0:T(8,128)(2,1)S(1)}, bf16[104,1024]{1,0:T(8,128)(2,1)S(1)}, u32[]{:S(2)}, u32[]{:S(2)}) collective-permute-start(bf16[104,1024]{1,0:T(8,128)(2,1)S(1)} %branch_1_fun.5), channel_id=1, source_target_pairs={{0,1},{1,0},{2,3},{3,2},{4,5},{5,4},{6,7},{7,6},{8,9},{9,8},{10,11... | collective-permute-start | bytes 638984 | tf_op jit(solution)/shard_map/cond/branch_1_fun/ppermute | solution.py:301
  82.5 1.7 %branch_1_fun.4 = bf16[104,1024]{1,0:T(8,128)(2,1)S(1)} custom-call(s32[1]{0:T(128)} %bitcast.half_ref, s32[8]{0:T(128)S(1)} %get-tuple-element.64.tiles_ref, bf16[4,4,144,128]{3,2,1,0:T(8,128)(2,1)S(1)} %bitcast.6, bf16[4,52,1024]{2,1,0:T(8,128)(2,1)S(1)} %all-to-all-done.heads_ref), custom_call_target="tpu_custom_call" | custom-call | flops 109051904 | bytes 2097152 | tf_op jit(solution)/shard_map/cond/branch_1_fun/pallas_call | solution.py:184
  84.2 1.8 %collective-permute-done = bf16[104,1024]{1,0:T(8,128)(2,1)S(1)} collective-permute-done((bf16[104,1024]{1,0:T(8,128)(2,1)S(1)}, bf16[104,1024]{1,0:T(8,128)(2,1)S(1)}, u32[]{:S(2)}, u32[]{:S(2)}) %collective-permute-start) | collective-permute-done | bytes 213024 | tf_op jit(solution)/shard_map/cond/branch_1_fun/ppermute | solution.py:301
  86.0 0.1 add_convert_fusion
  86.0 0.4 broadcast_in_dim.2
  86.5 35.1 %all_to_all.14 = bf16[16,104,1024]{2,1,0:T(8,128)(2,1)} all-to-all(bf16[16,104,1024]{2,1,0:T(8,128)(2,1)S(1)} %broadcast_in_dim.2), channel_id=1, replica_groups=mesh['core'=2,'x'=4,'zb'=2,'z1'=2,'z0'=2,'zh'=4,'y'=4] {'x','y'}, dimensions={0} | all-to-all | bytes 6815744 | tf_op jit(solution)/shard_map/all_to_all | solution.py:271
  121.6 0.0 all-gather.2.cloned.1.call-done.weight_ref
  121.6 5.1 %shard_map.113 = (f32[16,56,256]{2,1,0:T(8,128)}, bf16[16,56,256]{2,1,0:T(8,128)(2,1)}) custom-call(bf16[4,2,208,1024]{3,2,1,0:T(8,128)(2,1)} %bitcast.7, bf16[512,2048]{1,0:T(8,128)(2,1)} %all-gather.2.cloned.1.call-done.weight_ref), custom_call_target="tpu_custom_call" | custom-call | flops 1744830464 | bytes 7340032 | tf_op jit(solution)/shard_map/pallas_call | solution.py:232
  126.8 16.3 %collective-permute-start.1 = (bf16[16,56,256]{2,1,0:T(8,128)(2,1)}, bf16[16,56,256]{2,1,0:T(8,128)(2,1)S(1)}, u32[]{:S(2)}, u32[]{:S(2)}) collective-permute-start(bf16[16,56,256]{2,1,0:T(8,128)(2,1)} %get-tuple-element.58), channel_id=1, source_target_pairs={{0,512},{512,0},{1,513},{513,1},{2,514},{514,2},{3,515},{515,3},{4... | collective-permute-start | bytes 1376264 | tf_op jit(solution)/shard_map/ppermute | solution.py:314
  143.1 1.6 collective-permute-done.1
  144.7 1.3 add_convert_fusion.1
  146.0 13.0 %all_to_all.15.part_ref = bf16[16,56,256]{2,1,0:T(8,128)(2,1)S(1)} all-to-all(bf16[16,56,256]{2,1,0:T(8,128)(2,1)S(1)} %add_convert_fusion.1), channel_id=1, replica_groups=mesh['core'=2,'x'=4,'zb'=2,'z1'=2,'z0'=2,'zh'=4,'y'=4] {'x','y'}, dimensions={0} | all-to-all | bytes 917504 | tf_op jit(solution)/shard_map/all_to_all | solution.py:316
  159.0 1.0 shard_map.114
Async XLA Ops:
  6.5 4.0 %copy-start = (bf16[1,52,1024]{2,1,0:T(8,128)(2,1)S(1)}, bf16[1,52,1024]{2,1,0:T(8,128)(2,1)}, u32[]{:S(2)}) copy-start(bf16[1,52,1024]{2,1,0:T(8,128)(2,1)} %param.17) | copy-start | bytes 319492
  6.5 4.0 %copy-start.1 = (bf16[1,52,1024]{2,1,0:T(8,128)(2,1)S(1)}, bf16[1,52,1024]{2,1,0:T(8,128)(2,1)}, u32[]{:S(2)}) copy-start(bf16[1,52,1024]{2,1,0:T(8,128)(2,1)} %param.18) | copy-start | bytes 319492
  6.5 4.0 %copy-start.2 = (s32[8]{0:T(128)S(1)}, s32[8]{0:T(128)}, u32[]{:S(2)}) copy-start(s32[8]{0:T(128)} %param.22) | copy-start | bytes 100
  6.5 115.1 %all-gather.2.cloned.1.call-start = ((), (), s32[]{:S(2)}) async-start(), calls=%async_computation.3 | async-start | bytes 2228224 | tf_op jit(solution)/shard_map/all_gather | solution.py:290
  53.7 22.6 %all-to-all-start = ((bf16[4,52,1024]{2,1,0:T(8,128)(2,1)}), bf16[4,52,1024]{2,1,0:T(8,128)(2,1)S(1)}, u32[]{:S(2)}, u32[]{:S(2)}) async-start(bf16[4,52,1024]{2,1,0:T(8,128)(2,1)} %branch_1_fun.3), calls=%async_computation | async-start | bytes 917504 | tf_op jit(solution)/shard_map/cond/branch_1_fun/all_to_all | solution.py:297
  78.0 8.0 %collective-permute-start = (bf16[104,1024]{1,0:T(8,128)(2,1)S(1)}, bf16[104,1024]{1,0:T(8,128)(2,1)S(1)}, u32[]{:S(2)}, u32[]{:S(2)}) collective-permute-start(bf16[104,1024]{1,0:T(8,128)(2,1)S(1)} %branch_1_fun.5), channel_id=1, source_target_pairs={{0,1},{1,0},{2,3},{3,2},{4,5},{5,4},{6,7},{7,6},{8,9},{9,8},{10,11... | collective-permute-start | bytes 638984 | tf_op jit(solution)/shard_map/cond/branch_1_fun/ppermute | solution.py:301
  126.8 17.9 %collective-permute-start.1 = (bf16[16,56,256]{2,1,0:T(8,128)(2,1)}, bf16[16,56,256]{2,1,0:T(8,128)(2,1)S(1)}, u32[]{:S(2)}, u32[]{:S(2)}) collective-permute-start(bf16[16,56,256]{2,1,0:T(8,128)(2,1)} %get-tuple-element.58), channel_id=1, source_target_pairs={{0,512},{512,0},{1,513},{513,1},{2,514},{514,2},{3,515},{515,3},{4... | collective-permute-start | bytes 1376264 | tf_op jit(solution)/shard_map/ppermute | solution.py:314
Sparse Core Ops, SparseCore 0:
  10.0 109.4 all-gather.1
